TPU v7x, 256 devices: a whole 4x4x8 slice. The times are simulated.
256 devices in a mesh: fsdp: 64 (over z, y, x_lo), dp: 4 (over x_hi, core).
Axes of the slice: x: 4 (x_hi: 2, x_lo: 2; x = x_hi * 2 + x_lo), y: 4, z: 8, core: 2. Of those that a mesh axis runs over, the one named last changes fastest.
Arguments:
- grads: bfloat16 [4, 1024, 64, 1024], P('dp', 'fsdp'), may hold values from -4 to 4
- weights: float32 [1024, 64, 1024], P('fsdp', None, 'dp'), may hold values from -6 to 6
- moment_first: float32 [64, 1024, 1024], P('fsdp', None, 'dp'), may hold values from -3 to 3
- moment_second: float32 [64, 1024, 1024], P('fsdp', None, 'dp'), may hold values from 0.05 to 5
- left_basis: bfloat16 [64, 1024, 1024], P('fsdp'), may hold values from -0.1875 to 0.1875
- right_basis: bfloat16 [64, 1024, 1024], P('fsdp', 'dp'), may hold values from -0.1875 to 0.1875
Outputs:
- new_weights: float32 [1024, 64, 1024], P('fsdp', None, 'dp')
- new_first: float32 [64, 1024, 1024], P('fsdp', None, 'dp')
- new_second: float32 [64, 1024, 1024], P('fsdp', None, 'dp')
All inputs are finite; a program needn't handle non-finite values.
Results may differ from a plain program's by a relative error of at most 0.008.
Values may be sent and summed in bfloat16 or wider, within the bound.
No kernel may reach another device: no remote copies, remote signals or barrier semaphores. Data moves between devices by JAX's collectives and lax.ppermute only.
A program may use at most 64 MiB of HBM per device.

v0:
```python
import jax
import jax.numpy as jnp
from jax import lax
from jax.sharding import PartitionSpec as P


def local(grads, weights, moment_first, moment_second, left_basis, right_basis):
    replica_slab = grads[0]
    arrived = lax.all_to_all(replica_slab, "fsdp", split_axis=1, concat_axis=0, tiled=True)
    summed = lax.psum_scatter(
        arrived.astype(jnp.float32).astype(jnp.bfloat16), "dp", scatter_dimension=2, tiled=True
    ).astype(jnp.float32)
    grad_block = summed[:, 0, :].astype(jnp.bfloat16)
    left_block = left_basis[0]
    right_rows = right_basis[0]
    rotated_left = lax.dot_general(
        left_block, grad_block, (((0,), (0,)), ((), ())), preferred_element_type=jnp.float32
    ).astype(jnp.bfloat16)
    group_term = jnp.dot(rotated_left, right_rows, preferred_element_type=jnp.float32)
    rotated = lax.psum_scatter(
        group_term.astype(jnp.bfloat16), "dp", scatter_dimension=1, tiled=True
    ).astype(jnp.float32)
    bias_first = 1.0 - 0.9**10
    bias_second = 1.0 - 0.95**10
    first_new = 0.9 * moment_first[0] + 0.1 * rotated
    second_new = 0.95 * moment_second[0] + 0.05 * rotated * rotated
    direction = (first_new / bias_first / (jnp.sqrt(second_new / bias_second) + 1e-08)).astype(
        jnp.bfloat16
    )
    turned = lax.dot_general(
        lax.all_gather(direction, "dp", axis=1, tiled=True),
        right_rows,
        (((1,), (1,)), ((), ())),
        preferred_element_type=jnp.float32,
    ).astype(jnp.bfloat16)
    update = jnp.dot(left_block, turned, preferred_element_type=jnp.float32)
    returned = lax.all_to_all(
        update[:, None, :].astype(jnp.bfloat16), "fsdp", split_axis=0, concat_axis=1, tiled=True
    ).astype(jnp.float32)
    new_weights = weights - 0.5 * returned
    return (new_weights, first_new[None], second_new[None])


def solution(mesh):
    placed = (
        P("dp", "fsdp", None, None),
        P("fsdp", None, "dp"),
        P("fsdp", None, "dp"),
        P("fsdp", None, "dp"),
        P("fsdp", None, None),
        P("fsdp", "dp", None),
    )
    return jax.shard_map(
        local,
        mesh=mesh,
        in_specs=placed,
        out_specs=(P("fsdp", None, "dp"), P("fsdp", None, "dp"), P("fsdp", None, "dp")),
        check_vma=False,
    )
```

profile of v0, /device:TPU:32, one launch (start us, length us, event | category | flops | bytes accessed | tf_op | source)
XLA Modules:
  0.0 242.5 jit_solution(8640095850757688331)
XLA Ops:
  7.2 0.0 copy-start
  7.2 0.0 reduce-scatter.3.cloned.1.call-start
  7.2 2.9 %copy.22 = bf16[1,16,64,1024]{3,1,2,0:T(8,128)(2,1)S(1)} copy(bf16[1,16,64,1024]{3,2,1,0:T(8,128)(2,1)} %param.6) | data formatting | bytes 4194304 | tf_op args[0]
  10.1 62.9 %all_to_all.27 = bf16[16,64,1024]{2,0,1:T(8,128)(2,1)} all-to-all(bf16[16,64,1024]{2,0,1:T(8,128)(2,1)S(1)} %bitcast.58), channel_id=1, replica_groups=mesh['fsdp'=64,'dp'=4] {'fsdp'}, dimensions={1} | all-to-all | bytes 4194304 | tf_op jit(solution)/shard_map/all_to_all | solution.py:9
  73.0 0.0 copy-start.3
  73.0 0.0 reduce-scatter.3.cloned.1.call-update
  73.0 0.0 reduce-scatter.5.cloned.1.call-start
  73.1 41.0 %reduce-scatter.3.cloned.1.call-done = bf16[1024,1,256]{2,0,1:T(8,128)(2,1)} async-done(((bf16[1024,1,1024]{2,0,1:T(8,128)(2,1)}), bf16[1024,1,256]{2,0,1:T(8,128)(2,1)}) %reduce-scatter.3.cloned.1.call-update) | async-done | bytes 524304 | tf_op jit(solution)/shard_map/reduce_scatter | solution.py:10
  114.1 0.0 copy-done
  114.1 0.0 copy-done.3
  114.1 4.6 %convolution_convert_fusion = bf16[1024,1024]{1,0:T(8,128)(2,1)} fusion(bf16[1,1024,1024]{2,1,0:T(8,128)(2,1)S(1)} %copy-done, bf16[1,256,1024]{2,1,0:T(8,128)(2,1)S(1)} %copy-done.3, bf16[1024,1,256]{2,0,1:T(8,128)(2,1)} %reduce-scatter.3.cloned.1.call-done), kind=kOutput, calls=%fused_computation.5 | convolution fusion | flops 1075052544 | bytes 5242880 | tf_op jit(solution)/shard_map/dot_general | solution.py:19
  118.7 0.0 copy-start.1
  118.7 0.0 reduce-scatter.5.cloned.1.call-update
  118.7 0.0 all-gather.2.cloned.1.call-start
  118.8 43.0 %reduce-scatter.5.cloned.1.call-done = bf16[1024,256]{1,0:T(8,128)(2,1)} async-done(((bf16[1024,1024]{1,0:T(8,128)(2,1)}), bf16[1024,256]{1,0:T(8,128)(2,1)}) %reduce-scatter.5.cloned.1.call-update) | async-done | bytes 524304 | tf_op jit(solution)/shard_map/reduce_scatter | solution.py:20
  161.8 0.0 copy-done.1
  161.8 3.6 %fusion.18 = (f32[1,1024,256]{2,1,0:T(8,128)}, bf16[1024,256]{1,0:T(8,128)(2,1)}, f32[1,1024,256]{2,1,0:T(8,128)}) fusion(bf16[1024,256]{1,0:T(8,128)(2,1)} %reduce-scatter.5.cloned.1.call-done, f32[1,1024,256]{2,1,0:T(8,128)S(1)} %copy-done.1, f32[1,1024,256]{2,1,0:T(8,128)} %param.8), kind=kLoop, calls=%fused_computation.18 | loop fusion | flops 3407872 | bytes 5242880 | tf_op jit(solution)/shard_map/broadcast_in_dim | solution.py:41
  165.5 0.0 all-gather.2.cloned.1.call-update
  165.5 29.1 %all-gather.2.cloned.1.call-done = bf16[1024,1024]{1,0:T(8,128)(2,1)} async-done(((bf16[1024,256]{1,0:T(8,128)(2,1)}), bf16[1024,1024]{1,0:T(8,128)(2,1)}) %all-gather.2.cloned.1.call-update) | async-done | bytes 2097168 | tf_op jit(solution)/shard_map/all_gather | solution.py:31
  194.5 4.0 %fusion.10 = bf16[1024,1,256]{0,2,1:T(8,128)(2,1)S(1)} fusion(bf16[1,1024,1024]{2,1,0:T(8,128)(2,1)S(1)} %copy-done, bf16[1024,1024]{1,0:T(8,128)(2,1)} %all-gather.2.cloned.1.call-done, bf16[1,256,1024]{2,1,0:T(8,128)(2,1)} %param.11), kind=kOutput, calls=%fused_computation.11 | convolution fusion | flops 1074266112 | bytes 5242880 | tf_op jit(solution)/shard_map/dot_general | solution.py:36
  198.5 0.5 broadcast.12
  199.0 1.0 reduce
  200.1 0.2 copy.23
  200.3 0.1 reshape.18
  200.4 28.5 %all_to_all.28 = bf16[64,2,2048]{2,1,0:T(2,128)(2,1)} all-to-all(bf16[64,2,2048]{2,1,0:T(2,128)(2,1)S(1)} %reshape.18), channel_id=1, replica_groups=mesh['fsdp'=64,'dp'=4] {'fsdp'}, dimensions={0} | all-to-all | bytes 1048576 | tf_op jit(solution)/shard_map/all_to_all | solution.py:37
  228.9 3.6 %reshape.19 = bf16[1024,1,256]{2,1,0:T(2,128)(2,1)S(1)} reshape(bf16[64,2,2048]{2,1,0:T(2,128)(2,1)} %all_to_all.28) | data formatting | bytes 1048576
  232.5 0.0 copy-start.2
  232.6 0.1 convert_multiply_fusion.1
  232.7 1.1 copy-done.2
  233.8 0.6 copy_subtract_fusion
  234.4 1.6 copy.18
Async XLA Ops:
  7.2 107.0 %copy-start = (bf16[1,1024,1024]{2,1,0:T(8,128)(2,1)S(1)}, bf16[1,1024,1024]{2,1,0:T(8,128)(2,1)}, u32[]{:S(2)}) copy-start(bf16[1,1024,1024]{2,1,0:T(8,128)(2,1)} %param.10) | copy-start | bytes 6291460
  7.2 106.9 %reduce-scatter.3.cloned.1.call-start = ((), (), s32[]{:S(2)}) async-start(), calls=%async_computation.4 | async-start | bytes 2621440 | tf_op jit(solution)/shard_map/reduce_scatter | solution.py:10
  73.0 41.1 %copy-start.3 = (bf16[1,256,1024]{2,1,0:T(8,128)(2,1)S(1)}, bf16[1,256,1024]{2,1,0:T(8,128)(2,1)}, u32[]{:S(2)}) copy-start(bf16[1,256,1024]{2,1,0:T(8,128)(2,1)} %param.11) | copy-start | bytes 1572868
  73.0 88.8 %reduce-scatter.5.cloned.1.call-start = ((), (), s32[]{:S(2)}) async-start(), calls=%async_computation.5 | async-start | bytes 2621440 | tf_op jit(solution)/shard_map/reduce_scatter | solution.py:20
  118.7 43.1 %copy-start.1 = (f32[1,1024,256]{2,1,0:T(8,128)S(1)}, f32[1,1024,256]{2,1,0:T(8,128)}, u32[]{:S(2)}) copy-start(f32[1,1024,256]{2,1,0:T(8,128)} %param.9) | copy-start | bytes 3145732
  118.7 75.8 %all-gather.2.cloned.1.call-start = ((), (), s32[]{:S(2)}) async-start(), calls=%async_computation.6 | async-start | bytes 2621440 | tf_op jit(solution)/shard_map/all_gather | solution.py:31
  232.5 1.2 copy-start.2
Sparse Core Ops, SparseCore 0:
  73.1 40.9 reduce-scatter.2
  118.9 42.9 reduce-scatter.4
  165.6 28.8 all-gather.1
where the time goes:
time: 243 us
  waiting for transfers between devices  113 us (47%)
  blocking collectives  91.4 us (38%)
  between operations  13.8 us (6%)
  local copies, waits for them, and re-layouts  10.1 us (4%)
  matrix products  8.54 us (4%)
  other arithmetic  5.39 us (2%)
    all_to_all x1, blocking collectives, local(): lax.all_to_all(replica_slab, 'fsdp', split_axis=1, concat_axis=0, tiled=T...  62.9 us
    reduce_scatter x1, waiting for transfers between devices, local(): lax.psum_scatter(group_term.astype(jnp.bfloat16), 'dp', scatter_dimension...  43 us
    reduce_scatter x1, waiting for transfers between devices, local(): lax.psum_scatter(arrived.astype(jnp.float32).astype(jnp.bfloat16), 'dp',...  41 us
    all_gather x1, waiting for transfers between devices, local(): lax.all_gather(direction, 'dp', axis=1, tiled=True)  29.1 us
    all_to_all x1, blocking collectives, local(): lax.all_to_all(update[:, None, :].astype(jnp.bfloat16), 'fsdp', split_axi...  28.5 us
    unnamed x13, local copies, waits for them, and re-layouts  9.55 us
  transfers between devices with their start and end apart: 3, of which 3 were waited for; matrix products, arithmetic and copies ran while one was open for 0% of the time, Pallas kernels for 0%

commit v1 on v0

v1 whole, which is shorter than its diff:
```python
import jax
import jax.numpy as jnp
from jax import lax
from jax.sharding import Mesh, PartitionSpec as P

FSDP = ("z", "y", "x_lo")
DP = ("x_hi", "core")
SWAP = [(0, 1), (1, 0)]
F32 = jnp.float32
BF16 = jnp.bfloat16
Q = 256


def dot_f32(a, b, dims):
    return lax.dot_general(a, b, (dims, ((), ())), preferred_element_type=F32)


def local(grads, weights, moment_first, moment_second, left_basis, right_basis):
    core, x_hi = lax.axis_index("core"), lax.axis_index("x_hi")
    left = left_basis[0]
    right_own = right_basis[0]
    rows = grads.shape[1]
    blocks = grads.shape[2]

    low, high = right_own[:, : 2 * Q], right_own[:, 2 * Q :]
    right_half = jnp.where(x_hi == 0, low, high)
    right_far = lax.ppermute(jnp.where(x_hi == 0, high, low), "x_hi", SWAP)

    def part_of(half, which):
        return jnp.where(which == 0, half[:, :Q], half[:, Q:])

    right_cross = lax.ppermute(
        jnp.stack([part_of(right_half, 1 - core), part_of(right_far, 1 - core)]), "core", SWAP
    )

    turned_rows = jnp.transpose(grads[0], (1, 0, 2))

    def groups_of(which):
        return jnp.stack(
            [part_of(turned_rows[:, :, : 2 * Q].reshape(blocks * rows, 2 * Q), which).reshape(blocks, rows, Q),
             part_of(turned_rows[:, :, 2 * Q :].reshape(blocks * rows, 2 * Q), which).reshape(blocks, rows, Q)],
            axis=1,
        )

    arrived = lax.ppermute(groups_of(1 - core), "core", SWAP)
    chip_sum = (groups_of(core).astype(F32) + arrived.astype(F32)).astype(BF16)

    pieces = lax.all_to_all(
        chip_sum.reshape(2 * blocks, rows, Q), FSDP + ("x_hi",), split_axis=0, concat_axis=0, tiled=True
    ).reshape(blocks, 2, rows, Q)
    grad_block = (
        (pieces[:, 0].astype(F32) + pieces[:, 1].astype(F32)).astype(BF16).reshape(blocks * rows, Q)
    )

    rl_own = dot_f32(left, grad_block, ((0,), (0,))).astype(BF16)
    rl_far = lax.ppermute(rl_own, "x_hi", SWAP)
    rl_near = lax.ppermute(rl_own, "core", SWAP)
    rl_cross = lax.ppermute(rl_far, "core", SWAP)
    plain = ((1,), (0,))
    rotated = (
        dot_f32(rl_own, part_of(right_half, core), plain)
        + dot_f32(rl_near, right_cross[0], plain)
        + dot_f32(rl_far, part_of(right_far, core), plain)
        + dot_f32(rl_cross, right_cross[1], plain)
    )

    bias_first = 1.0 - 0.9**10
    bias_second = 1.0 - 0.95**10
    first_new = 0.9 * moment_first[0] + 0.1 * rotated
    second_new = 0.95 * moment_second[0] + 0.05 * rotated * rotated
    direction = (first_new / bias_first / (jnp.sqrt(second_new / bias_second) + 1e-08)).astype(BF16)

    near = lax.ppermute(direction, "core", SWAP)
    both = jnp.concatenate(
        [jnp.where(core == 0, direction, near), jnp.where(core == 0, near, direction)], axis=1
    )
    shares = []
    for group in range(2):
        right_rows = jnp.where(x_hi == group, right_half, right_far)
        turned = dot_f32(both, right_rows, ((1,), (1,))).astype(BF16)
        shares.append(dot_f32(left, turned, plain).astype(BF16).reshape(blocks, rows, Q))
    returned = lax.all_to_all(
        jnp.stack(shares, axis=1).reshape(2 * blocks, rows, Q),
        FSDP + ("x_hi",),
        split_axis=0,
        concat_axis=0,
        tiled=True,
    ).reshape(blocks, 2, rows, Q)
    update = jnp.transpose(returned[:, 0].astype(F32) + returned[:, 1].astype(F32), (1, 0, 2))
    new_weights = weights - 0.5 * update
    return (new_weights, first_new[None], second_new[None])


def solution(mesh):
    fine = Mesh(mesh.devices.reshape(8, 4, 2, 2, 2), FSDP + DP)
    placed = (
        P(DP, FSDP, None, None),
        P(FSDP, None, DP),
        P(FSDP, None, DP),
        P(FSDP, None, DP),
        P(FSDP, None, None),
        P(FSDP, DP, None),
    )
    return jax.shard_map(
        local,
        mesh=fine,
        in_specs=placed,
        out_specs=(P(FSDP, None, DP), P(FSDP, None, DP), P(FSDP, None, DP)),
        check_vma=False,
    )
```

time: 243 us -> 153 us (0.63)
  blocking collectives: 91.4 us -> 0 us
  waiting for transfers between devices: 113 us -> 62.8 us
  starting transfers between devices: 0.12 us -> 27.6 us
  local copies, waits for them, and re-layouts: 10.1 us -> 35.2 us
  between operations: 13.8 us -> 0.81 us
  other arithmetic: 5.39 us -> 13.3 us
  matrix products: 8.54 us -> 11.8 us
    all_to_all x2 -> x0, blocking collectives: 91.4 us -> none  [the longest x1 62.9 us: local(): lax.all_to_all(replica_slab, 'fsdp', split_axis=1, concat_axis=0, tiled=T...]
    reduce_scatter x2 -> x0, waiting for transfers between devices: 84.1 us -> none  [the longest x1 43 us: local(): lax.psum_scatter(group_term.astype(jnp.bfloat16), 'dp', scatter_dimension...]
    all_to_all x0 -> x2, waiting for transfers between devices: none -> 47 us  [the longest x1 25.9 us: local(): lax.all_to_all(jnp.stack(shares, axis=1).reshape(2 * blocks, rows, Q), FS...]
    all_gather x1 -> x0, waiting for transfers between devices: 29.1 us -> none  [local(): lax.all_gather(direction, 'dp', axis=1, tiled=True)]
    all_to_all x0 -> x2, starting transfers between devices: none -> 21.8 us  [the longest x1 15 us: local(): lax.all_to_all(chip_sum.reshape(2 * blocks, rows, Q), FSDP + ('x_hi',), s...]
    ppermute x0 -> x7, waiting for transfers between devices: none -> 15.9 us  [the longest x1 12.1 us: local(): rl_far = lax.ppermute(rl_own, 'x_hi', SWAP)]
    unnamed x13 -> x20, local copies, waits for them, and re-layouts: 9.55 us -> 22.9 us
    select_n x0 -> x3, other arithmetic: none -> 6.25 us  [the longest x1 2.58 us: part_of(): return jnp.where(which == 0, half[:, :Q], half[:, Q:])]
  transfers between devices with their start and end apart: 3 -> 9, of which waited for: 3 -> 6; matrix products, arithmetic and copies ran while one was open for 0% -> 11% of each run, Pallas kernels for 0% -> 0%
where the time goes in v1:
time: 153 us; the launch traced here: 152 us
  waiting for transfers between devices  62.8 us (41%)
  local copies, waits for them, and re-layouts  35.2 us (23%)
  starting transfers between devices  27.6 us (18%)
  other arithmetic  13.3 us (9%)
  matrix products  11.8 us (8%)
    all_to_all x1, waiting for transfers between devices, local(): lax.all_to_all(jnp.stack(shares, axis=1).reshape(2 * blocks, rows, Q), FS...  25.9 us
    unnamed x20, local copies, waits for them, and re-layouts  22.9 us
    all_to_all x1, waiting for transfers between devices, local(): lax.all_to_all(chip_sum.reshape(2 * blocks, rows, Q), FSDP + ('x_hi',), s...  21 us
    all_to_all x1, starting transfers between devices, local(): lax.all_to_all(chip_sum.reshape(2 * blocks, rows, Q), FSDP + ('x_hi',), s...  15 us
    ppermute x1, waiting for transfers between devices, local(): rl_far = lax.ppermute(rl_own, 'x_hi', SWAP)  12.1 us
    dot_general x7, matrix products, dot_f32(): return lax.dot_general(a, b, (dims, ((), ())), preferred_element_type=F32)  11.8 us
    all_to_all x1, starting transfers between devices, local(): lax.all_to_all(jnp.stack(shares, axis=1).reshape(2 * blocks, rows, Q), FS...  6.82 us
    select_n x4, local copies, waits for them, and re-layouts, part_of(): return jnp.where(which == 0, half[:, :Q], half[:, Q:])  5.35 us
  transfers between devices with their start and end apart: 9, of which 6 were waited for; matrix products, arithmetic and copies ran while one was open for 11% of the time, Pallas kernels for 0%

profile of v1, /device:TPU:32, one launch (start us, length us, event | category | flops | bytes accessed | tf_op | source)
XLA Modules:
  0.0 151.6 jit_solution(10408874441944623776)
XLA Ops:
  0.7 2.9 %copy.40 = bf16[1,16,64,1024]{3,1,2,0:T(8,128)(2,1)S(1)} copy(bf16[1,16,64,1024]{3,2,1,0:T(8,128)(2,1)} %param.6) | data formatting | bytes 4194304 | tf_op args[0]
  3.5 0.2 fusion.45
  3.7 1.0 fusion.46
  4.8 2.1 %copy.34 = bf16[1024,256]{0,1:T(8,128)(2,1)} copy(bf16[1024,256]{1,0:T(8,128)(2,1)} %get-tuple-element.21) | data formatting | bytes 1048576
  6.8 2.0 %copy.35 = bf16[1024,256]{0,1:T(8,128)(2,1)} copy(bf16[1024,256]{1,0:T(8,128)(2,1)} %get-tuple-element.20) | data formatting | bytes 1048576
  8.9 1.0 fusion.47
  9.9 2.1 %copy.36 = bf16[1024,256]{0,1:T(8,128)(2,1)} copy(bf16[1024,256]{1,0:T(8,128)(2,1)} %get-tuple-element.23) | data formatting | bytes 1048576
  12.0 2.0 %copy.37 = bf16[1024,256]{0,1:T(8,128)(2,1)} copy(bf16[1024,256]{1,0:T(8,128)(2,1)} %get-tuple-element.22) | data formatting | bytes 1048576
  14.1 2.6 %broadcast_select_fusion.4 = (bf16[1024,256]{0,1:T(8,128)(2,1)S(1)}, bf16[1024,256]{0,1:T(8,128)(2,1)}, bf16[1024,256]{0,1:T(8,128)(2,1)}, bf16[1024,256]{0,1:T(8,128)(2,1)}) fusion(bf16[1024,256]{0,1:T(8,128)(2,1)} %copy.36, bf16[1024,256]{0,1:T(8,128)(2,1)} %copy.37, pred[]{:T(512)S(6)} %eq.8, pred[]{:T(512)S(6)} %eq.9, ...), kind=kLoop, calls=%fused_computation.31 | loop fusion | flops 1048576 | bytes 4194306 | tf_op jit(solution)/shard_map/jit(_where)/select_n | solution.py:30
  16.6 2.1 %copy.23 = bf16[1024,256]{1,0:T(8,128)(2,1)} copy(bf16[1024,256]{0,1:T(8,128)(2,1)} %get-tuple-element.26) | data formatting | bytes 1048576 | tf_op jit(solution)/shard_map/jit(_where)/select_n | solution.py:30
  18.8 2.0 %copy.24 = bf16[1024,256]{1,0:T(8,128)(2,1)} copy(bf16[1024,256]{0,1:T(8,128)(2,1)} %get-tuple-element.19) | data formatting | bytes 1048576 | tf_op jit(solution)/shard_map/jit(_where)/select_n | solution.py:30
  20.8 2.3 %pad_maximum_fusion = bf16[64,2,16,256]{3,2,0,1:T(8,128)(2,1)} fusion(bf16[64,1,16,256]{3,2,0,1:T(8,128)(2,1)} %bitcast.92, bf16[64,1,16,256]{3,2,0,1:T(8,128)(2,1)} %bitcast.91), kind=kLoop, calls=%fused_computation.20 | loop fusion | flops 524288 | bytes 2097152 | tf_op jit(solution)/shard_map/stack | solution.py:39
  23.1 1.0 copy.19
  24.1 0.2 copy.22
  24.3 1.8 %collective-permute-done = bf16[64,2,16,256]{3,2,0,1:T(8,128)(2,1)} collective-permute-done((bf16[64,2,16,256]{3,2,0,1:T(8,128)(2,1)}, bf16[64,2,16,256]{3,2,0,1:T(8,128)(2,1)}, u32[]{:S(2)}, u32[]{:S(2)}) %collective-permute-start) | collective-permute-done | bytes 1048608 | tf_op jit(solution)/shard_map/ppermute | solution.py:45
  26.1 1.6 %add_convert_fusion = bf16[64,2,16,256]{3,2,0,1:T(8,128)(2,1)S(1)} fusion(bf16[64,2,16,256]{3,2,0,1:T(8,128)(2,1)} %collective-permute-done, bf16[64,1,16,256]{3,2,0,1:T(8,128)(2,1)S(1)} %bitcast.90, bf16[64,1,16,256]{3,2,0,1:T(8,128)(2,1)} %bitcast.88), kind=kLoop, calls=%fused_computation.7 | loop fusion | flops 2621440 | bytes 3145728 | tf_op jit(solution)/shard_map/convert_element_type | solution.py:46
  27.7 1.1 copy.25
  28.8 15.0 %all-to-all-start = ((bf16[128,16,256]{2,1,0:T(8,128)(2,1)}), bf16[128,16,256]{2,1,0:T(8,128)(2,1)S(1)}, u32[]{:S(2)}, u32[]{:S(2)}) async-start(bf16[128,16,256]{2,1,0:T(8,128)(2,1)} %bitcast.81), calls=%async_computation | async-start | bytes 2097152 | tf_op jit(solution)/shard_map/all_to_all | solution.py:48
  43.8 1.8 %broadcast_select_fusion.6 = (bf16[256,512]{1,0:T(8,128)(2,1)}, bf16[256,512]{1,0:T(8,128)(2,1)S(1)}) fusion(pred[]{:T(512)S(6)} %eq.10, bf16[256,1024]{1,0:T(8,128)(2,1)} %bitcast.94), kind=kLoop, calls=%fused_computation.40 | loop fusion | flops 262144 | bytes 1048577 | tf_op jit(solution)/shard_map/jit(_where)/select_n | solution.py:27
  45.6 3.0 %collective-permute-start.2 = (bf16[256,512]{1,0:T(8,128)(2,1)}, bf16[256,512]{1,0:T(8,128)(2,1)}, u32[]{:S(2)}, u32[]{:S(2)}) collective-permute-start(bf16[256,512]{1,0:T(8,128)(2,1)} %get-tuple-element.24), channel_id=1, source_target_pairs={{0,2},{2,0},{1,3},{3,1},{4,6},{6,4},{5,7},{7,5},{8,10},{10,8},{9,1... | collective-permute-start | bytes 786440 | tf_op jit(solution)/shard_map/ppermute | solution.py:27
  48.6 2.5 %copy.15 = f32[1,1024,256]{1,2,0:T(8,128)} copy(f32[1,1024,256]{2,1,0:T(8,128)} %param.8) | data formatting | bytes 2097152 | tf_op args[2]
  51.1 2.5 %copy.26 = f32[1,1024,256]{1,2,0:T(8,128)} copy(f32[1,1024,256]{2,1,0:T(8,128)} %param.9) | data formatting | bytes 2097152 | tf_op args[3]
  53.7 21.0 %all-to-all-done = bf16[128,16,256]{2,1,0:T(8,128)(2,1)S(1)} async-done(((bf16[128,16,256]{2,1,0:T(8,128)(2,1)}), bf16[128,16,256]{2,1,0:T(8,128)(2,1)S(1)}, u32[]{:S(2)}, u32[]{:S(2)}) %all-to-all-start) | async-done | bytes 1048608 | tf_op jit(solution)/shard_map/all_to_all | solution.py:48
  74.7 0.1 add_convert_fusion.1
  74.8 0.7 fusion.6
  75.7 2.1 %collective-permute-start.4 = (bf16[1024,256]{0,1:T(8,128)(2,1)S(1)}, bf16[1024,256]{0,1:T(8,128)(2,1)S(1)}, u32[]{:S(2)}, u32[]{:S(2)}) collective-permute-start(bf16[1024,256]{0,1:T(8,128)(2,1)S(1)} %bitcast.87), channel_id=1, source_target_pairs={{0,2},{2,0},{1,3},{3,1},{4,6},{6,4},{5,7},{7,5},{8,10},{10,8},{9,1... | collective-permute-start | bytes 1572872 | tf_op jit(solution)/shard_map/ppermute | solution.py:56
  77.8 1.0 select_bitcast_fusion
  78.8 0.2 collective-permute-start.3
  79.1 0.3 fusion.33
  79.4 12.1 %collective-permute-done.4 = bf16[1024,256]{0,1:T(8,128)(2,1)S(1)} collective-permute-done((bf16[1024,256]{0,1:T(8,128)(2,1)S(1)}, bf16[1024,256]{0,1:T(8,128)(2,1)S(1)}, u32[]{:S(2)}, u32[]{:S(2)}) %collective-permute-start.4) | collective-permute-done | bytes 524320 | tf_op jit(solution)/shard_map/ppermute | solution.py:56
  91.5 0.3 convolution_add_fusion.2
  91.9 1.3 convolution_add_fusion.1
  93.2 0.2 collective-permute-done.5
  93.4 2.2 %fusion.23 = (f32[1,1024,256]{1,2,0:T(8,128)}, bf16[1024,256]{0,1:T(8,128)(2,1)S(1)}, f32[1,1024,256]{1,2,0:T(8,128)}) fusion(f32[1,1024,256]{1,2,0:T(8,128)S(1)} %copy-done.4, f32[1,1024,256]{1,2,0:T(8,128)S(1)} %copy-done.3, f32[1024,256]{0,1:T(8,128)S(1)} %convolution_add_fusion.1, bf16[1024,256]{0,1:T(8,128)(2,1)S(1)} %collective-permute-done.5, ...), kind=kOutput, calls=%fused_computation.34 | convolution fusion | flops 137625600 | bytes 6422528 | tf_op jit(solution)/shard_map/dot_general | solution.py:15
  95.7 0.3 collective-permute-start.6
  96.0 1.7 %collective-permute-done.6 = bf16[1024,256]{0,1:T(8,128)(2,1)} collective-permute-done((bf16[1024,256]{0,1:T(8,128)(2,1)S(1)}, bf16[1024,256]{0,1:T(8,128)(2,1)}, u32[]{:S(2)}, u32[]{:S(2)}) %collective-permute-start.6) | collective-permute-done | bytes 524320 | tf_op jit(solution)/shard_map/ppermute | solution.py:73
  97.7 1.9 %broadcast_select_fusion.3 = (bf16[1024,256]{0,1:T(8,128)(2,1)S(1)}, bf16[1024,256]{0,1:T(8,128)(2,1)}) fusion(bf16[1024,256]{0,1:T(8,128)(2,1)S(1)} %get-tuple-element.10, bf16[1024,256]{0,1:T(8,128)(2,1)} %collective-permute-done.6, pred[]{:T(512)S(6)} %eq.8), kind=kLoop, calls=%fused_computation.30 | loop fusion | flops 524288 | bytes 2097153 | tf_op jit(solution)/shard_map/jit(_where)/select_n | solution.py:75
  99.6 3.4 %fusion.18 = bf16[1024,256]{0,1:T(8,128)(2,1)} fusion(bf16[1,1024,1024]{2,1,0:T(8,128)(2,1)S(1)} %copy-done, bf16[1024,256]{0,1:T(8,128)(2,1)} %get-tuple-element.15, bf16[1024,256]{0,1:T(8,128)(2,1)S(1)} %get-tuple-element.14, bf16[256,512]{1,0:T(8,128)(2,1)S(1)} %get-tuple-element.25, bf16[256,512]{1,0:T(8,128)(2,1)} %collective-permute-done.2, pred[]{:T(512)S(6)} %eq.10), kind=kOutput, calls=%fused_computation.18 | convolution fusion | flops 808058880 | bytes 4194305 | tf_op jit(solution)/shard_map/dot_general | solution.py:15
  103.0 1.2 copy.27
  104.3 3.5 %fusion.15 = bf16[1024,256]{0,1:T(8,128)(2,1)} fusion(bf16[1,1024,1024]{2,1,0:T(8,128)(2,1)S(1)} %copy-done, bf16[1024,256]{0,1:T(8,128)(2,1)} %get-tuple-element.15, bf16[1024,256]{0,1:T(8,128)(2,1)S(1)} %get-tuple-element.14, bf16[256,512]{1,0:T(8,128)(2,1)S(1)} %get-tuple-element.25, bf16[256,512]{1,0:T(8,128)(2,1)} %collective-permute-done.2, pred[]{:T(512)S(6)} %eq.11), kind=kOutput, calls=%fused_computation.17 | convolution fusion | flops 808058880 | bytes 4194305 | tf_op jit(solution)/shard_map/dot_general | solution.py:15
  107.7 1.2 copy.28
  109.1 1.2 copy.29
  110.3 6.8 %all-to-all-start.1 = ((bf16[128,16,256]{2,1,0:T(8,128)(2,1)}), bf16[128,16,256]{2,1,0:T(8,128)(2,1)S(1)}, u32[]{:S(2)}, u32[]{:S(2)}) async-start(bf16[128,16,256]{2,1,0:T(8,128)(2,1)} %bitcast.82), calls=%async_computation.1 | async-start | bytes 2097152 | tf_op jit(solution)/shard_map/all_to_all | solution.py:82
  117.1 2.5 %copy.32 = f32[1,1024,256]{2,1,0:T(8,128)} copy(f32[1,1024,256]{1,2,0:T(8,128)} %get-tuple-element.11) | data formatting | bytes 2097152
  119.6 2.5 %copy.33 = f32[1,1024,256]{2,1,0:T(8,128)} copy(f32[1,1024,256]{1,2,0:T(8,128)} %get-tuple-element.9) | data formatting | bytes 2097152
  122.1 25.9 %all-to-all-done.1 = bf16[128,16,256]{2,1,0:T(8,128)(2,1)S(1)} async-done(((bf16[128,16,256]{2,1,0:T(8,128)(2,1)}), bf16[128,16,256]{2,1,0:T(8,128)(2,1)S(1)}, u32[]{:S(2)}, u32[]{:S(2)}) %all-to-all-start.1) | async-done | bytes 1048608 | tf_op jit(solution)/shard_map/all_to_all | solution.py:82
  148.1 1.9 %bitcast_subtract_fusion = f32[16,64,256]{2,0,1:T(8,128)S(1)} fusion(f32[16,64,256]{2,1,0:T(8,128)} %param.7, bf16[64,2,16,256]{3,2,1,0:T(8,128)(2,1)S(1)} %bitcast.79), kind=kLoop, calls=%fused_computation.23 | loop fusion | flops 1310720 | bytes 3145728 | tf_op jit(solution)/shard_map/sub | solution.py:90
  150.0 1.6 %copy.31 = f32[16,64,256]{2,1,0:T(8,128)} copy(f32[16,64,256]{2,0,1:T(8,128)S(1)} %bitcast_subtract_fusion) | data formatting | bytes 2097152
  (19 shorter events, 0.3 us)
Async XLA Ops:
  0.6 74.2 %copy-start = (bf16[1,1024,1024]{2,1,0:T(8,128)(2,1)S(1)}, bf16[1,1024,1024]{2,1,0:T(8,128)(2,1)}, u32[]{:S(2)}) copy-start(bf16[1,1024,1024]{2,1,0:T(8,128)(2,1)} %param.10) | copy-start | bytes 6291460
  9.9 4.1 %copy-start.1 = (bf16[1024,256]{0,1:T(8,128)(2,1)S(1)}, bf16[1024,256]{0,1:T(8,128)(2,1)}, u32[]{:S(2)}) copy-start(bf16[1024,256]{0,1:T(8,128)(2,1)} %copy.34) | copy-start | bytes 1572868
  16.6 6.4 %copy-start.2 = (bf16[1024,256]{0,1:T(8,128)(2,1)S(1)}, bf16[1024,256]{0,1:T(8,128)(2,1)}, u32[]{:S(2)}) copy-start(bf16[1024,256]{0,1:T(8,128)(2,1)} %get-tuple-element.27) | copy-start | bytes 1572868
  23.1 3.0 %collective-permute-start = (bf16[64,2,16,256]{3,2,0,1:T(8,128)(2,1)}, bf16[64,2,16,256]{3,2,0,1:T(8,128)(2,1)}, u32[]{:S(2)}, u32[]{:S(2)}) collective-permute-start(bf16[64,2,16,256]{3,2,0,1:T(8,128)(2,1)} %pad_maximum_fusion), channel_id=1, source_target_pairs={{0,1},{1,0},{2,3},{3,2},{4,5},{5,4},{6,7},{7,6},{8,9},{9,8},{10,11... | collective-permute-start | bytes 3145736 | tf_op jit(solution)/shard_map/ppermute | solution.py:45
  28.8 45.9 %all-to-all-start = ((bf16[128,16,256]{2,1,0:T(8,128)(2,1)}), bf16[128,16,256]{2,1,0:T(8,128)(2,1)S(1)}, u32[]{:S(2)}, u32[]{:S(2)}) async-start(bf16[128,16,256]{2,1,0:T(8,128)(2,1)} %bitcast.81), calls=%async_computation | async-start | bytes 2097152 | tf_op jit(solution)/shard_map/all_to_all | solution.py:48
  45.6 32.2 %collective-permute-start.2 = (bf16[256,512]{1,0:T(8,128)(2,1)}, bf16[256,512]{1,0:T(8,128)(2,1)}, u32[]{:S(2)}, u32[]{:S(2)}) collective-permute-start(bf16[256,512]{1,0:T(8,128)(2,1)} %get-tuple-element.24), channel_id=1, source_target_pairs={{0,2},{2,0},{1,3},{3,1},{4,6},{6,4},{5,7},{7,5},{8,10},{10,8},{9,1... | collective-permute-start | bytes 786440 | tf_op jit(solution)/shard_map/ppermute | solution.py:27
  75.6 16.0 %collective-permute-start.1 = (bf16[1024,256]{0,1:T(8,128)(2,1)S(1)}, bf16[1024,256]{0,1:T(8,128)(2,1)S(1)}, u32[]{:S(2)}, u32[]{:S(2)}) collective-permute-start(bf16[1024,256]{0,1:T(8,128)(2,1)S(1)} %bitcast.86), channel_id=1, source_target_pairs={{0,1},{1,0},{2,3},{3,2},{4,5},{5,4},{6,7},{7,6},{8,9},{9,8},{10,11... | collective-permute-start | bytes 1572872 | tf_op jit(solution)/shard_map/ppermute | solution.py:57
  75.7 15.8 %collective-permute-start.4 = (bf16[1024,256]{0,1:T(8,128)(2,1)S(1)}, bf16[1024,256]{0,1:T(8,128)(2,1)S(1)}, u32[]{:S(2)}, u32[]{:S(2)}) collective-permute-start(bf16[1024,256]{0,1:T(8,128)(2,1)S(1)} %bitcast.87), channel_id=1, source_target_pairs={{0,2},{2,0},{1,3},{3,1},{4,6},{6,4},{5,7},{7,5},{8,10},{10,8},{9,1... | collective-permute-start | bytes 1572872 | tf_op jit(solution)/shard_map/ppermute | solution.py:56
  78.8 12.7 %collective-permute-start.3 = (bf16[2,256,256]{2,1,0:T(8,128)(2,1)S(1)}, bf16[2,256,256]{2,1,0:T(8,128)(2,1)S(1)}, u32[]{:S(2)}, u32[]{:S(2)}) collective-permute-start(bf16[2,256,256]{2,1,0:T(8,128)(2,1)S(1)} %pad_maximum_fusion.7), channel_id=1, source_target_pairs={{0,1},{1,0},{2,3},{3,2},{4,5},{5,4},{6,7},{7,6},{8,9},{9,8},{10,11... | collective-permute-start | bytes 786440 | tf_op jit(solution)/shard_map/ppermute | solution.py:32
  79.4 14.0 %copy-start.3 = (f32[1,1024,256]{1,2,0:T(8,128)S(1)}, f32[1,1024,256]{1,2,0:T(8,128)}, u32[]{:S(2)}) copy-start(f32[1,1024,256]{1,2,0:T(8,128)} %copy.15) | copy-start | bytes 3145732
  79.4 14.0 %copy-start.4 = (f32[1,1024,256]{1,2,0:T(8,128)S(1)}, f32[1,1024,256]{1,2,0:T(8,128)}, u32[]{:S(2)}) copy-start(f32[1,1024,256]{1,2,0:T(8,128)} %copy.26) | copy-start | bytes 3145732
  91.5 1.9 %collective-permute-start.5 = (bf16[1024,256]{0,1:T(8,128)(2,1)S(1)}, bf16[1024,256]{0,1:T(8,128)(2,1)S(1)}, u32[]{:S(2)}, u32[]{:S(2)}) collective-permute-start(bf16[1024,256]{0,1:T(8,128)(2,1)S(1)} %collective-permute-done.4), channel_id=1, source_target_pairs={{0,1},{1,0},{2,3},{3,2},{4,5},{5,4},{6,7},{7,6},{8,9},{9,8},{10,11... | collective-permute-start | bytes 1572872 | tf_op jit(solution)/shard_map/ppermute | solution.py:58
  95.7 2.0 %collective-permute-start.6 = (bf16[1024,256]{0,1:T(8,128)(2,1)S(1)}, bf16[1024,256]{0,1:T(8,128)(2,1)}, u32[]{:S(2)}, u32[]{:S(2)}) collective-permute-start(bf16[1024,256]{0,1:T(8,128)(2,1)S(1)} %get-tuple-element.10), channel_id=1, source_target_pairs={{0,1},{1,0},{2,3},{3,2},{4,5},{5,4},{6,7},{7,6},{8,9},{9,8},{10,11... | collective-permute-start | bytes 1572872 | tf_op jit(solution)/shard_map/ppermute | solution.py:73
  110.3 37.8 %all-to-all-start.1 = ((bf16[128,16,256]{2,1,0:T(8,128)(2,1)}), bf16[128,16,256]{2,1,0:T(8,128)(2,1)S(1)}, u32[]{:S(2)}, u32[]{:S(2)}) async-start(bf16[128,16,256]{2,1,0:T(8,128)(2,1)} %bitcast.82), calls=%async_computation.1 | async-start | bytes 2097152 | tf_op jit(solution)/shard_map/all_to_all | solution.py:82

commit v2 on v1

v2 whole, which is shorter than its diff:
```python
import jax
import jax.numpy as jnp
from jax import lax
from jax.experimental import pallas as pl
from jax.experimental.pallas import tpu as pltpu
from jax.sharding import Mesh, PartitionSpec as P

FSDP = ("z", "y", "x_lo")
DP = ("x_hi", "core")
SWAP = [(0, 1), (1, 0)]
F32 = jnp.float32
BF16 = jnp.bfloat16
BS = 1024
NB = 64
ROWS = 16
Q = 256
PLAIN = ((1,), (0,))
PARAMS = pltpu.CompilerParams(vmem_limit_bytes=16 << 20)


def dot_f32(a, b, dims=PLAIN):
    return lax.dot_general(a, b, (dims, ((), ())), preferred_element_type=F32)


def cost(flops, moved):
    return pl.CostEstimate(flops=flops, bytes_accessed=moved, transcendentals=0)


def swap_matrix():
    to = lax.broadcasted_iota(jnp.int32, (Q, Q), 0)
    come = lax.broadcasted_iota(jnp.int32, (Q, Q), 1)
    hit = (to // ROWS == come % ROWS) & (to % ROWS == come // ROWS)
    return jnp.where(hit, 1.0, 0.0).astype(BF16)


def pick_kernel(core_ref, grads_ref, out_ref):
    out_ref[0] = grads_ref[...]


def pick(core, grads):
    return pl.pallas_call(
        pick_kernel,
        grid_spec=pltpu.PrefetchScalarGridSpec(
            num_scalar_prefetch=1,
            grid=(2,),
            in_specs=[pl.BlockSpec((ROWS, NB, Q), lambda g, core: (0, 0, 2 * g + 1 - core[0]))],
            out_specs=pl.BlockSpec((1, ROWS, NB, Q), lambda g, core: (g, 0, 0, 0)),
        ),
        out_shape=jax.ShapeDtypeStruct((2, ROWS, NB, Q), BF16),
        compiler_params=PARAMS,
        cost_estimate=cost(0, 4 << 20),
        name="pick",
    )(core, grads)


def pack_kernel(core_ref, grads_ref, arrived_ref, out_ref):
    swap = swap_matrix()
    for part in range(NB // ROWS):
        here = pl.ds(part * ROWS, ROWS)
        total = dot_f32(swap, grads_ref[:, here, :].reshape(Q, Q))
        total += dot_f32(swap, arrived_ref[0, :, here, :].reshape(Q, Q))
        out_ref[here, 0] = total.astype(BF16).reshape(ROWS, ROWS, Q)


def pack(core, grads, arrived):
    return pl.pallas_call(
        pack_kernel,
        grid_spec=pltpu.PrefetchScalarGridSpec(
            num_scalar_prefetch=1,
            grid=(2,),
            in_specs=[
                pl.BlockSpec((ROWS, NB, Q), lambda g, core: (0, 0, 2 * g + core[0])),
                pl.BlockSpec((1, ROWS, NB, Q), lambda g, core: (g, 0, 0, 0)),
            ],
            out_specs=pl.BlockSpec((NB, 1, ROWS, Q), lambda g, core: (0, g, 0, 0)),
        ),
        out_shape=jax.ShapeDtypeStruct((NB, 2, ROWS, Q), BF16),
        compiler_params=PARAMS,
        cost_estimate=cost(4 * BS * Q * Q, 3 << 20),
        name="pack",
    )(core, grads, arrived)


def adam_kernel(own, near, far, cross, r_own, r_near, r_far, r_cross, m1, m2, first, second, direction):
    rotated = dot_f32(own[...], r_own[...]) + dot_f32(near[...], r_near[...])
    rotated += dot_f32(far[...], r_far[...]) + dot_f32(cross[...], r_cross[...])
    new1 = 0.9 * m1[0] + 0.1 * rotated
    new2 = 0.95 * m2[0] + 0.05 * rotated * rotated
    first[0] = new1
    second[0] = new2
    bias_first = 1.0 - 0.9**10
    bias_second = 1.0 - 0.95**10
    direction[...] = (new1 / bias_first / (jnp.sqrt(new2 / bias_second) + 1e-08)).astype(BF16)


def adam(terms, rights, moment_first, moment_second):
    tile = 256
    rows = pl.BlockSpec((tile, Q), lambda i: (i, 0))
    whole = pl.BlockSpec((Q, Q), lambda i: (0, 0))
    moment = pl.BlockSpec((1, tile, Q), lambda i: (0, i, 0))
    return pl.pallas_call(
        adam_kernel,
        grid=(BS // tile,),
        in_specs=[rows] * 4 + [whole] * 4 + [moment] * 2,
        out_specs=[moment, moment, rows],
        out_shape=[
            jax.ShapeDtypeStruct((1, BS, Q), F32),
            jax.ShapeDtypeStruct((1, BS, Q), F32),
            jax.ShapeDtypeStruct((BS, Q), BF16),
        ],
        compiler_params=PARAMS,
        cost_estimate=cost(8 * BS * Q * Q, 7 << 20),
        name="adam",
    )(*terms, *rights, moment_first, moment_second)


def update_kernel(own, near, r_own, r_near, left, out, turned):
    @pl.when(pl.program_id(0) == 0)
    def _():
        both = ((1,), (1,))
        total = dot_f32(own[...], r_own[...], both) + dot_f32(near[...], r_near[...], both)
        turned[...] = total.astype(BF16)

    share = dot_f32(left[...], turned[...]).astype(BF16)
    for group in range(2):
        out[:, group] = share[:, group * Q : (group + 1) * Q].reshape(out.shape[0], ROWS, Q)


def update(own, near, r_own, r_near, left):
    tile = 256
    whole = pl.BlockSpec((BS, Q), lambda i: (0, 0))
    right = pl.BlockSpec((2 * Q, Q), lambda i: (0, 0))
    return pl.pallas_call(
        update_kernel,
        grid=(BS // tile,),
        in_specs=[whole, whole, right, right, pl.BlockSpec((tile, BS), lambda i: (i, 0))],
        out_specs=pl.BlockSpec((tile // ROWS, 2, ROWS, Q), lambda i: (i, 0, 0, 0)),
        out_shape=jax.ShapeDtypeStruct((NB, 2, ROWS, Q), BF16),
        scratch_shapes=[pltpu.VMEM((BS, 2 * Q), BF16)],
        compiler_params=PARAMS,
        cost_estimate=cost(2 * BS * BS * 2 * Q + 8 * BS * Q * Q, 5 << 20),
        name="update",
    )(own, near, r_own, r_near, left)


def apply_kernel(pieces, weights, out):
    swap = swap_matrix()
    total = dot_f32(swap, pieces[:, 0].reshape(Q, Q)) + dot_f32(swap, pieces[:, 1].reshape(Q, Q))
    out[...] = weights[...] - 0.5 * total.reshape(ROWS, ROWS, Q)


def apply(pieces, weights):
    held = pl.BlockSpec((ROWS, ROWS, Q), lambda i: (0, i, 0))
    return pl.pallas_call(
        apply_kernel,
        grid=(NB // ROWS,),
        in_specs=[pl.BlockSpec((ROWS, 2, ROWS, Q), lambda i: (i, 0, 0, 0)), held],
        out_specs=held,
        out_shape=jax.ShapeDtypeStruct((ROWS, NB, Q), F32),
        compiler_params=PARAMS,
        cost_estimate=cost(4 * BS * Q * Q, 3 << 20),
        name="apply",
    )(pieces, weights)


def exchange(pieces):
    return lax.all_to_all(
        pieces.reshape(2 * NB, ROWS, Q), FSDP + ("x_hi",), split_axis=0, concat_axis=0, tiled=True
    ).reshape(NB, 2, ROWS, Q)


def local(grads, weights, moment_first, moment_second, left_basis, right_basis):
    core, x_hi = lax.axis_index("core"), lax.axis_index("x_hi")
    core_ref = core.astype(jnp.int32).reshape(1)
    left = left_basis[0]

    arrived = lax.ppermute(pick(core_ref, grads[0]), "core", SWAP)
    pieces = exchange(pack(core_ref, grads[0], arrived))

    low, high = right_basis[0, :, : 2 * Q], right_basis[0, :, 2 * Q :]
    right_half = jnp.where(x_hi == 0, low, high)
    right_far = lax.ppermute(jnp.where(x_hi == 0, high, low), "x_hi", SWAP)

    def part_of(half, which):
        return jnp.where(which == 0, half[:, :Q], half[:, Q:])

    r_own, r_far = part_of(right_half, core), part_of(right_far, core)
    n_own, n_far = part_of(right_half, 1 - core), part_of(right_far, 1 - core)
    r_near = lax.ppermute(n_own, "core", SWAP)
    r_cross = lax.ppermute(n_far, "core", SWAP)

    def by_chip(own, far):
        return jnp.where(x_hi == 0, jnp.concatenate([own, far]), jnp.concatenate([far, own]))

    rows_own, rows_near = by_chip(r_own, r_far), by_chip(n_own, n_far)

    grad_block = (pieces[:, 0].astype(F32) + pieces[:, 1].astype(F32)).astype(BF16).reshape(BS, Q)
    rl_own = dot_f32(left, grad_block, ((0,), (0,))).astype(BF16)
    rl_far = lax.ppermute(rl_own, "x_hi", SWAP)
    rl_near = lax.ppermute(rl_own, "core", SWAP)
    rl_cross = lax.ppermute(rl_far, "core", SWAP)
    first_new, second_new, direction = adam(
        (rl_own, rl_near, rl_far, rl_cross), (r_own, r_near, r_far, r_cross), moment_first, moment_second
    )
    near = lax.ppermute(direction, "core", SWAP)
    returned = exchange(update(direction, near, rows_own, rows_near, left))
    return (apply(returned, weights), first_new, second_new)


def solution(mesh):
    fine = Mesh(mesh.devices.reshape(8, 4, 2, 2, 2), FSDP + DP)
    placed = (
        P(DP, FSDP, None, None),
        P(FSDP, None, DP),
        P(FSDP, None, DP),
        P(FSDP, None, DP),
        P(FSDP, None, None),
        P(FSDP, DP, None),
    )
    return jax.shard_map(
        local,
        mesh=fine,
        in_specs=placed,
        out_specs=(P(FSDP, None, DP), P(FSDP, None, DP), P(FSDP, None, DP)),
        check_vma=False,
    )
```

time: 153 us -> 123 us (0.80); the launches traced: 152 us -> 123 us
  blocking collectives: 0 us -> 83.1 us
  waiting for transfers between devices: 62.8 us -> 20 us
  local copies, waits for them, and re-layouts: 35.2 us -> 1.62 us
  starting transfers between devices: 27.6 us -> 4.55 us
  matrix products: 11.8 us -> 0.94 us
  other arithmetic: 13.3 us -> 3.12 us
  Pallas kernels: 0 us -> 9.08 us
    all_to_all x0 -> x2, blocking collectives: none -> 83.1 us  [exchange(): lax.all_to_all(pieces.reshape(2 * NB, ROWS, Q), FSDP + ('x_hi',), split_a...]
    all_to_all x2 -> x0, waiting for transfers between devices: 47 us -> none  [the longest x1 25.9 us: local(): lax.all_to_all(jnp.stack(shares, axis=1).reshape(2 * blocks, rows, Q), FS...]
    all_to_all x2 -> x0, starting transfers between devices: 21.8 us -> none  [the longest x1 15 us: local(): lax.all_to_all(chip_sum.reshape(2 * blocks, rows, Q), FSDP + ('x_hi',), s...]
    unnamed x20 -> x12, local copies, waits for them, and re-layouts: 22.9 us -> 1.62 us
    dot_general x7 -> x1, matrix products: 11.8 us -> 0.94 us  [dot_f32(): return lax.dot_general(a, b, (dims, ((), ())), preferred_element_type=F32)]
    pallas_call x0 -> x5, Pallas kernels: none -> 9.08 us  [the longest x1 2.94 us: adam(): pl.pallas_call(adam_kernel, grid=(BS // tile,), in_specs=[rows] * 4 + [wh...]
    select_n x4 -> x0, local copies, waits for them, and re-layouts: 5.35 us -> none  [part_of(): return jnp.where(which == 0, half[:, :Q], half[:, Q:])]
    convert_element_type x3 -> x0, local copies, waits for them, and re-layouts: 3.58 us -> none  [the longest x2 2.49 us: local(): dot_f32(left, turned, plain).astype(BF16).reshape(blocks, rows, Q)]
  transfers between devices with their start and end apart: 9 -> 8, of which waited for: 6 -> 5; matrix products, arithmetic and copies ran while one was open for 11% -> 2% of each run, Pallas kernels for 0% -> 0%
where the time goes in v2:
time: 123 us
  blocking collectives  83.1 us (68%)
  waiting for transfers between devices  20 us (16%)
  Pallas kernels  9.08 us (7%)
  starting transfers between devices  4.55 us (4%)
  other arithmetic  3.12 us (3%)
  local copies, waits for them, and re-layouts  1.62 us (1%)
    all_to_all x2, blocking collectives, exchange(): lax.all_to_all(pieces.reshape(2 * NB, ROWS, Q), FSDP + ('x_hi',), split_a...  83.1 us
    ppermute x1, waiting for transfers between devices, local(): rl_far = lax.ppermute(rl_own, 'x_hi', SWAP)  11.1 us
    ppermute x1, waiting for transfers between devices, local(): right_far = lax.ppermute(jnp.where(x_hi == 0, high, low), 'x_hi', SWAP)  3.4 us
    pallas_call x1, Pallas kernels, adam(): pl.pallas_call(adam_kernel, grid=(BS // tile,), in_specs=[rows] * 4 + [wh...  2.94 us
    ppermute x1, waiting for transfers between devices, local(): arrived = lax.ppermute(pick(core_ref, grads[0]), 'core', SWAP)  2.65 us
    pallas_call x1, Pallas kernels, update(): pl.pallas_call(update_kernel, grid=(BS // tile,), in_specs=[whole, whole,...  2.52 us
  transfers between devices with their start and end apart: 8, of which 5 were waited for; matrix products, arithmetic and copies ran while one was open for 2% of the time, Pallas kernels for 0%

profile of v2, /device:TPU:32, one launch (start us, length us, event | category | flops | bytes accessed | tf_op | source)
XLA Modules:
  0.0 123.2 jit_solution(10678693798919980621)
XLA Ops:
  0.6 0.0 copy-start
  0.6 1.6 %copy-done = bf16[1,16,64,1024]{3,2,1,0:T(8,128)(2,1)S(1)} copy-done((bf16[1,16,64,1024]{3,2,1,0:T(8,128)(2,1)S(1)}, bf16[1,16,64,1024]{3,2,1,0:T(8,128)(2,1)}, u32[]{:S(2)}) %copy-start) | copy-done | bytes 2097176
  2.2 0.3 pick.1
  2.5 0.1 collective-permute-start
  2.6 2.6 %collective-permute-done.arrived_ref = bf16[2,16,64,256]{3,2,1,0:T(8,128)(2,1)S(1)} collective-permute-done((bf16[2,16,64,256]{3,2,1,0:T(8,128)(2,1)S(1)}, bf16[2,16,64,256]{3,2,1,0:T(8,128)(2,1)S(1)}, u32[]{:S(2)}, u32[]{:S(2)}) %collective-permute-start) | collective-permute-done | bytes 1048608 | tf_op jit(solution)/shard_map/ppermute | solution.py:177
  5.3 1.1 pack.1
  6.4 0.0 copy-start.4
  6.4 45.8 %all_to_all.10 = bf16[128,16,256]{2,1,0:T(8,128)(2,1)S(1)} all-to-all(bf16[128,16,256]{2,1,0:T(8,128)(2,1)S(1)} %bitcast.19), channel_id=1, replica_groups=mesh['z'=8,'y'=4,'x_lo'=2,'x_hi'=2,'core'=2] {'z','y','x_lo','x_hi'}, dimensions={0} | all-to-all | bytes 2097152 | tf_op jit(solution)/shard_map/all_to_all | solution.py:167
  52.2 0.1 add_convert_fusion
  52.4 0.0 copy-done.4
  52.4 0.0 copy-start.2
  52.4 0.0 copy-start.3
  52.4 0.9 fusion.own
  53.4 2.1 %collective-permute-start.2 = (bf16[1024,256]{1,0:T(8,128)(2,1)S(1)}, bf16[1024,256]{1,0:T(8,128)(2,1)S(1)}, u32[]{:S(2)}, u32[]{:S(2)}) collective-permute-start(bf16[1024,256]{1,0:T(8,128)(2,1)S(1)} %fusion.own), channel_id=1, source_target_pairs={{0,2},{2,0},{1,3},{3,1},{4,6},{6,4},{5,7},{7,5},{8,10},{10,8},{9,1... | collective-permute-start | bytes 1572872 | tf_op jit(solution)/shard_map/ppermute | solution.py:199
  55.5 1.8 %select_bitcast_fusion = (bf16[256,512]{1,0:T(8,128)(2,1)}, bf16[256,512]{1,0:T(8,128)(2,1)S(1)}) fusion(pred[]{:T(512)S(6)} %eq.7, bf16[1,256,1024]{2,1,0:T(8,128)(2,1)} %param.11), kind=kLoop, calls=%fused_computation.5 | loop fusion | flops 262144 | bytes 1048577 | tf_op jit(solution)/shard_map/jit(_where)/select_n | solution.py:182
  57.3 1.5 %collective-permute-start.5 = (bf16[256,512]{1,0:T(8,128)(2,1)}, bf16[256,512]{1,0:T(8,128)(2,1)}, u32[]{:S(2)}, u32[]{:S(2)}) collective-permute-start(bf16[256,512]{1,0:T(8,128)(2,1)} %get-tuple-element.9), channel_id=1, source_target_pairs={{0,2},{2,0},{1,3},{3,1},{4,6},{6,4},{5,7},{7,5},{8,10},{10,8},{9,1... | collective-permute-start | bytes 786440 | tf_op jit(solution)/shard_map/ppermute | solution.py:182
  58.8 0.0 collective-permute-start.1
  58.8 11.1 %collective-permute-done.2.far = bf16[1024,256]{1,0:T(8,128)(2,1)S(1)} collective-permute-done((bf16[1024,256]{1,0:T(8,128)(2,1)S(1)}, bf16[1024,256]{1,0:T(8,128)(2,1)S(1)}, u32[]{:S(2)}, u32[]{:S(2)}) %collective-permute-start.2) | collective-permute-done | bytes 524320 | tf_op jit(solution)/shard_map/ppermute | solution.py:199
  69.8 0.0 collective-permute-start.3
  69.8 0.6 collective-permute-start.4
  70.4 3.4 %collective-permute-done.5 = bf16[256,512]{1,0:T(8,128)(2,1)} collective-permute-done((bf16[256,512]{1,0:T(8,128)(2,1)}, bf16[256,512]{1,0:T(8,128)(2,1)}, u32[]{:S(2)}, u32[]{:S(2)}) %collective-permute-start.5) | collective-permute-done | bytes 262176 | tf_op jit(solution)/shard_map/ppermute | solution.py:182
  73.8 1.0 broadcast_select_fusion
  74.8 0.1 collective-permute-start.6
  74.9 0.0 collective-permute-done.4.r_near
  75.0 1.3 %collective-permute-done.6.r_cross = bf16[256,256]{1,0:T(8,128)(2,1)S(1)} collective-permute-done((bf16[256,256]{1,0:T(8,128)(2,1)S(1)}, bf16[256,256]{1,0:T(8,128)(2,1)S(1)}, u32[]{:S(2)}, u32[]{:S(2)}) %collective-permute-start.6) | collective-permute-done | bytes 131104 | tf_op jit(solution)/shard_map/ppermute | solution.py:190
  76.3 0.0 collective-permute-done.1.near
  76.3 0.0 collective-permute-done.3.cross
  76.3 0.0 copy-done.2
  76.3 0.0 copy-done.3
  76.3 0.0 copy-start.5
  76.3 2.9 %adam.1 = (f32[1,1024,256]{2,1,0:T(8,128)}, f32[1,1024,256]{2,1,0:T(8,128)}, bf16[1024,256]{1,0:T(8,128)(2,1)S(1)}) custom-call(bf16[1024,256]{1,0:T(8,128)(2,1)S(1)} %fusion.own, bf16[1024,256]{1,0:T(8,128)(2,1)S(1)} %collective-permute-done.1.near, bf16[1024,256]{1,0:T(8,128)(2,1)S(1)} %collective-permute-done.2.far, ...), custom_call_target="tpu_custom_call" | custom-call | flops 536870912 | bytes 7340032 | tf_op jit(solution)/shard_map/adam/pallas_call | solution.py:101
  79.2 0.1 collective-permute-start.7
  79.4 0.2 maximum_select_fusion
  79.6 1.6 %collective-permute-done.7.near = bf16[1024,256]{1,0:T(8,128)(2,1)S(1)} collective-permute-done((bf16[1024,256]{1,0:T(8,128)(2,1)S(1)}, bf16[1024,256]{1,0:T(8,128)(2,1)S(1)}, u32[]{:S(2)}, u32[]{:S(2)}) %collective-permute-start.7) | collective-permute-done | bytes 524320 | tf_op jit(solution)/shard_map/ppermute | solution.py:205
  81.2 0.0 copy-done.5
  81.2 2.5 %update.1 = bf16[64,2,16,256]{3,2,1,0:T(8,128)(2,1)S(1)} custom-call(bf16[1024,256]{1,0:T(8,128)(2,1)S(1)} %get-tuple-element.6.own, bf16[1024,256]{1,0:T(8,128)(2,1)S(1)} %collective-permute-done.7.near, bf16[512,256]{1,0:T(8,128)(2,1)S(1)} %get-tuple-element.15.r_own, bf16[512,256]{1,0:T(8,128)(2,1)S(1)} %get-tuple-element.16.r_near, ...), custom_call_target="tpu_custom_call" | custom-call | flops 1610612736 | bytes 5242880 | tf_op jit(solution)/shard_map/update/pallas_call | solution.py:133
  83.7 0.0 copy-start.1
  83.7 37.3 %all_to_all.11 = bf16[128,16,256]{2,1,0:T(8,128)(2,1)S(1)} all-to-all(bf16[128,16,256]{2,1,0:T(8,128)(2,1)S(1)} %bitcast.21), channel_id=1, replica_groups=mesh['z'=8,'y'=4,'x_lo'=2,'x_hi'=2,'core'=2] {'z','y','x_lo','x_hi'}, dimensions={0} | all-to-all | bytes 2097152 | tf_op jit(solution)/shard_map/all_to_all | solution.py:167
  121.0 0.0 copy-done.1
  121.0 2.2 %apply.1 = f32[16,64,256]{2,1,0:T(8,128)} custom-call(bf16[64,2,16,256]{3,2,1,0:T(8,128)(2,1)S(1)} %bitcast.20, f32[16,64,256]{2,1,0:T(8,128)S(1)} %copy-done.1), custom_call_target="tpu_custom_call" | custom-call | flops 268435456 | bytes 3145728 | tf_op jit(solution)/shard_map/apply/pallas_call | solution.py:154
  (1 shorter events, 0.0 us)
Async XLA Ops:
  0.6 1.6 %copy-start = (bf16[1,16,64,1024]{3,2,1,0:T(8,128)(2,1)S(1)}, bf16[1,16,64,1024]{3,2,1,0:T(8,128)(2,1)}, u32[]{:S(2)}) copy-start(bf16[1,16,64,1024]{3,2,1,0:T(8,128)(2,1)} %param.6) | copy-start | bytes 6291460
  2.5 2.7 %collective-permute-start = (bf16[2,16,64,256]{3,2,1,0:T(8,128)(2,1)S(1)}, bf16[2,16,64,256]{3,2,1,0:T(8,128)(2,1)S(1)}, u32[]{:S(2)}, u32[]{:S(2)}) collective-permute-start(bf16[2,16,64,256]{3,2,1,0:T(8,128)(2,1)S(1)} %pick.1), channel_id=1, source_target_pairs={{0,1},{1,0},{2,3},{3,2},{4,5},{5,4},{6,7},{7,6},{8,9},{9,8},{10,11... | collective-permute-start | bytes 3145736 | tf_op jit(solution)/shard_map/ppermute | solution.py:177
  6.4 46.0 %copy-start.4 = (bf16[1,1024,1024]{2,1,0:T(8,128)(2,1)S(1)}, bf16[1,1024,1024]{2,1,0:T(8,128)(2,1)}, u32[]{:S(2)}) copy-start(bf16[1,1024,1024]{2,1,0:T(8,128)(2,1)} %param.10) | copy-start | bytes 6291460
  52.4 23.9 %copy-start.2 = (f32[1,1024,256]{2,1,0:T(8,128)S(1)}, f32[1,1024,256]{2,1,0:T(8,128)}, u32[]{:S(2)}) copy-start(f32[1,1024,256]{2,1,0:T(8,128)} %m1.1) | copy-start | bytes 3145732
  52.4 23.9 %copy-start.3 = (f32[1,1024,256]{2,1,0:T(8,128)S(1)}, f32[1,1024,256]{2,1,0:T(8,128)}, u32[]{:S(2)}) copy-start(f32[1,1024,256]{2,1,0:T(8,128)} %m2.1) | copy-start | bytes 3145732
  53.4 16.5 %collective-permute-start.2 = (bf16[1024,256]{1,0:T(8,128)(2,1)S(1)}, bf16[1024,256]{1,0:T(8,128)(2,1)S(1)}, u32[]{:S(2)}, u32[]{:S(2)}) collective-permute-start(bf16[1024,256]{1,0:T(8,128)(2,1)S(1)} %fusion.own), channel_id=1, source_target_pairs={{0,2},{2,0},{1,3},{3,1},{4,6},{6,4},{5,7},{7,5},{8,10},{10,8},{9,1... | collective-permute-start | bytes 1572872 | tf_op jit(solution)/shard_map/ppermute | solution.py:199
  57.3 16.6 %collective-permute-start.5 = (bf16[256,512]{1,0:T(8,128)(2,1)}, bf16[256,512]{1,0:T(8,128)(2,1)}, u32[]{:S(2)}, u32[]{:S(2)}) collective-permute-start(bf16[256,512]{1,0:T(8,128)(2,1)} %get-tuple-element.9), channel_id=1, source_target_pairs={{0,2},{2,0},{1,3},{3,1},{4,6},{6,4},{5,7},{7,5},{8,10},{10,8},{9,1... | collective-permute-start | bytes 786440 | tf_op jit(solution)/shard_map/ppermute | solution.py:182
  58.8 17.5 %collective-permute-start.1 = (bf16[1024,256]{1,0:T(8,128)(2,1)S(1)}, bf16[1024,256]{1,0:T(8,128)(2,1)S(1)}, u32[]{:S(2)}, u32[]{:S(2)}) collective-permute-start(bf16[1024,256]{1,0:T(8,128)(2,1)S(1)} %fusion.own), channel_id=1, source_target_pairs={{0,1},{1,0},{2,3},{3,2},{4,5},{5,4},{6,7},{7,6},{8,9},{9,8},{10,11... | collective-permute-start | bytes 1572872 | tf_op jit(solution)/shard_map/ppermute | solution.py:200
  69.8 6.5 %collective-permute-start.3 = (bf16[1024,256]{1,0:T(8,128)(2,1)S(1)}, bf16[1024,256]{1,0:T(8,128)(2,1)S(1)}, u32[]{:S(2)}, u32[]{:S(2)}) collective-permute-start(bf16[1024,256]{1,0:T(8,128)(2,1)S(1)} %collective-permute-done.2.far), channel_id=1, source_target_pairs={{0,1},{1,0},{2,3},{3,2},{4,5},{5,4},{6,7},{7,6},{8,9},{9,8},{10,11... | collective-permute-start | bytes 1572872 | tf_op jit(solution)/shard_map/ppermute | solution.py:201
  69.8 5.1 %collective-permute-start.4 = (bf16[256,256]{1,0:T(8,128)(2,1)S(1)}, bf16[256,256]{1,0:T(8,128)(2,1)S(1)}, u32[]{:S(2)}, u32[]{:S(2)}) collective-permute-start(bf16[256,256]{1,0:T(8,128)(2,1)S(1)} %get-tuple-element.13), channel_id=1, source_target_pairs={{0,1},{1,0},{2,3},{3,2},{4,5},{5,4},{6,7},{7,6},{8,9},{9,8},{10,11... | collective-permute-start | bytes 393224 | tf_op jit(solution)/shard_map/ppermute | solution.py:189
  74.8 1.4 %collective-permute-start.6 = (bf16[256,256]{1,0:T(8,128)(2,1)S(1)}, bf16[256,256]{1,0:T(8,128)(2,1)S(1)}, u32[]{:S(2)}, u32[]{:S(2)}) collective-permute-start(bf16[256,256]{1,0:T(8,128)(2,1)S(1)} %get-tuple-element.11), channel_id=1, source_target_pairs={{0,1},{1,0},{2,3},{3,2},{4,5},{5,4},{6,7},{7,6},{8,9},{9,8},{10,11... | collective-permute-start | bytes 393224 | tf_op jit(solution)/shard_map/ppermute | solution.py:190
  76.3 4.9 %copy-start.5 = (bf16[1,1024,1024]{2,1,0:T(8,128)(2,1)S(1)}, bf16[1,1024,1024]{2,1,0:T(8,128)(2,1)}, u32[]{:S(2)}) copy-start(bf16[1,1024,1024]{2,1,0:T(8,128)(2,1)} %param.10) | copy-start | bytes 6291460
  79.2 1.9 %collective-permute-start.7 = (bf16[1024,256]{1,0:T(8,128)(2,1)S(1)}, bf16[1024,256]{1,0:T(8,128)(2,1)S(1)}, u32[]{:S(2)}, u32[]{:S(2)}) collective-permute-start(bf16[1024,256]{1,0:T(8,128)(2,1)S(1)} %get-tuple-element.6.own), channel_id=1, source_target_pairs={{0,1},{1,0},{2,3},{3,2},{4,5},{5,4},{6,7},{7,6},{8,9},{9,8},{10,11... | collective-permute-start | bytes 1572872 | tf_op jit(solution)/shard_map/ppermute | solution.py:205
  83.7 37.3 %copy-start.1 = (f32[16,64,256]{2,1,0:T(8,128)S(1)}, f32[16,64,256]{2,1,0:T(8,128)}, u32[]{:S(2)}) copy-start(f32[16,64,256]{2,1,0:T(8,128)} %weights.1) | copy-start | bytes 3145732

commit v3 on v2

v3 whole, which is shorter than its diff:
```python
import jax
import jax.numpy as jnp
from jax import lax
from jax.experimental import pallas as pl
from jax.experimental.pallas import tpu as pltpu
from jax.sharding import Mesh, PartitionSpec as P

FSDP = ("z", "y", "x_lo")
DP = ("x_hi", "core")
SWAP = [(0, 1), (1, 0)]
F32 = jnp.float32
BF16 = jnp.bfloat16
BS = 1024
NB = 64
ROWS = 16
Q = 256
H = 128
PLAIN = ((1,), (0,))
WIDE = pltpu.CompilerParams(vmem_limit_bytes=60 << 20)
PARAMS = pltpu.CompilerParams(vmem_limit_bytes=16 << 20)


def dot_f32(a, b, dims=PLAIN):
    return lax.dot_general(a, b, (dims, ((), ())), preferred_element_type=F32)


def cost(flops, moved):
    return pl.CostEstimate(flops=flops, bytes_accessed=moved, transcendentals=0)


def swap_matrix():
    to = lax.broadcasted_iota(jnp.int32, (Q, Q), 0)
    come = lax.broadcasted_iota(jnp.int32, (Q, Q), 1)
    hit = (to // ROWS == come % ROWS) & (to % ROWS == come // ROWS)
    return jnp.where(hit, 1.0, 0.0).astype(BF16)


def pick_kernel(at_ref, grads_ref, out_ref):
    out_ref[0] = grads_ref[...]


def pick(at, grads):
    return pl.pallas_call(
        pick_kernel,
        grid_spec=pltpu.PrefetchScalarGridSpec(
            num_scalar_prefetch=1,
            grid=(2,),
            in_specs=[pl.BlockSpec((ROWS, NB, H), lambda g, at: (0, 0, 4 * g + at[0]))],
            out_specs=pl.BlockSpec((1, ROWS, NB, H), lambda g, at: (g, 0, 0, 0)),
        ),
        out_shape=jax.ShapeDtypeStruct((2, ROWS, NB, H), BF16),
        compiler_params=WIDE,
        cost_estimate=cost(0, 2 << 20),
        name="pick",
    )(at, grads)


def pair_sum(grads_ref, arrived_ref, store):
    swap = swap_matrix()
    for part in range(NB // ROWS):
        here = pl.ds(part * ROWS, ROWS)
        total = dot_f32(swap, grads_ref[:, here, :].reshape(Q, H))
        total += dot_f32(swap, arrived_ref[0, :, here, :].reshape(Q, H))
        store(here, total.astype(BF16).reshape(ROWS, ROWS, H))


def pack_both_kernel(at_ref, grads_ref, arrived_ref, out_ref):
    def store(here, value):
        out_ref[here, 0] = value

    pair_sum(grads_ref, arrived_ref, store)


def pack_both(at, grads, arrived):
    return pl.pallas_call(
        pack_both_kernel,
        grid_spec=pltpu.PrefetchScalarGridSpec(
            num_scalar_prefetch=1,
            grid=(2,),
            in_specs=[
                pl.BlockSpec((ROWS, NB, H), lambda g, at: (0, 0, 4 * g + at[0])),
                pl.BlockSpec((1, ROWS, NB, H), lambda g, at: (g, 0, 0, 0)),
            ],
            out_specs=pl.BlockSpec((NB, 1, ROWS, H), lambda g, at: (0, g, 0, 0)),
        ),
        out_shape=jax.ShapeDtypeStruct((NB, 2, ROWS, H), BF16),
        compiler_params=WIDE,
        cost_estimate=cost(4 * BS * Q * Q, 2 << 20),
        name="pack_both",
    )(at, grads, arrived)


def pack_one_kernel(at_ref, grads_ref, arrived_ref, out_ref):
    def store(here, value):
        out_ref[here] = value

    pair_sum(grads_ref, arrived_ref, store)


def pack_one(at, grads, arrived):
    return pl.pallas_call(
        pack_one_kernel,
        grid_spec=pltpu.PrefetchScalarGridSpec(
            num_scalar_prefetch=1,
            grid=(1,),
            in_specs=[
                pl.BlockSpec((ROWS, NB, H), lambda g, at: (0, 0, at[0])),
                pl.BlockSpec((1, ROWS, NB, H), lambda g, at: (at[1], 0, 0, 0)),
            ],
            out_specs=pl.BlockSpec((NB, ROWS, H), lambda g, at: (0, 0, 0)),
        ),
        out_shape=jax.ShapeDtypeStruct((NB, ROWS, H), BF16),
        compiler_params=PARAMS,
        cost_estimate=cost(2 * BS * Q * Q, 1 << 20),
        name="pack_one",
    )(at, grads, arrived)


def double_kernel(here, there, out):
    total = (here[...].astype(F32) + there[...].astype(F32)).astype(BF16)
    out[:, 0] = total
    out[:, 1] = total


def double(here, there):
    part = NB // 2
    held = pl.BlockSpec((part, ROWS, H), lambda i: (i, 0, 0))
    return pl.pallas_call(
        double_kernel,
        grid=(2,),
        in_specs=[held, held],
        out_specs=pl.BlockSpec((part, 2, ROWS, H), lambda i: (i, 0, 0, 0)),
        out_shape=jax.ShapeDtypeStruct((NB, 2, ROWS, H), BF16),
        compiler_params=PARAMS,
        cost_estimate=cost(1 << 18, 1 << 20),
        name="double",
    )(here, there)


def total_kernel(pieces, after, more, out):
    total = pieces[:, 0].astype(F32) + pieces[:, 1].astype(F32)
    out[...] = total.astype(BF16).reshape(BS, H)


def total(pieces, after, more):
    return pl.pallas_call(
        total_kernel,
        grid=(1,),
        in_specs=[
            pl.BlockSpec((NB, 2, ROWS, H), lambda i: (0, 0, 0, 0)),
            pl.BlockSpec(memory_space=pl.ANY),
            pl.BlockSpec(memory_space=pl.ANY),
        ],
        out_specs=pl.BlockSpec((BS, H), lambda i: (0, 0)),
        out_shape=jax.ShapeDtypeStruct((BS, H), BF16),
        compiler_params=PARAMS,
        cost_estimate=cost(1 << 18, 1 << 20),
        name="total",
    )(pieces, after, more)


def join_kernel(pieces, after, out):
    for group in range(2):
        out[:, group * H : (group + 1) * H] = pieces[:, group].reshape(BS, H)


def join(pieces, after):
    return pl.pallas_call(
        join_kernel,
        grid=(1,),
        in_specs=[
            pl.BlockSpec((NB, 2, ROWS, H), lambda i: (0, 0, 0, 0)),
            pl.BlockSpec(memory_space=pl.ANY),
        ],
        out_specs=pl.BlockSpec((BS, Q), lambda i: (0, 0)),
        out_shape=jax.ShapeDtypeStruct((BS, Q), BF16),
        compiler_params=PARAMS,
        cost_estimate=cost(0, 1 << 20),
        name="join",
    )(pieces, after)


def adam_kernel(chip, own, far, near, cross, mine, other, r_mine, r_other, m1, m2, first, second, direction):
    def side(left_a, left_b, b, right):
        a = jnp.concatenate([left_a[...], left_b[...]], axis=1)
        right_a = right[:, :H].reshape(Q, Q)
        right_b = jnp.concatenate([right[chip[0], H:], right[1 - chip[0], H:]], axis=0)
        return dot_f32(a, right_a) + dot_f32(b[...], right_b)

    rotated = side(own, far, mine, r_mine) + side(near, cross, other, r_other)
    new1 = 0.9 * m1[0] + 0.1 * rotated
    new2 = 0.95 * m2[0] + 0.05 * rotated * rotated
    first[0] = new1
    second[0] = new2
    bias_first = 1.0 - 0.9**10
    bias_second = 1.0 - 0.95**10
    direction[...] = (new1 / bias_first / (jnp.sqrt(new2 / bias_second) + 1e-08)).astype(BF16)


def adam(chip, halves, wholes, rights, moment_first, moment_second):
    tile = 256
    half = pl.BlockSpec((tile, H), lambda i, chip: (i, 0))
    rows = pl.BlockSpec((tile, Q), lambda i, chip: (i, 0))
    right = pl.BlockSpec((2, Q, Q), lambda i, chip: (0, 0, 0))
    moment = pl.BlockSpec((1, tile, Q), lambda i, chip: (0, i, 0))
    return pl.pallas_call(
        adam_kernel,
        grid_spec=pltpu.PrefetchScalarGridSpec(
            num_scalar_prefetch=1,
            grid=(BS // tile,),
            in_specs=[half] * 4 + [rows] * 2 + [right] * 2 + [moment] * 2,
            out_specs=[moment, moment, rows],
        ),
        out_shape=[
            jax.ShapeDtypeStruct((1, BS, Q), F32),
            jax.ShapeDtypeStruct((1, BS, Q), F32),
            jax.ShapeDtypeStruct((BS, Q), BF16),
        ],
        compiler_params=PARAMS,
        cost_estimate=cost(8 * BS * Q * Q, 7 << 20),
        name="adam",
    )(chip, *halves, *wholes, *rights, moment_first, moment_second)


def update_kernel(chip, own, near, r_own, r_near, left, out, turned):
    @pl.when(pl.program_id(0) == 0)
    def _():
        both = ((1,), (1,))
        for group in range(2):
            at = chip[0] if group == 0 else 1 - chip[0]
            total = dot_f32(own[...], r_own[at], both) + dot_f32(near[...], r_near[at], both)
            turned[:, group * Q : (group + 1) * Q] = total.astype(BF16)

    share = dot_f32(left[...], turned[...]).astype(BF16)
    for group in range(2):
        out[:, group] = share[:, group * Q : (group + 1) * Q].reshape(out.shape[0], ROWS, Q)


def update(chip, own, near, r_own, r_near, left):
    tile = 256
    whole = pl.BlockSpec((BS, Q), lambda i, chip: (0, 0))
    right = pl.BlockSpec((2, Q, Q), lambda i, chip: (0, 0, 0))
    return pl.pallas_call(
        update_kernel,
        grid_spec=pltpu.PrefetchScalarGridSpec(
            num_scalar_prefetch=1,
            grid=(BS // tile,),
            in_specs=[whole, whole, right, right, pl.BlockSpec((tile, BS), lambda i, chip: (i, 0))],
            out_specs=pl.BlockSpec((tile // ROWS, 2, ROWS, Q), lambda i, chip: (i, 0, 0, 0)),
            scratch_shapes=[pltpu.VMEM((BS, 2 * Q), BF16)],
        ),
        out_shape=jax.ShapeDtypeStruct((NB, 2, ROWS, Q), BF16),
        compiler_params=PARAMS,
        cost_estimate=cost(2 * BS * BS * 2 * Q + 8 * BS * Q * Q, 5 << 20),
        name="update",
    )(chip, own, near, r_own, r_near, left)


def apply_kernel(pieces, weights, out):
    swap = swap_matrix()
    total = dot_f32(swap, pieces[:, 0].reshape(Q, Q)) + dot_f32(swap, pieces[:, 1].reshape(Q, Q))
    out[...] = weights[...] - 0.5 * total.reshape(ROWS, ROWS, Q)


def apply(pieces, weights):
    held = pl.BlockSpec((ROWS, ROWS, Q), lambda i: (0, i, 0))
    return pl.pallas_call(
        apply_kernel,
        grid=(NB // ROWS,),
        in_specs=[pl.BlockSpec((ROWS, 2, ROWS, Q), lambda i: (i, 0, 0, 0)), held],
        out_specs=held,
        out_shape=jax.ShapeDtypeStruct((ROWS, NB, Q), F32),
        compiler_params=PARAMS,
        cost_estimate=cost(4 * BS * Q * Q, 3 << 20),
        name="apply",
    )(pieces, weights)


def exchange(pieces):
    width = pieces.shape[-1]
    return lax.all_to_all(
        pieces.reshape(2 * NB, ROWS, width), FSDP + ("x_hi",), split_axis=0, concat_axis=0, tiled=True
    ).reshape(NB, 2, ROWS, width)


def local(grads, weights, moment_first, moment_second, left_basis, right_basis):
    core = lax.axis_index("core").astype(jnp.int32)
    x_hi = lax.axis_index("x_hi").astype(jnp.int32)
    slab = grads[0]
    left = left_basis[0]

    mine, other = 2 * core, 2 * (1 - core)
    sent_a = lax.ppermute(pick(other.reshape(1), slab), "core", SWAP)
    sent_b = lax.ppermute(pick((other + 1).reshape(1), slab), "core", SWAP)

    pieces_a = exchange(pack_both(mine.reshape(1), slab, sent_a))

    def group_b(group):
        return pack_one(jnp.stack([4 * group + mine + 1, group]), slab, sent_b)

    far_b = lax.ppermute(group_b(1 - x_hi), "x_hi", SWAP)
    both_b = double(group_b(x_hi), far_b)
    pieces_b = exchange(both_b)

    low, high = right_basis[0, :, : 2 * Q], right_basis[0, :, 2 * Q :]
    right_half = jnp.where(x_hi == 0, low, high)
    right_far = lax.ppermute(jnp.where(x_hi == 0, high, low), "x_hi", SWAP)
    right_rows = jnp.stack([right_half, right_far])
    r_mine = jnp.where(core == 0, right_rows[:, :, :Q], right_rows[:, :, Q:])
    r_near = jnp.where(core == 0, right_rows[:, :, Q:], right_rows[:, :, :Q])
    r_other = lax.ppermute(r_near, "core", SWAP)

    rl_a = dot_f32(left, total(pieces_a, both_b, r_other), ((0,), (0,))).astype(BF16)
    far_a = lax.ppermute(rl_a, "x_hi", SWAP)
    near_a = lax.ppermute(rl_a, "core", SWAP)
    cross_a = lax.ppermute(far_a, "core", SWAP)
    rl_b = dot_f32(left, join(pieces_b, far_a), ((0,), (0,))).astype(BF16)
    chip = x_hi.reshape(1)
    first_new, second_new, direction = adam(
        chip,
        (rl_a, far_a, near_a, cross_a),
        (rl_b, lax.ppermute(rl_b, "core", SWAP)),
        (r_mine, r_other),
        moment_first,
        moment_second,
    )
    near = lax.ppermute(direction, "core", SWAP)
    share = update(chip, direction, near, r_mine, r_near, left)
    return (apply(exchange(share), weights), first_new, second_new)


def solution(mesh):
    fine = Mesh(mesh.devices.reshape(8, 4, 2, 2, 2), FSDP + DP)
    placed = (
        P(DP, FSDP, None, None),
        P(FSDP, None, DP),
        P(FSDP, None, DP),
        P(FSDP, None, DP),
        P(FSDP, None, None),
        P(FSDP, DP, None),
    )
    return jax.shard_map(
        local,
        mesh=fine,
        in_specs=placed,
        out_specs=(P(FSDP, None, DP), P(FSDP, None, DP), P(FSDP, None, DP)),
        check_vma=False,
    )
```

time: 123 us -> 129 us (1.049)
  blocking collectives: 83.1 us -> 40.5 us
  starting transfers between devices: 4.55 us -> 34.6 us
  Pallas kernels: 9.08 us -> 17.7 us
  waiting for transfers between devices: 20 us -> 28.6 us
    all_to_all x2 -> x1, blocking collectives: 83.1 us -> 40.5 us  [exchange(): lax.all_to_all(pieces.reshape(2 * NB, ROWS, width), FSDP + ('x_hi',), spl...]
    all_to_all x0 -> x2, starting transfers between devices: none -> 27 us  [exchange(): lax.all_to_all(pieces.reshape(2 * NB, ROWS, width), FSDP + ('x_hi',), spl...]
    all_to_all x0 -> x2, waiting for transfers between devices: none -> 11.9 us  [exchange(): lax.all_to_all(pieces.reshape(2 * NB, ROWS, width), FSDP + ('x_hi',), spl...]
    pallas_call x3 -> x8, Pallas kernels: 6.59 us -> 12 us  [the longest x1 2.98 us: adam(): pl.pallas_call(adam_kernel, grid_spec=pltpu.PrefetchScalarGridSpec(num_sc...]
    ppermute x6 -> x8, starting transfers between devices: 2.9 us -> 6.9 us  [the longest x1 3.06 us: local(): far_b = lax.ppermute(group_b(1 - x_hi), 'x_hi', SWAP)]
    ppermute x1, waiting for transfers between devices: 3.4 us -> 0.01 us  [local(): right_far = lax.ppermute(jnp.where(x_hi == 0, high, low), 'x_hi', SWAP)]
    pallas_call x1 -> x2, Pallas kernels: 0.27 us -> 3.56 us  [pick(): pl.pallas_call(pick_kernel, grid_spec=pltpu.PrefetchScalarGridSpec(num_sc...]
    select_n x4 -> x2, other arithmetic: 2.98 us -> 2.14 us  [the longest x1 1.31 us: local(): r_mine = jnp.where(core == 0, right_rows[:, :, :Q], right_rows[:, :, Q:])]
  transfers between devices with their start and end apart: 8 -> 12, of which waited for: 5 -> 9; matrix products, arithmetic and copies ran while one was open for 2% -> 3% of each run, Pallas kernels for 0% -> 4%
where the time goes in v3:
time: 129 us
  blocking collectives  40.5 us (31%)
  starting transfers between devices  34.6 us (27%)
  waiting for transfers between devices  28.6 us (22%)
  Pallas kernels  17.7 us (14%)
  other arithmetic  2.29 us (2%)
  local copies, waits for them, and re-layouts  2.21 us (2%)
  matrix products  1.87 us (1%)
    all_to_all x1, blocking collectives, exchange(): lax.all_to_all(pieces.reshape(2 * NB, ROWS, width), FSDP + ('x_hi',), spl...  40.5 us
    all_to_all x2, starting transfers between devices, exchange(): lax.all_to_all(pieces.reshape(2 * NB, ROWS, width), FSDP + ('x_hi',), spl...  27 us
    all_to_all x2, waiting for transfers between devices, exchange(): lax.all_to_all(pieces.reshape(2 * NB, ROWS, width), FSDP + ('x_hi',), spl...  11.9 us
    ppermute x1, waiting for transfers between devices, local(): far_b = lax.ppermute(group_b(1 - x_hi), 'x_hi', SWAP)  7.82 us
    pallas_call x2, Pallas kernels, pick(): pl.pallas_call(pick_kernel, grid_spec=pltpu.PrefetchScalarGridSpec(num_sc...  3.56 us
    ppermute x1, starting transfers between devices, local(): far_b = lax.ppermute(group_b(1 - x_hi), 'x_hi', SWAP)  3.06 us
    ppermute x1, starting transfers between devices, local(): far_a = lax.ppermute(rl_a, 'x_hi', SWAP)  3.05 us
    pallas_call x1, Pallas kernels, adam(): pl.pallas_call(adam_kernel, grid_spec=pltpu.PrefetchScalarGridSpec(num_sc...  2.98 us
  transfers between devices with their start and end apart: 12, of which 9 were waited for; matrix products, arithmetic and copies ran while one was open for 3% of the time, Pallas kernels for 4%

profile of v3, /device:TPU:32, one launch (start us, length us, event | category | flops | bytes accessed | tf_op | source)
XLA Modules:
  0.0 128.5 jit_solution(9263094390085988662)
XLA Ops:
  0.6 1.8 %pick.2 = bf16[2,16,64,128]{3,2,1,0:T(8,128)(2,1)} custom-call(s32[1]{0:T(128)} %bitcast.3.at_ref, bf16[16,64,1024]{2,1,0:T(8,128)(2,1)} %bitcast.28), custom_call_target="tpu_custom_call" | custom-call | bytes 2097152 | tf_op jit(solution)/shard_map/pick/pallas_call | solution.py:43
  2.4 0.0 collective-permute-start
  2.4 2.1 %collective-permute-done.arrived_ref = bf16[2,16,64,128]{3,2,1,0:T(8,128)(2,1)S(1)} collective-permute-done((bf16[2,16,64,128]{3,2,1,0:T(8,128)(2,1)}, bf16[2,16,64,128]{3,2,1,0:T(8,128)(2,1)S(1)}, u32[]{:S(2)}, u32[]{:S(2)}) %collective-permute-start) | collective-permute-done | bytes 524320 | tf_op jit(solution)/shard_map/ppermute | solution.py:293
  4.5 0.8 copy-done.10
  5.3 2.6 %pack_both.1 = bf16[64,2,16,128]{3,2,1,0:T(8,128)(2,1)} custom-call(s32[1]{0:T(128)} %bitcast.1.at_ref, bf16[16,64,1024]{2,1,0:T(8,128)(2,1)} %bitcast.29, bf16[2,16,64,128]{3,2,1,0:T(8,128)(2,1)} %copy-done.10), custom_call_target="tpu_custom_call" | custom-call | flops 268435456 | bytes 2097152 | tf_op jit(solution)/shard_map/pack_both/pallas_call | solution.py:75
  8.0 15.1 %all-to-all-start = ((bf16[128,16,128]{2,1,0:T(8,128)(2,1)}), bf16[128,16,128]{2,1,0:T(8,128)(2,1)S(1)}, u32[]{:S(2)}, u32[]{:S(2)}) async-start(bf16[128,16,128]{2,1,0:T(8,128)(2,1)} %bitcast.38), calls=%async_computation | async-start | bytes 1048576 | tf_op jit(solution)/shard_map/all_to_all | solution.py:281
  23.1 1.8 %pick.3 = bf16[2,16,64,128]{3,2,1,0:T(8,128)(2,1)} custom-call(s32[1]{0:T(128)} %bitcast.7.at_ref, bf16[16,64,1024]{2,1,0:T(8,128)(2,1)} %bitcast.30), custom_call_target="tpu_custom_call" | custom-call | bytes 2097152 | tf_op jit(solution)/shard_map/pick/pallas_call | solution.py:43
  24.9 0.0 collective-permute-start.1
  24.9 0.1 pad_add_fusion.1.at_ref
  25.0 2.0 %collective-permute-done.1.arrived_ref = bf16[2,16,64,128]{3,2,1,0:T(8,128)(2,1)S(1)} collective-permute-done((bf16[2,16,64,128]{3,2,1,0:T(8,128)(2,1)}, bf16[2,16,64,128]{3,2,1,0:T(8,128)(2,1)S(1)}, u32[]{:S(2)}, u32[]{:S(2)}) %collective-permute-start.1) | collective-permute-done | bytes 524320 | tf_op jit(solution)/shard_map/ppermute | solution.py:294
  27.0 1.0 pack_one.3
  28.0 3.1 %collective-permute-start.2 = (bf16[64,16,128]{2,1,0:T(8,128)(2,1)S(1)}, bf16[64,16,128]{2,1,0:T(8,128)(2,1)}, u32[]{:S(2)}, u32[]{:S(2)}) collective-permute-start(bf16[64,16,128]{2,1,0:T(8,128)(2,1)S(1)} %pack_one.3), channel_id=1, source_target_pairs={{0,2},{2,0},{1,3},{3,1},{4,6},{6,4},{5,7},{7,5},{8,10},{10,8},{9,1... | collective-permute-start | bytes 786440 | tf_op jit(solution)/shard_map/ppermute | solution.py:301
  31.1 0.8 broadcast_select_fusion
  31.9 0.6 collective-permute-start.3
  32.5 0.1 pad_add_fusion.at_ref
  32.5 1.0 pack_one.2.here
  33.5 7.8 %collective-permute-done.2.there = bf16[64,16,128]{2,1,0:T(8,128)(2,1)} collective-permute-done((bf16[64,16,128]{2,1,0:T(8,128)(2,1)S(1)}, bf16[64,16,128]{2,1,0:T(8,128)(2,1)}, u32[]{:S(2)}, u32[]{:S(2)}) %collective-permute-start.2) | collective-permute-done | bytes 262176 | tf_op jit(solution)/shard_map/ppermute | solution.py:301
  41.3 1.7 %double.1.after = bf16[64,2,16,128]{3,2,1,0:T(8,128)(2,1)} custom-call(bf16[64,16,128]{2,1,0:T(8,128)(2,1)S(1)} %pack_one.2.here, bf16[64,16,128]{2,1,0:T(8,128)(2,1)} %collective-permute-done.2.there), custom_call_target="tpu_custom_call" | custom-call | flops 262144 | bytes 1048576 | tf_op jit(solution)/shard_map/double/pallas_call | solution.py:128
  43.1 0.2 all-to-all-done
  43.2 11.8 %all-to-all-start.1 = ((bf16[128,16,128]{2,1,0:T(8,128)(2,1)}), bf16[128,16,128]{2,1,0:T(8,128)(2,1)S(1)}, u32[]{:S(2)}, u32[]{:S(2)}) async-start(bf16[128,16,128]{2,1,0:T(8,128)(2,1)} %bitcast.14), calls=%async_computation.1 | async-start | bytes 1048576 | tf_op jit(solution)/shard_map/all_to_all | solution.py:281
  55.1 0.0 collective-permute-done.3
  55.1 1.3 %broadcast_select_fusion.1 = (bf16[2,256,256]{2,1,0:T(8,128)(2,1)S(1)}, bf16[2,256,256]{2,1,0:T(8,128)(2,1)S(1)}) fusion(pred[]{:T(512)S(6)} %eq.8, bf16[1,256,512]{2,1,0:T(8,128)(2,1)} %bitcast.11, bf16[1,256,512]{2,1,0:T(8,128)(2,1)} %get-tuple-element.11), kind=kLoop, calls=%fused_computation.10 | loop fusion | flops 1835008 | bytes 1048577 | tf_op jit(solution)/shard_map/jit(_where)/select_n | solution.py:309
  56.4 0.1 collective-permute-start.4
  56.5 0.0 copy-start.7
  56.5 0.7 copy-done.7
  57.2 0.8 collective-permute-done.4.more.r_other
  58.0 0.1 total.1
  58.1 0.0 copy-start.5
  58.1 0.7 copy-done.5
  58.8 0.9 fusion.1.own
  59.7 3.1 %collective-permute-start.5 = (bf16[1024,128]{1,0:T(8,128)(2,1)S(1)}, bf16[1024,128]{1,0:T(8,128)(2,1)S(1)}, u32[]{:S(2)}, u32[]{:S(2)}) collective-permute-start(bf16[1024,128]{1,0:T(8,128)(2,1)S(1)} %fusion.1.own), channel_id=1, source_target_pairs={{0,2},{2,0},{1,3},{3,1},{4,6},{6,4},{5,7},{7,5},{8,10},{10,8},{9,1... | collective-permute-start | bytes 786440 | tf_op jit(solution)/shard_map/ppermute | solution.py:314
  62.8 11.8 %all-to-all-done.1 = bf16[128,16,128]{2,1,0:T(8,128)(2,1)S(1)} async-done(((bf16[128,16,128]{2,1,0:T(8,128)(2,1)}), bf16[128,16,128]{2,1,0:T(8,128)(2,1)S(1)}, u32[]{:S(2)}, u32[]{:S(2)}) %all-to-all-start.1) | async-done | bytes 524320 | tf_op jit(solution)/shard_map/all_to_all | solution.py:281
  74.6 0.0 collective-permute-done.5.after.far
  74.6 0.1 join.1
  74.7 0.9 fusion.mine
  75.6 0.1 collective-permute-start.8
  75.7 0.5 collective-permute-start.6
  76.2 0.1 collective-permute-start.7
  76.3 1.7 %collective-permute-done.6.near = bf16[1024,128]{1,0:T(8,128)(2,1)S(1)} collective-permute-done((bf16[1024,128]{1,0:T(8,128)(2,1)S(1)}, bf16[1024,128]{1,0:T(8,128)(2,1)S(1)}, u32[]{:S(2)}, u32[]{:S(2)}) %collective-permute-start.6) | collective-permute-done | bytes 262176 | tf_op jit(solution)/shard_map/ppermute | solution.py:315
  78.0 0.4 collective-permute-done.7.cross
  78.3 0.0 collective-permute-done.8.other
  78.4 3.0 %adam.1 = (f32[1,1024,256]{2,1,0:T(8,128)}, f32[1,1024,256]{2,1,0:T(8,128)}, bf16[1024,256]{1,0:T(8,128)(2,1)S(1)}) custom-call(s32[1]{0:T(128)} %bitcast.chip, bf16[1024,128]{1,0:T(8,128)(2,1)S(1)} %fusion.1.own, bf16[1024,128]{1,0:T(8,128)(2,1)S(1)} %collective-permute-done.5.after.far, bf16[1024,128]{1,0:T(8,128)(2,1)S(1)} %collective-permute-done.6.near, ...), custom_call_target="tpu_custom_call" | custom-call | flops 536870912 | bytes 7340032 | tf_op jit(solution)/shard_map/adam/pallas_call | solution.py:206
  81.4 0.1 collective-permute-start.9
  81.5 1.8 %collective-permute-done.9.near = bf16[1024,256]{1,0:T(8,128)(2,1)S(1)} collective-permute-done((bf16[1024,256]{1,0:T(8,128)(2,1)S(1)}, bf16[1024,256]{1,0:T(8,128)(2,1)S(1)}, u32[]{:S(2)}, u32[]{:S(2)}) %collective-permute-start.9) | collective-permute-done | bytes 524320 | tf_op jit(solution)/shard_map/ppermute | solution.py:327
  83.3 2.5 %update.1 = bf16[64,2,16,256]{3,2,1,0:T(8,128)(2,1)S(1)} custom-call(s32[1]{0:T(128)} %bitcast.chip, bf16[1024,256]{1,0:T(8,128)(2,1)S(1)} %get-tuple-element.6.own, bf16[1024,256]{1,0:T(8,128)(2,1)S(1)} %collective-permute-done.9.near, bf16[2,256,256]{2,1,0:T(8,128)(2,1)S(1)} %get-tuple-element.9.r_mine.r_own, bf16[2,256,256]{2,1,0:T(8,128)(2,1)S(1)} %copy-done.8, ...), custom_call_target="tpu_custom_call" | custom-call | flops 1610612736 | bytes 5242880 | tf_op jit(solution)/shard_map/update/pallas_call | solution.py:243
  85.8 0.0 copy-start.4
  85.8 40.5 %all_to_all.15 = bf16[128,16,256]{2,1,0:T(8,128)(2,1)S(1)} all-to-all(bf16[128,16,256]{2,1,0:T(8,128)(2,1)S(1)} %bitcast.37), channel_id=1, replica_groups=mesh['z'=8,'y'=4,'x_lo'=2,'x_hi'=2,'core'=2] {'z','y','x_lo','x_hi'}, dimensions={0} | all-to-all | bytes 2097152 | tf_op jit(solution)/shard_map/all_to_all | solution.py:281
  126.3 2.2 %apply.1 = f32[16,64,256]{2,1,0:T(8,128)} custom-call(bf16[64,2,16,256]{3,2,1,0:T(8,128)(2,1)S(1)} %bitcast.33, f32[16,64,256]{2,1,0:T(8,128)S(1)} %copy-done.4), custom_call_target="tpu_custom_call" | custom-call | flops 268435456 | bytes 3145728 | tf_op jit(solution)/shard_map/apply/pallas_call | solution.py:267
  (16 shorter events, 0.0 us)
Async XLA Ops:
  2.4 2.1 %collective-permute-start = (bf16[2,16,64,128]{3,2,1,0:T(8,128)(2,1)}, bf16[2,16,64,128]{3,2,1,0:T(8,128)(2,1)S(1)}, u32[]{:S(2)}, u32[]{:S(2)}) collective-permute-start(bf16[2,16,64,128]{3,2,1,0:T(8,128)(2,1)} %pick.2), channel_id=1, source_target_pairs={{0,1},{1,0},{2,3},{3,2},{4,5},{5,4},{6,7},{7,6},{8,9},{9,8},{10,11... | collective-permute-start | bytes 1572872 | tf_op jit(solution)/shard_map/ppermute | solution.py:293
  4.5 0.8 copy-start.10
  8.0 19.1 %copy-start = (bf16[1,16,64,1024]{3,2,1,0:T(8,128)(2,1)S(1)}, bf16[1,16,64,1024]{3,2,1,0:T(8,128)(2,1)}, u32[]{:S(2)}) copy-start(bf16[1,16,64,1024]{3,2,1,0:T(8,128)(2,1)} %param.6) | copy-start | bytes 6291460
  8.0 35.3 %all-to-all-start = ((bf16[128,16,128]{2,1,0:T(8,128)(2,1)}), bf16[128,16,128]{2,1,0:T(8,128)(2,1)S(1)}, u32[]{:S(2)}, u32[]{:S(2)}) async-start(bf16[128,16,128]{2,1,0:T(8,128)(2,1)} %bitcast.38), calls=%async_computation | async-start | bytes 1048576 | tf_op jit(solution)/shard_map/all_to_all | solution.py:281
  24.9 2.1 %collective-permute-start.1 = (bf16[2,16,64,128]{3,2,1,0:T(8,128)(2,1)}, bf16[2,16,64,128]{3,2,1,0:T(8,128)(2,1)S(1)}, u32[]{:S(2)}, u32[]{:S(2)}) collective-permute-start(bf16[2,16,64,128]{3,2,1,0:T(8,128)(2,1)} %pick.3), channel_id=1, source_target_pairs={{0,1},{1,0},{2,3},{3,2},{4,5},{5,4},{6,7},{7,6},{8,9},{9,8},{10,11... | collective-permute-start | bytes 1572872 | tf_op jit(solution)/shard_map/ppermute | solution.py:294
  24.9 6.2 %copy-start.9 = (bf16[1,256,1024]{2,1,0:T(8,128)(2,1)S(1)}, bf16[1,256,1024]{2,1,0:T(8,128)(2,1)}, u32[]{:S(2)}) copy-start(bf16[1,256,1024]{2,1,0:T(8,128)(2,1)} %param.11) | copy-start | bytes 1572868
  28.0 13.3 %collective-permute-start.2 = (bf16[64,16,128]{2,1,0:T(8,128)(2,1)S(1)}, bf16[64,16,128]{2,1,0:T(8,128)(2,1)}, u32[]{:S(2)}, u32[]{:S(2)}) collective-permute-start(bf16[64,16,128]{2,1,0:T(8,128)(2,1)S(1)} %pack_one.3), channel_id=1, source_target_pairs={{0,2},{2,0},{1,3},{3,1},{4,6},{6,4},{5,7},{7,5},{8,10},{10,8},{9,1... | collective-permute-start | bytes 786440 | tf_op jit(solution)/shard_map/ppermute | solution.py:301
  31.9 23.2 %collective-permute-start.3 = (bf16[256,512]{1,0:T(8,128)(2,1)}, bf16[256,512]{1,0:T(8,128)(2,1)}, u32[]{:S(2)}, u32[]{:S(2)}) collective-permute-start(bf16[256,512]{1,0:T(8,128)(2,1)} %get-tuple-element.12), channel_id=1, source_target_pairs={{0,2},{2,0},{1,3},{3,1},{4,6},{6,4},{5,7},{7,5},{8,10},{10,8},{9,1... | collective-permute-start | bytes 786440 | tf_op jit(solution)/shard_map/ppermute | solution.py:307
  43.1 15.7 %copy-start.1 = (bf16[1,1024,1024]{2,1,0:T(8,128)(2,1)S(1)}, bf16[1,1024,1024]{2,1,0:T(8,128)(2,1)}, u32[]{:S(2)}) copy-start(bf16[1,1024,1024]{2,1,0:T(8,128)(2,1)} %param.10) | copy-start | bytes 6291460
  43.2 31.3 %all-to-all-start.1 = ((bf16[128,16,128]{2,1,0:T(8,128)(2,1)}), bf16[128,16,128]{2,1,0:T(8,128)(2,1)S(1)}, u32[]{:S(2)}, u32[]{:S(2)}) async-start(bf16[128,16,128]{2,1,0:T(8,128)(2,1)} %bitcast.14), calls=%async_computation.1 | async-start | bytes 1048576 | tf_op jit(solution)/shard_map/all_to_all | solution.py:281
  56.4 1.6 %collective-permute-start.4 = (bf16[2,256,256]{2,1,0:T(8,128)(2,1)S(1)}, bf16[2,256,256]{2,1,0:T(8,128)(2,1)S(1)}, u32[]{:S(2)}, u32[]{:S(2)}) collective-permute-start(bf16[2,256,256]{2,1,0:T(8,128)(2,1)S(1)} %get-tuple-element.10.r_near), channel_id=1, source_target_pairs={{0,1},{1,0},{2,3},{3,2},{4,5},{5,4},{6,7},{7,6},{8,9},{9,8},{10,11... | collective-permute-start | bytes 786440 | tf_op jit(solution)/shard_map/ppermute | solution.py:311
  56.5 0.7 copy-start.7
  58.1 0.7 copy-start.5
  59.7 14.9 %collective-permute-start.5 = (bf16[1024,128]{1,0:T(8,128)(2,1)S(1)}, bf16[1024,128]{1,0:T(8,128)(2,1)S(1)}, u32[]{:S(2)}, u32[]{:S(2)}) collective-permute-start(bf16[1024,128]{1,0:T(8,128)(2,1)S(1)} %fusion.1.own), channel_id=1, source_target_pairs={{0,2},{2,0},{1,3},{3,1},{4,6},{6,4},{5,7},{7,5},{8,10},{10,8},{9,1... | collective-permute-start | bytes 786440 | tf_op jit(solution)/shard_map/ppermute | solution.py:314
  74.6 3.8 %copy-start.2 = (f32[1,1024,256]{2,1,0:T(8,128)S(1)}, f32[1,1024,256]{2,1,0:T(8,128)}, u32[]{:S(2)}) copy-start(f32[1,1024,256]{2,1,0:T(8,128)} %m1.1) | copy-start | bytes 3145732
  74.6 3.8 %copy-start.3 = (f32[1,1024,256]{2,1,0:T(8,128)S(1)}, f32[1,1024,256]{2,1,0:T(8,128)}, u32[]{:S(2)}) copy-start(f32[1,1024,256]{2,1,0:T(8,128)} %m2.1) | copy-start | bytes 3145732
  74.6 3.8 %copy-start.6 = (bf16[2,256,256]{2,1,0:T(8,128)(2,1)S(1)}, bf16[2,256,256]{2,1,0:T(8,128)(2,1)}, u32[]{:S(2)}) copy-start(bf16[2,256,256]{2,1,0:T(8,128)(2,1)} %copy-done.5) | copy-start | bytes 786436
  75.6 2.8 %collective-permute-start.8 = (bf16[1024,256]{1,0:T(8,128)(2,1)S(1)}, bf16[1024,256]{1,0:T(8,128)(2,1)S(1)}, u32[]{:S(2)}, u32[]{:S(2)}) collective-permute-start(bf16[1024,256]{1,0:T(8,128)(2,1)S(1)} %fusion.mine), channel_id=1, source_target_pairs={{0,1},{1,0},{2,3},{3,2},{4,5},{5,4},{6,7},{7,6},{8,9},{9,8},{10,11... | collective-permute-start | bytes 1572872 | tf_op jit(solution)/shard_map/ppermute | solution.py:322
  75.7 2.3 %collective-permute-start.6 = (bf16[1024,128]{1,0:T(8,128)(2,1)S(1)}, bf16[1024,128]{1,0:T(8,128)(2,1)S(1)}, u32[]{:S(2)}, u32[]{:S(2)}) collective-permute-start(bf16[1024,128]{1,0:T(8,128)(2,1)S(1)} %fusion.1.own), channel_id=1, source_target_pairs={{0,1},{1,0},{2,3},{3,2},{4,5},{5,4},{6,7},{7,6},{8,9},{9,8},{10,11... | collective-permute-start | bytes 786440 | tf_op jit(solution)/shard_map/ppermute | solution.py:315
  76.2 2.1 %collective-permute-start.7 = (bf16[1024,128]{1,0:T(8,128)(2,1)S(1)}, bf16[1024,128]{1,0:T(8,128)(2,1)S(1)}, u32[]{:S(2)}, u32[]{:S(2)}) collective-permute-start(bf16[1024,128]{1,0:T(8,128)(2,1)S(1)} %collective-permute-done.5.after.far), channel_id=1, source_target_pairs={{0,1},{1,0},{2,3},{3,2},{4,5},{5,4},{6,7},{7,6},{8,9},{9,8},{10,11... | collective-permute-start | bytes 786440 | tf_op jit(solution)/shard_map/ppermute | solution.py:316
  78.4 4.9 %copy-start.8 = (bf16[2,256,256]{2,1,0:T(8,128)(2,1)S(1)}, bf16[2,256,256]{2,1,0:T(8,128)(2,1)}, u32[]{:S(2)}) copy-start(bf16[2,256,256]{2,1,0:T(8,128)(2,1)} %copy-done.7) | copy-start | bytes 786436
  81.4 1.9 %collective-permute-start.9 = (bf16[1024,256]{1,0:T(8,128)(2,1)S(1)}, bf16[1024,256]{1,0:T(8,128)(2,1)S(1)}, u32[]{:S(2)}, u32[]{:S(2)}) collective-permute-start(bf16[1024,256]{1,0:T(8,128)(2,1)S(1)} %get-tuple-element.6.own), channel_id=1, source_target_pairs={{0,1},{1,0},{2,3},{3,2},{4,5},{5,4},{6,7},{7,6},{8,9},{9,8},{10,11... | collective-permute-start | bytes 1572872 | tf_op jit(solution)/shard_map/ppermute | solution.py:327
  85.8 40.5 %copy-start.4 = (f32[16,64,256]{2,1,0:T(8,128)S(1)}, f32[16,64,256]{2,1,0:T(8,128)}, u32[]{:S(2)}) copy-start(f32[16,64,256]{2,1,0:T(8,128)} %weights.1) | copy-start | bytes 3145732

commit v4 on v2

v4 whole, which is shorter than its diff:
```python
import jax
import jax.numpy as jnp
from jax import lax
from jax.experimental import pallas as pl
from jax.experimental.pallas import tpu as pltpu
from jax.sharding import Mesh, PartitionSpec as P

FSDP = ("z", "y", "x_lo")
DP = ("x_hi", "core")
SWAP = [(0, 1), (1, 0)]
F32 = jnp.float32
BF16 = jnp.bfloat16
BS = 1024
NB = 64
ROWS = 16
Q = 256
PARTS = 2
PLAIN = ((1,), (0,))
PARAMS = pltpu.CompilerParams(vmem_limit_bytes=16 << 20)


def dot_f32(a, b, dims=PLAIN):
    return lax.dot_general(a, b, (dims, ((), ())), preferred_element_type=F32)


def cost(flops, moved):
    return pl.CostEstimate(flops=flops, bytes_accessed=moved, transcendentals=0)


def swap_matrix():
    to = lax.broadcasted_iota(jnp.int32, (Q, Q), 0)
    come = lax.broadcasted_iota(jnp.int32, (Q, Q), 1)
    hit = (to // ROWS == come % ROWS) & (to % ROWS == come // ROWS)
    return jnp.where(hit, 1.0, 0.0).astype(BF16)


def pick_kernel(core_ref, grads_ref, out_ref):
    out_ref[0] = grads_ref[...]


def pick(core, grads):
    return pl.pallas_call(
        pick_kernel,
        grid_spec=pltpu.PrefetchScalarGridSpec(
            num_scalar_prefetch=1,
            grid=(2,),
            in_specs=[pl.BlockSpec((ROWS, NB, Q), lambda g, core: (0, 0, 2 * g + 1 - core[0]))],
            out_specs=pl.BlockSpec((1, ROWS, NB, Q), lambda g, core: (g, 0, 0, 0)),
        ),
        out_shape=jax.ShapeDtypeStruct((2, ROWS, NB, Q), BF16),
        compiler_params=PARAMS,
        cost_estimate=cost(0, 4 << 20),
        name="pick",
    )(core, grads)


def pack_kernel(core_ref, grads_ref, arrived_ref, out_ref):
    swap = swap_matrix()
    for part in range(NB // ROWS):
        here = pl.ds(part * ROWS, ROWS)
        total = dot_f32(swap, grads_ref[:, here, :].reshape(Q, Q))
        total += dot_f32(swap, arrived_ref[0, :, here, :].reshape(Q, Q))
        out_ref[here] = total.astype(BF16).reshape(ROWS, ROWS, Q)


def pack(core, grads, arrived):
    return pl.pallas_call(
        pack_kernel,
        grid_spec=pltpu.PrefetchScalarGridSpec(
            num_scalar_prefetch=1,
            grid=(2,),
            in_specs=[
                pl.BlockSpec((ROWS, NB, Q), lambda g, core: (0, 0, 2 * g + core[0])),
                pl.BlockSpec((1, ROWS, NB, Q), lambda g, core: (g, 0, 0, 0)),
            ],
            out_specs=pl.BlockSpec((NB, ROWS, Q), lambda g, core: (0, 0, g)),
        ),
        out_shape=jax.ShapeDtypeStruct((NB, ROWS, 2 * Q), BF16),
        compiler_params=PARAMS,
        cost_estimate=cost(4 * BS * Q * Q, 3 << 20),
        name="pack",
    )(core, grads, arrived)


def term_kernel(at, left_own, left_far, own_send, far_send, own_keep, far_keep, send, keep):
    send[0] = (dot_f32(left_own[...], own_send[...]) + dot_f32(left_far[...], far_send[...])).astype(BF16)
    keep[0] = dot_f32(left_own[...], own_keep[...]) + dot_f32(left_far[...], far_keep[...])


def term(at, left, right_own, right_far):
    size = BS // PARTS

    def right(other):
        return pl.BlockSpec((Q, Q), lambda g, at: (0, 2 * g + (1 - at[1] if other else at[1])))

    held = pl.BlockSpec((1, size, Q), lambda g, at: (g, 0, 0))
    return pl.pallas_call(
        term_kernel,
        grid_spec=pltpu.PrefetchScalarGridSpec(
            num_scalar_prefetch=1,
            grid=(2,),
            in_specs=[
                pl.BlockSpec((size, Q), lambda g, at: (0, at[0])),
                pl.BlockSpec((size, Q), lambda g, at: (0, 1 - at[0])),
                right(True),
                right(True),
                right(False),
                right(False),
            ],
            out_specs=[held, held],
        ),
        out_shape=[jax.ShapeDtypeStruct((2, size, Q), BF16), jax.ShapeDtypeStruct((2, size, Q), F32)],
        compiler_params=PARAMS,
        cost_estimate=cost(16 * size * Q * Q, 4 << 20),
        name="term",
    )(at, left, left, right_own, right_far, right_own, right_far)


def chip_kernel(at, far_keep, far_arrived, own_keep, own_arrived, send, keep):
    send[...] = (far_keep[0] + far_arrived[0].astype(F32)).astype(BF16)
    keep[...] = own_keep[0] + own_arrived[0].astype(F32)


def chip_sum(at, keep, arrived):
    size = BS // PARTS
    far = pl.BlockSpec((1, size, Q), lambda i, at: (1 - at[0], 0, 0))
    own = pl.BlockSpec((1, size, Q), lambda i, at: (at[0], 0, 0))
    held = pl.BlockSpec((size, Q), lambda i, at: (0, 0))
    return pl.pallas_call(
        chip_kernel,
        grid_spec=pltpu.PrefetchScalarGridSpec(
            num_scalar_prefetch=1, grid=(1,), in_specs=[far, far, own, own], out_specs=[held, held]
        ),
        out_shape=[jax.ShapeDtypeStruct((size, Q), BF16), jax.ShapeDtypeStruct((size, Q), F32)],
        compiler_params=PARAMS,
        cost_estimate=cost(4 * size * Q, 1 << 20),
        name="chip_sum",
    )(at, keep, arrived, keep, arrived)


def adam_kernel(own, far, m1, m2, *rest):
    first, second, direction = rest[-3:]
    rotated = own[...] + far[...].astype(F32)
    new1 = 0.9 * m1[0] + 0.1 * rotated
    new2 = 0.95 * m2[0] + 0.05 * rotated * rotated
    first[0] = new1
    second[0] = new2
    bias_first = 1.0 - 0.9**10
    bias_second = 1.0 - 0.95**10
    direction[...] = (new1 / bias_first / (jnp.sqrt(new2 / bias_second) + 1e-08)).astype(BF16)


def adam(part, own, far, moments, done):
    tile = 256
    steps = BS // PARTS // tile
    rows = pl.BlockSpec((tile, Q), lambda i: (i, 0))
    moment = pl.BlockSpec((1, tile, Q), lambda i: (0, steps * part + i, 0))
    return pl.pallas_call(
        adam_kernel,
        grid=(steps,),
        in_specs=[rows] * 2 + [moment] * 2 + [pl.BlockSpec(memory_space=pl.ANY)] * len(done),
        out_specs=[moment, moment, rows],
        out_shape=[
            jax.ShapeDtypeStruct((1, BS, Q), F32),
            jax.ShapeDtypeStruct((1, BS, Q), F32),
            jax.ShapeDtypeStruct((BS // PARTS, Q), BF16),
        ],
        input_output_aliases={4 + n: n for n in range(len(done))},
        compiler_params=PARAMS,
        cost_estimate=cost(1 << 18, 1 << 18),
        name="adam",
    )(own, far, *moments, *done)


def far_kernel(at, own0, own1, near0, near1, own_own, own_near, far_own, far_near, left, out, turned, far):
    @pl.when(pl.program_id(0) == 0)
    def _():
        both = ((1,), (1,))
        for part, (own, near) in enumerate(((own0, near0), (own1, near1))):
            rows = slice(part * BS // PARTS, (part + 1) * BS // PARTS)
            for r_own, r_near, to in ((own_own, own_near, turned), (far_own, far_near, far)):
                total = dot_f32(own[...], r_own[...], both) + dot_f32(near[...], r_near[...], both)
                to[rows] = total.astype(BF16)

    out[...] = dot_f32(left[...], far[...]).astype(BF16).reshape(out.shape)


def far_share(at, own, near, right_own, right_far, left):
    tile = 256
    half = pl.BlockSpec((BS // PARTS, Q), lambda i, at: (0, 0))
    r_own = pl.BlockSpec((Q, Q), lambda i, at: (0, 2 * at[0] + at[1]))
    r_near = pl.BlockSpec((Q, Q), lambda i, at: (0, 2 * at[0] + 1 - at[1]))
    return pl.pallas_call(
        far_kernel,
        grid_spec=pltpu.PrefetchScalarGridSpec(
            num_scalar_prefetch=1,
            grid=(BS // tile,),
            in_specs=[half] * 4 + [r_own, r_near] * 2 + [pl.BlockSpec((tile, BS), lambda i, at: (i, 0))],
            out_specs=[
                pl.BlockSpec((tile // ROWS, ROWS, Q), lambda i, at: (i, 0, 0)),
                pl.BlockSpec((BS, Q), lambda i, at: (0, 0)),
            ],
            scratch_shapes=[pltpu.VMEM((BS, Q), BF16)],
        ),
        out_shape=[
            jax.ShapeDtypeStruct((NB, ROWS, Q), BF16),
            jax.ShapeDtypeStruct((BS, Q), BF16),
        ],
        compiler_params=PARAMS,
        cost_estimate=cost(2 * BS * BS * Q + 8 * BS * Q * Q, 5 << 20),
        name="far_share",
    )(at, *own, *near, right_own, right_own, right_far, right_far, left)


def own_kernel(left, turned, out):
    out[...] = dot_f32(left[...], turned[...]).reshape(out.shape)


def own_share(left, turned):
    tile = 256
    return pl.pallas_call(
        own_kernel,
        grid=(BS // tile,),
        in_specs=[pl.BlockSpec((tile, BS), lambda i: (i, 0)), pl.BlockSpec((BS, Q), lambda i: (0, 0))],
        out_specs=pl.BlockSpec((tile // ROWS, ROWS, Q), lambda i: (i, 0, 0)),
        out_shape=jax.ShapeDtypeStruct((NB, ROWS, Q), F32),
        compiler_params=PARAMS,
        cost_estimate=cost(2 * BS * BS * Q, 4 << 20),
        name="own_share",
    )(left, turned)


def add_kernel(here, there, out):
    out[...] = (here[...] + there[...].astype(F32)).astype(BF16)


def add(here, there):
    held = pl.BlockSpec((NB, ROWS, Q), lambda i: (0, 0, 0))
    return pl.pallas_call(
        add_kernel,
        grid=(1,),
        in_specs=[held, held],
        out_specs=held,
        out_shape=jax.ShapeDtypeStruct((NB, ROWS, Q), BF16),
        compiler_params=PARAMS,
        cost_estimate=cost(1 << 18, 2 << 20),
        name="add",
    )(here, there)


def apply_kernel(pieces, weights, out):
    total = dot_f32(swap_matrix(), pieces[...].reshape(Q, Q))
    out[...] = weights[...] - 0.5 * total.reshape(ROWS, ROWS, Q)


def apply(pieces, weights):
    held = pl.BlockSpec((ROWS, ROWS, Q), lambda i: (0, i, 0))
    return pl.pallas_call(
        apply_kernel,
        grid=(NB // ROWS,),
        in_specs=[pl.BlockSpec((ROWS, ROWS, Q), lambda i: (i, 0, 0)), held],
        out_specs=held,
        out_shape=jax.ShapeDtypeStruct((ROWS, NB, Q), F32),
        compiler_params=PARAMS,
        cost_estimate=cost(2 * BS * Q * Q, 3 << 20),
        name="apply",
    )(pieces, weights)


def exchange(pieces, axes):
    return lax.all_to_all(pieces, axes, split_axis=0, concat_axis=0, tiled=True)


def local(grads, weights, moment_first, moment_second, left_basis, right_basis):
    core = lax.axis_index("core").astype(jnp.int32)
    x_hi = lax.axis_index("x_hi").astype(jnp.int32)
    core_ref = core.reshape(1)
    left = left_basis[0]

    at = jnp.stack([x_hi, core])

    arrived = lax.ppermute(pick(core_ref, grads[0]), "core", SWAP)
    pieces = exchange(pack(core_ref, grads[0], arrived), FSDP)
    right_own = right_basis[0]
    right_far = lax.ppermute(right_own, "x_hi", SWAP)
    pieces, right_far = lax.optimization_barrier((pieces, right_far))

    half = BS // PARTS
    grad_block = pieces.reshape(BS, 2 * Q)
    parts = range(PARTS)
    sent, kept = [], []
    for part in parts:
        rotated_left = dot_f32(left[:, part * half : (part + 1) * half], grad_block, ((0,), (0,))).astype(BF16)
        send, keep = term(at, rotated_left, right_own, right_far)
        sent.append(lax.ppermute(send, "core", SWAP))
        kept.append(keep)
    sums = [chip_sum(at, kept[part], sent[part]) for part in parts]
    far = [lax.ppermute(send, "x_hi", SWAP) for send, _ in sums]
    done, own, near = (), [], []
    for part in parts:
        if part:
            far[part], own[-1] = lax.optimization_barrier((far[part], own[-1]))
        *done, direction = adam(part, sums[part][1], far[part], (moment_first, moment_second), done)
        own.append(direction)
        near.append(lax.ppermute(direction, "core", SWAP))

    far, turned = far_share(at, own, near, right_own, right_far, left)
    there = lax.ppermute(far, "x_hi", SWAP)
    returned = exchange(add(own_share(left, turned), there), FSDP)
    return (apply(returned, weights), *done)


def solution(mesh):
    fine = Mesh(mesh.devices.reshape(8, 4, 2, 2, 2), FSDP + DP)
    placed = (
        P(DP, FSDP, None, None),
        P(FSDP, None, DP),
        P(FSDP, None, DP),
        P(FSDP, None, DP),
        P(FSDP, None, None),
        P(FSDP, DP, None),
    )
    return jax.shard_map(
        local,
        mesh=fine,
        in_specs=placed,
        out_specs=(P(FSDP, None, DP), P(FSDP, None, DP), P(FSDP, None, DP)),
        check_vma=False,
    )
```

time: 123 us -> 121 us (0.984)
  blocking collectives: 83.1 us -> 23.7 us
  waiting for transfers between devices: 20 us -> 51.6 us
  starting transfers between devices: 4.55 us -> 23.1 us
  Pallas kernels: 9.08 us -> 14.7 us
  other arithmetic: 3.12 us -> 0.07 us
  matrix products: 0.94 us -> 3.95 us
    all_to_all x2 -> x1, blocking collectives: 83.1 us -> 23.7 us  [exchange(): return lax.all_to_all(pieces, axes, split_axis=0, concat_axis=0, tiled=True)]
    ppermute x7 -> x8, waiting for transfers between devices: 17.4 us -> 44.2 us  [the longest x1 21.2 us: local(): right_far = lax.ppermute(right_own, 'x_hi', SWAP)]
    all_to_all x0 -> x1, starting transfers between devices: none -> 13 us  [exchange(): return lax.all_to_all(pieces, axes, split_axis=0, concat_axis=0, tiled=True)]
    pallas_call x2 -> x9, Pallas kernels: 5.46 us -> 11.2 us  [the longest x2 3.52 us: term(): pl.pallas_call(term_kernel, grid_spec=pltpu.PrefetchScalarGridSpec(num_sc...]
    ppermute x7 -> x8, starting transfers between devices: 4.46 us -> 10 us  [the longest x2 3.7 us: local(): far = [lax.ppermute(send, 'x_hi', SWAP) for send, _ in sums]]
    all_to_all x0 -> x1, waiting for transfers between devices: none -> 4.83 us  [exchange(): return lax.all_to_all(pieces, axes, split_axis=0, concat_axis=0, tiled=True)]
    dot_general x1 -> x2, matrix products: 0.94 us -> 3.95 us  [dot_f32(): return lax.dot_general(a, b, (dims, ((), ())), preferred_element_type=F32)]
    select_n x4 -> x0, other arithmetic: 2.98 us -> none  [the longest x1 1.77 us: local(): right_far = lax.ppermute(jnp.where(x_hi == 0, high, low), 'x_hi', SWAP)]
  transfers between devices with their start and end apart: 8 -> 10, of which waited for: 5 -> 7; matrix products, arithmetic and copies ran while one was open for 2% -> 0% of each run, Pallas kernels for 0% -> 5%
where the time goes in v4:
time: 121 us
  waiting for transfers between devices  51.6 us (43%)
  blocking collectives  23.7 us (20%)
  starting transfers between devices  23.1 us (19%)
  Pallas kernels  14.7 us (12%)
  matrix products  3.95 us (3%)
  local copies, waits for them, and re-layouts  2.57 us (2%)
    all_to_all x1, blocking collectives, exchange(): return lax.all_to_all(pieces, axes, split_axis=0, concat_axis=0, tiled=True)  23.7 us
    ppermute x1, waiting for transfers between devices, local(): right_far = lax.ppermute(right_own, 'x_hi', SWAP)  21.2 us
    all_to_all x1, starting transfers between devices, exchange(): return lax.all_to_all(pieces, axes, split_axis=0, concat_axis=0, tiled=True)  13 us
    ppermute x1, waiting for transfers between devices, local(): there = lax.ppermute(far, 'x_hi', SWAP)  11.5 us
    ppermute x2, waiting for transfers between devices, local(): far = [lax.ppermute(send, 'x_hi', SWAP) for send, _ in sums]  9.92 us
    all_to_all x1, waiting for transfers between devices, exchange(): return lax.all_to_all(pieces, axes, split_axis=0, concat_axis=0, tiled=True)  4.83 us
    dot_general x2, matrix products, dot_f32(): return lax.dot_general(a, b, (dims, ((), ())), preferred_element_type=F32)  3.95 us
    ppermute x2, starting transfers between devices, local(): far = [lax.ppermute(send, 'x_hi', SWAP) for send, _ in sums]  3.7 us
  transfers between devices with their start and end apart: 10, of which 7 were waited for; matrix products, arithmetic and copies ran while one was open for 0% of the time, Pallas kernels for 5%

profile of v4, /device:TPU:32, one launch (start us, length us, event | category | flops | bytes accessed | tf_op | source)
XLA Modules:
  0.0 120.5 jit_solution(18193108815018307343)
XLA Ops:
  0.6 0.0 copy-start.2
  0.6 1.6 %copy-done.2 = bf16[1,16,64,1024]{3,2,1,0:T(8,128)(2,1)S(1)} copy-done((bf16[1,16,64,1024]{3,2,1,0:T(8,128)(2,1)S(1)}, bf16[1,16,64,1024]{3,2,1,0:T(8,128)(2,1)}, u32[]{:S(2)}) %copy-start.2) | copy-done | bytes 2097176
  2.2 0.3 pick.1
  2.5 0.1 collective-permute-start
  2.6 2.6 %collective-permute-done.arrived_ref = bf16[2,16,64,256]{3,2,1,0:T(8,128)(2,1)S(1)} collective-permute-done((bf16[2,16,64,256]{3,2,1,0:T(8,128)(2,1)S(1)}, bf16[2,16,64,256]{3,2,1,0:T(8,128)(2,1)S(1)}, u32[]{:S(2)}, u32[]{:S(2)}) %collective-permute-start) | collective-permute-done | bytes 1048608 | tf_op jit(solution)/shard_map/ppermute | solution.py:282
  5.3 1.1 pack.1
  6.4 0.0 copy-start.3
  6.4 1.0 copy-done.3
  7.4 13.0 %all-to-all-start = ((bf16[64,16,512]{2,1,0:T(8,128)(2,1)}), bf16[64,16,512]{2,1,0:T(8,128)(2,1)}, u32[]{:S(2)}, u32[]{:S(2)}) async-start(bf16[64,16,512]{2,1,0:T(8,128)(2,1)} %copy-done.3), calls=%async_computation | async-start | bytes 2097152 | tf_op jit(solution)/shard_map/all_to_all | solution.py:271
  20.4 0.0 copy-done
  20.4 2.8 %collective-permute-start.1 = (bf16[256,1024]{1,0:T(8,128)(2,1)S(1)}, bf16[256,1024]{1,0:T(8,128)(2,1)S(1)}, u32[]{:S(2)}, u32[]{:S(2)}) collective-permute-start(bf16[256,1024]{1,0:T(8,128)(2,1)S(1)} %bitcast.12), channel_id=1, source_target_pairs={{0,2},{2,0},{1,3},{3,1},{4,6},{6,4},{5,7},{7,5},{8,10},{10,8},{9,1... | collective-permute-start | bytes 1572872 | tf_op jit(solution)/shard_map/ppermute | solution.py:285
  23.2 0.1 pad_add_fusion.at
  23.3 21.2 %collective-permute-done.1.far_send.far_keep.far_own.far_near = bf16[256,1024]{1,0:T(8,128)(2,1)S(1)} collective-permute-done((bf16[256,1024]{1,0:T(8,128)(2,1)S(1)}, bf16[256,1024]{1,0:T(8,128)(2,1)S(1)}, u32[]{:S(2)}, u32[]{:S(2)}) %collective-permute-start.1) | collective-permute-done | bytes 524320 | tf_op jit(solution)/shard_map/ppermute | solution.py:285
  44.5 4.8 %all-to-all-done = bf16[64,16,512]{2,1,0:T(8,128)(2,1)} async-done(((bf16[64,16,512]{2,1,0:T(8,128)(2,1)}), bf16[64,16,512]{2,1,0:T(8,128)(2,1)}, u32[]{:S(2)}, u32[]{:S(2)}) %all-to-all-start) | async-done | bytes 1048608 | tf_op jit(solution)/shard_map/all_to_all | solution.py:271
  49.4 0.0 copy-done.1
  49.4 2.0 %fusion.left_own.left_far = bf16[512,512]{1,0:T(8,128)(2,1)S(1)} fusion(bf16[1024,512]{1,0:T(8,128)(2,1)} %bitcast.5, bf16[1024,1024]{1,0:T(8,128)(2,1)S(1)} %bitcast.19), kind=kOutput, calls=%fused_computation.2 | convolution fusion | flops 537133056 | bytes 2621440 | tf_op jit(solution)/shard_map/dot_general | solution.py:23
  51.3 2.0 %fusion.1.left_own.left_far = bf16[512,512]{1,0:T(8,128)(2,1)S(1)} fusion(bf16[1024,512]{1,0:T(8,128)(2,1)} %bitcast.5, bf16[1024,1024]{1,0:T(8,128)(2,1)S(1)} %bitcast.20), kind=kOutput, calls=%fused_computation.3 | convolution fusion | flops 537133056 | bytes 2621440 | tf_op jit(solution)/shard_map/dot_general | solution.py:23
  53.3 1.8 %term.3 = (bf16[2,512,256]{2,1,0:T(8,128)(2,1)S(1)}, f32[2,512,256]{2,1,0:T(8,128)S(1)}) custom-call(s32[2]{0:T(128)S(1)} %pad_add_fusion.at, bf16[512,512]{1,0:T(8,128)(2,1)S(1)} %fusion.1.left_own.left_far, bf16[512,512]{1,0:T(8,128)(2,1)S(1)} %fusion.1.left_own.left_far, bf16[256,1024]{1,0:T(8,128)(2,1)S(1)} %bitcast.13, ...), custom_call_target="tpu_custom_call" | custom-call | flops 536870912 | bytes 4194304 | tf_op jit(solution)/shard_map/term/pallas_call | solution.py:97
  55.1 0.1 collective-permute-start.4
  55.2 1.8 %term.2 = (bf16[2,512,256]{2,1,0:T(8,128)(2,1)S(1)}, f32[2,512,256]{2,1,0:T(8,128)S(1)}) custom-call(s32[2]{0:T(128)S(1)} %pad_add_fusion.at, bf16[512,512]{1,0:T(8,128)(2,1)S(1)} %fusion.left_own.left_far, bf16[512,512]{1,0:T(8,128)(2,1)S(1)} %fusion.left_own.left_far, bf16[256,1024]{1,0:T(8,128)(2,1)S(1)} %bitcast.15, ...), custom_call_target="tpu_custom_call" | custom-call | flops 536870912 | bytes 4194304 | tf_op jit(solution)/shard_map/term/pallas_call | solution.py:97
  57.0 0.6 collective-permute-start.2
  57.5 0.0 collective-permute-done.4.far_arrived.own_arrived
  57.5 0.7 chip_sum.3
  58.2 0.0 copy-start.4
  58.2 0.0 copy-start.5
  58.2 2.8 %collective-permute-start.5 = (bf16[512,256]{1,0:T(8,128)(2,1)S(1)}, bf16[512,256]{1,0:T(8,128)(2,1)S(1)}, u32[]{:S(2)}, u32[]{:S(2)}) collective-permute-start(bf16[512,256]{1,0:T(8,128)(2,1)S(1)} %get-tuple-element.31), channel_id=1, source_target_pairs={{0,2},{2,0},{1,3},{3,1},{4,6},{6,4},{5,7},{7,5},{8,10},{10,8},{9,1... | collective-permute-start | bytes 786440 | tf_op jit(solution)/shard_map/ppermute | solution.py:298
  61.1 0.0 collective-permute-done.2.far_arrived.own_arrived
  61.1 0.7 chip_sum.2
  61.7 0.9 collective-permute-start.3
  62.6 6.4 %collective-permute-done.5.far = bf16[512,256]{1,0:T(8,128)(2,1)S(1)} collective-permute-done((bf16[512,256]{1,0:T(8,128)(2,1)S(1)}, bf16[512,256]{1,0:T(8,128)(2,1)S(1)}, u32[]{:S(2)}, u32[]{:S(2)}) %collective-permute-start.5) | collective-permute-done | bytes 262176 | tf_op jit(solution)/shard_map/ppermute | solution.py:298
  69.0 0.0 copy-done.4
  69.0 0.0 copy-done.5
  69.0 1.1 adam.2
  70.1 0.0 collective-permute-start.6
  70.1 3.5 %collective-permute-done.3.far = bf16[512,256]{1,0:T(8,128)(2,1)S(1)} collective-permute-done((bf16[512,256]{1,0:T(8,128)(2,1)S(1)}, bf16[512,256]{1,0:T(8,128)(2,1)S(1)}, u32[]{:S(2)}, u32[]{:S(2)}) %collective-permute-start.3) | collective-permute-done | bytes 262176 | tf_op jit(solution)/shard_map/ppermute | solution.py:298
  73.7 1.1 adam.3
  74.8 0.0 collective-permute-start.7
  74.8 0.0 collective-permute-done.6.near0
  74.8 1.5 %collective-permute-done.7.near1 = bf16[512,256]{1,0:T(8,128)(2,1)S(1)} collective-permute-done((bf16[512,256]{1,0:T(8,128)(2,1)S(1)}, bf16[512,256]{1,0:T(8,128)(2,1)S(1)}, u32[]{:S(2)}, u32[]{:S(2)}) %collective-permute-start.7) | collective-permute-done | bytes 262176 | tf_op jit(solution)/shard_map/ppermute | solution.py:305
  76.3 2.8 %far_share.1 = (bf16[64,16,256]{2,1,0:T(8,128)(2,1)S(1)}, bf16[1024,256]{1,0:T(8,128)(2,1)S(1)}) custom-call(s32[2]{0:T(128)S(1)} %pad_add_fusion.at, bf16[512,256]{1,0:T(8,128)(2,1)S(1)} %get-tuple-element.33.own0, bf16[512,256]{1,0:T(8,128)(2,1)S(1)} %get-tuple-element.38.own1, bf16[512,256]{1,0:T(8,128)(2,1)S(1)} %collective-permute-done.6.near0, ...), custom_call_target="tpu_custom_call" | custom-call | flops 1073741824 | bytes 5242880 | tf_op jit(solution)/shard_map/far_share/pallas_call | solution.py:193
  79.1 2.8 %collective-permute-start.8 = (bf16[64,16,256]{2,1,0:T(8,128)(2,1)S(1)}, bf16[64,16,256]{2,1,0:T(8,128)(2,1)S(1)}, u32[]{:S(2)}, u32[]{:S(2)}) collective-permute-start(bf16[64,16,256]{2,1,0:T(8,128)(2,1)S(1)} %get-tuple-element.40), channel_id=1, source_target_pairs={{0,2},{2,0},{1,3},{3,1},{4,6},{6,4},{5,7},{7,5},{8,10},{10,8},{9,1... | collective-permute-start | bytes 1572872 | tf_op jit(solution)/shard_map/ppermute | solution.py:308
  81.9 1.2 %own_share.1.here = f32[64,16,256]{2,1,0:T(8,128)S(1)} custom-call(bf16[1024,1024]{1,0:T(8,128)(2,1)S(1)} %bitcast.22, bf16[1024,256]{1,0:T(8,128)(2,1)S(1)} %get-tuple-element.39.turned), custom_call_target="tpu_custom_call" | custom-call | flops 536870912 | bytes 4194304 | tf_op jit(solution)/shard_map/own_share/pallas_call | solution.py:221
  83.2 0.0 copy-start.6
  83.2 11.5 %collective-permute-done.8.there = bf16[64,16,256]{2,1,0:T(8,128)(2,1)S(1)} collective-permute-done((bf16[64,16,256]{2,1,0:T(8,128)(2,1)S(1)}, bf16[64,16,256]{2,1,0:T(8,128)(2,1)S(1)}, u32[]{:S(2)}, u32[]{:S(2)}) %collective-permute-start.8) | collective-permute-done | bytes 524320 | tf_op jit(solution)/shard_map/ppermute | solution.py:308
  94.7 0.1 add.3
  94.7 23.7 %all_to_all.10.pieces = bf16[64,16,256]{2,1,0:T(8,128)(2,1)S(1)} all-to-all(bf16[64,16,256]{2,1,0:T(8,128)(2,1)S(1)} %add.3), channel_id=1, replica_groups=mesh['z'=8,'y'=4,'x_lo'=2,'x_hi'=2,'core'=2] {'z','y','x_lo'}, dimensions={0} | all-to-all | bytes 1048576 | tf_op jit(solution)/shard_map/all_to_all | solution.py:271
  118.4 0.0 copy-done.6
  118.4 2.1 %apply.1 = f32[16,64,256]{2,1,0:T(8,128)} custom-call(bf16[64,16,256]{2,1,0:T(8,128)(2,1)S(1)} %all_to_all.10.pieces, f32[16,64,256]{2,1,0:T(8,128)S(1)} %copy-done.6), custom_call_target="tpu_custom_call" | custom-call | flops 134217728 | bytes 3145728 | tf_op jit(solution)/shard_map/apply/pallas_call | solution.py:258
  (2 shorter events, 0.0 us)
Async XLA Ops:
  0.6 1.6 %copy-start.2 = (bf16[1,16,64,1024]{3,2,1,0:T(8,128)(2,1)S(1)}, bf16[1,16,64,1024]{3,2,1,0:T(8,128)(2,1)}, u32[]{:S(2)}) copy-start(bf16[1,16,64,1024]{3,2,1,0:T(8,128)(2,1)} %param.6) | copy-start | bytes 6291460
  2.5 2.7 %collective-permute-start = (bf16[2,16,64,256]{3,2,1,0:T(8,128)(2,1)S(1)}, bf16[2,16,64,256]{3,2,1,0:T(8,128)(2,1)S(1)}, u32[]{:S(2)}, u32[]{:S(2)}) collective-permute-start(bf16[2,16,64,256]{3,2,1,0:T(8,128)(2,1)S(1)} %pick.1), channel_id=1, source_target_pairs={{0,1},{1,0},{2,3},{3,2},{4,5},{5,4},{6,7},{7,6},{8,9},{9,8},{10,11... | collective-permute-start | bytes 3145736 | tf_op jit(solution)/shard_map/ppermute | solution.py:282
  5.3 44.1 %copy-start.1 = (bf16[1,1024,1024]{2,1,0:T(8,128)(2,1)S(1)}, bf16[1,1024,1024]{2,1,0:T(8,128)(2,1)}, u32[]{:S(2)}) copy-start(bf16[1,1024,1024]{2,1,0:T(8,128)(2,1)} %param.10) | copy-start | bytes 6291460
  6.4 1.0 copy-start.3
  7.4 13.0 %copy-start = (bf16[1,256,1024]{2,1,0:T(8,128)(2,1)S(1)}, bf16[1,256,1024]{2,1,0:T(8,128)(2,1)}, u32[]{:S(2)}) copy-start(bf16[1,256,1024]{2,1,0:T(8,128)(2,1)} %param.11) | copy-start | bytes 1572868
  7.4 42.0 %all-to-all-start = ((bf16[64,16,512]{2,1,0:T(8,128)(2,1)}), bf16[64,16,512]{2,1,0:T(8,128)(2,1)}, u32[]{:S(2)}, u32[]{:S(2)}) async-start(bf16[64,16,512]{2,1,0:T(8,128)(2,1)} %copy-done.3), calls=%async_computation | async-start | bytes 2097152 | tf_op jit(solution)/shard_map/all_to_all | solution.py:271
  20.4 24.1 %collective-permute-start.1 = (bf16[256,1024]{1,0:T(8,128)(2,1)S(1)}, bf16[256,1024]{1,0:T(8,128)(2,1)S(1)}, u32[]{:S(2)}, u32[]{:S(2)}) collective-permute-start(bf16[256,1024]{1,0:T(8,128)(2,1)S(1)} %bitcast.12), channel_id=1, source_target_pairs={{0,2},{2,0},{1,3},{3,1},{4,6},{6,4},{5,7},{7,5},{8,10},{10,8},{9,1... | collective-permute-start | bytes 1572872 | tf_op jit(solution)/shard_map/ppermute | solution.py:285
  55.1 2.4 %collective-permute-start.4 = (bf16[2,512,256]{2,1,0:T(8,128)(2,1)S(1)}, bf16[2,512,256]{2,1,0:T(8,128)(2,1)S(1)}, u32[]{:S(2)}, u32[]{:S(2)}) collective-permute-start(bf16[2,512,256]{2,1,0:T(8,128)(2,1)S(1)} %get-tuple-element.29), channel_id=1, source_target_pairs={{0,1},{1,0},{2,3},{3,2},{4,5},{5,4},{6,7},{7,6},{8,9},{9,8},{10,11... | collective-permute-start | bytes 1572872 | tf_op jit(solution)/shard_map/ppermute | solution.py:295
  57.0 4.1 %collective-permute-start.2 = (bf16[2,512,256]{2,1,0:T(8,128)(2,1)S(1)}, bf16[2,512,256]{2,1,0:T(8,128)(2,1)S(1)}, u32[]{:S(2)}, u32[]{:S(2)}) collective-permute-start(bf16[2,512,256]{2,1,0:T(8,128)(2,1)S(1)} %get-tuple-element.26), channel_id=1, source_target_pairs={{0,1},{1,0},{2,3},{3,2},{4,5},{5,4},{6,7},{7,6},{8,9},{9,8},{10,11... | collective-permute-start | bytes 1572872 | tf_op jit(solution)/shard_map/ppermute | solution.py:295
  58.2 10.8 %copy-start.4 = (f32[1,1024,256]{2,1,0:T(8,128)S(1)}, f32[1,1024,256]{2,1,0:T(8,128)}, u32[]{:S(2)}) copy-start(f32[1,1024,256]{2,1,0:T(8,128)} %m1.3) | copy-start | bytes 3145732
  58.2 10.8 %copy-start.5 = (f32[1,1024,256]{2,1,0:T(8,128)S(1)}, f32[1,1024,256]{2,1,0:T(8,128)}, u32[]{:S(2)}) copy-start(f32[1,1024,256]{2,1,0:T(8,128)} %m2.3) | copy-start | bytes 3145732
  58.2 10.8 %collective-permute-start.5 = (bf16[512,256]{1,0:T(8,128)(2,1)S(1)}, bf16[512,256]{1,0:T(8,128)(2,1)S(1)}, u32[]{:S(2)}, u32[]{:S(2)}) collective-permute-start(bf16[512,256]{1,0:T(8,128)(2,1)S(1)} %get-tuple-element.31), channel_id=1, source_target_pairs={{0,2},{2,0},{1,3},{3,1},{4,6},{6,4},{5,7},{7,5},{8,10},{10,8},{9,1... | collective-permute-start | bytes 786440 | tf_op jit(solution)/shard_map/ppermute | solution.py:298
  61.7 12.0 %collective-permute-start.3 = (bf16[512,256]{1,0:T(8,128)(2,1)S(1)}, bf16[512,256]{1,0:T(8,128)(2,1)S(1)}, u32[]{:S(2)}, u32[]{:S(2)}) collective-permute-start(bf16[512,256]{1,0:T(8,128)(2,1)S(1)} %get-tuple-element.27), channel_id=1, source_target_pairs={{0,2},{2,0},{1,3},{3,1},{4,6},{6,4},{5,7},{7,5},{8,10},{10,8},{9,1... | collective-permute-start | bytes 786440 | tf_op jit(solution)/shard_map/ppermute | solution.py:298
  70.1 4.7 %collective-permute-start.6 = (bf16[512,256]{1,0:T(8,128)(2,1)S(1)}, bf16[512,256]{1,0:T(8,128)(2,1)S(1)}, u32[]{:S(2)}, u32[]{:S(2)}) collective-permute-start(bf16[512,256]{1,0:T(8,128)(2,1)S(1)} %get-tuple-element.33.own0), channel_id=1, source_target_pairs={{0,1},{1,0},{2,3},{3,2},{4,5},{5,4},{6,7},{7,6},{8,9},{9,8},{10,11... | collective-permute-start | bytes 786440 | tf_op jit(solution)/shard_map/ppermute | solution.py:305
  74.8 1.5 %collective-permute-start.7 = (bf16[512,256]{1,0:T(8,128)(2,1)S(1)}, bf16[512,256]{1,0:T(8,128)(2,1)S(1)}, u32[]{:S(2)}, u32[]{:S(2)}) collective-permute-start(bf16[512,256]{1,0:T(8,128)(2,1)S(1)} %get-tuple-element.38.own1), channel_id=1, source_target_pairs={{0,1},{1,0},{2,3},{3,2},{4,5},{5,4},{6,7},{7,6},{8,9},{9,8},{10,11... | collective-permute-start | bytes 786440 | tf_op jit(solution)/shard_map/ppermute | solution.py:305
  79.1 15.6 %collective-permute-start.8 = (bf16[64,16,256]{2,1,0:T(8,128)(2,1)S(1)}, bf16[64,16,256]{2,1,0:T(8,128)(2,1)S(1)}, u32[]{:S(2)}, u32[]{:S(2)}) collective-permute-start(bf16[64,16,256]{2,1,0:T(8,128)(2,1)S(1)} %get-tuple-element.40), channel_id=1, source_target_pairs={{0,2},{2,0},{1,3},{3,1},{4,6},{6,4},{5,7},{7,5},{8,10},{10,8},{9,1... | collective-permute-start | bytes 1572872 | tf_op jit(solution)/shard_map/ppermute | solution.py:308
  83.2 35.3 %copy-start.6 = (f32[16,64,256]{2,1,0:T(8,128)S(1)}, f32[16,64,256]{2,1,0:T(8,128)}, u32[]{:S(2)}) copy-start(f32[16,64,256]{2,1,0:T(8,128)} %weights.1) | copy-start | bytes 3145732

commit v5 on v0

v5 whole, which is shorter than its diff:
```python
import functools

import jax
import jax.numpy as jnp
import numpy as np
from jax import lax
from jax.experimental import pallas as pl
from jax.experimental.pallas import tpu as pltpu
from jax.sharding import Mesh, PartitionSpec as P

FSDP = ("z", "y", "x_lo")
DP = ("x_hi", "core")
SWAP = [(0, 1), (1, 0)]
F32 = jnp.float32
BF16 = jnp.bfloat16
BS = 1024
NB = 64
ROWS = 16
Q = 256
PARTS = 2
PLAIN = ((1,), (0,))
PARAMS = pltpu.CompilerParams(vmem_limit_bytes=16 << 20)


def dot_f32(a, b, dims=PLAIN):
    return lax.dot_general(a, b, (dims, ((), ())), preferred_element_type=F32)


def cost(flops, moved):
    return pl.CostEstimate(flops=flops, bytes_accessed=moved, transcendentals=0)


SWAP_ROWS = np.eye(Q, dtype=np.float32).reshape(ROWS, ROWS, Q).transpose(1, 0, 2).reshape(Q, Q)


def group_at(n, at):
    chip = at[0] if n < 2 else 1 - at[0]
    return 2 * chip + (at[1] if n % 2 == 0 else 1 - at[1])


def group_specs(shape, lead):
    return [
        pl.BlockSpec(shape, lambda i, at, n=n: (0,) * lead + (group_at(n, at),)) for n in range(4)
    ]


def split_kernel(at, *refs):
    for n in range(4):
        refs[4 + n][...] = refs[n][...]


def split(at, grads):
    held = pl.BlockSpec((ROWS, NB, Q), lambda i, at: (0, 0, 0))
    return pl.pallas_call(
        split_kernel,
        grid_spec=pltpu.PrefetchScalarGridSpec(
            num_scalar_prefetch=1,
            grid=(1,),
            in_specs=group_specs((ROWS, NB, Q), 2),
            out_specs=[held] * 4,
        ),
        out_shape=[jax.ShapeDtypeStruct((ROWS, NB, Q), BF16)] * 4,
        compiler_params=PARAMS,
        cost_estimate=cost(0, 4 << 20),
        name="split",
    )(at, grads, grads, grads, grads)


def arrange_kernel(at, *refs):
    for n in range(4):
        refs[4][n] = refs[n][...]


def arrange(at, right):
    return pl.pallas_call(
        arrange_kernel,
        grid_spec=pltpu.PrefetchScalarGridSpec(
            num_scalar_prefetch=1,
            grid=(1,),
            in_specs=group_specs((Q, Q), 1),
            out_specs=pl.BlockSpec((4, Q, Q), lambda i, at: (0, 0, 0)),
        ),
        out_shape=jax.ShapeDtypeStruct((4, Q, Q), BF16),
        compiler_params=PARAMS,
        cost_estimate=cost(0, 1 << 20),
        name="arrange",
    )(at, right, right, right, right)


def whole(kernel, outs, *args, flops=0, name):
    def spec(value):
        return pl.BlockSpec(value.shape, lambda i, rank=len(value.shape): (0,) * rank)

    return pl.pallas_call(
        kernel,
        grid=(1,),
        in_specs=[spec(value) for value in args],
        out_specs=[spec(value) for value in outs],
        out_shape=outs,
        compiler_params=PARAMS,
        cost_estimate=cost(flops, 1 << 10),
        name=name,
    )(*args)


def shape(*dims, kind=BF16):
    return jax.ShapeDtypeStruct(dims, kind)


def pack_kernel(swap_ref, kept, arrived, out):
    swap = swap_ref[...]
    for part in range(NB // ROWS):
        here = pl.ds(part * ROWS, ROWS)
        total = dot_f32(swap, kept[:, here, :].reshape(Q, Q)) + dot_f32(swap, arrived[:, here, :].reshape(Q, Q))
        out[here] = total.astype(out.dtype).reshape(ROWS, ROWS, Q)


def pack(kept, arrived, kind):
    swap = jnp.asarray(SWAP_ROWS, BF16)
    return whole(pack_kernel, [shape(NB, ROWS, Q, kind=kind)], swap, kept, arrived, name="pack")[0]


def add_kernel(here, there, out):
    out[...] = (here[...] + there[...].astype(F32)).astype(BF16)


def add(here, there):
    return whole(add_kernel, [shape(NB, ROWS, Q)], here, there, name="add")[0]


def flip_kernel(values, out):
    out[...] = values[...].T


def flip(values):
    tile = 512
    return pl.pallas_call(
        flip_kernel,
        grid=(BS // tile, BS // tile),
        in_specs=[pl.BlockSpec((tile, tile), lambda i, j: (i, j))],
        out_specs=pl.BlockSpec((tile, tile), lambda i, j: (j, i)),
        out_shape=jax.ShapeDtypeStruct((BS, BS), BF16),
        compiler_params=PARAMS,
        cost_estimate=cost(0, 8 << 20),
        name="flip",
    )(values)


def term_kernel(part, left, grad, right, send, keep):
    size = send.shape[1]
    rotated_left = dot_f32(left[part * size : (part + 1) * size], grad[...]).astype(BF16)
    for chip in range(2):
        send[chip] = dot_f32(rotated_left, right[2 * chip + 1]).astype(BF16)
        keep[chip] = dot_f32(rotated_left, right[2 * chip])


def term(part, left_turned, grad, right):
    size = BS // PARTS
    outs = [shape(2, size, Q), shape(2, size, Q, kind=F32)]
    flops = 16 * size * Q * Q
    kernel = functools.partial(term_kernel, part)
    return whole(kernel, outs, left_turned, grad, right, flops=flops, name="term")


def chip_kernel(kept, arrived, send, keep):
    send[...] = (kept[1] + arrived[1].astype(F32)).astype(BF16)
    keep[...] = kept[0] + arrived[0].astype(F32)


def chip_sum(kept, arrived):
    size = BS // PARTS
    return whole(chip_kernel, [shape(size, Q), shape(size, Q, kind=F32)], kept, arrived, name="chip_sum")


def adam_kernel(part, own, far, m1, m2, *rest):
    first, second, direction = rest[-3:]
    size = own.shape[0]
    rows = slice(part * size, (part + 1) * size)
    rotated = own[...] + far[...].astype(F32)
    new1 = 0.9 * m1[0, rows] + 0.1 * rotated
    new2 = 0.95 * m2[0, rows] + 0.05 * rotated * rotated
    first[0] = new1
    second[0] = new2
    bias_first = 1.0 - 0.9**10
    bias_second = 1.0 - 0.95**10
    direction[...] = (new1 / bias_first / (jnp.sqrt(new2 / bias_second) + 1e-08)).astype(BF16)


def adam(part, own, far, moments, done):
    size = BS // PARTS
    rows = pl.BlockSpec((size, Q), lambda i: (0, 0))
    old = pl.BlockSpec((1, BS, Q), lambda i: (0, 0, 0))
    new = pl.BlockSpec((1, size, Q), lambda i: (0, part, 0))
    return pl.pallas_call(
        functools.partial(adam_kernel, part),
        grid=(1,),
        in_specs=[rows] * 2 + [old] * 2 + [pl.BlockSpec(memory_space=pl.ANY)] * len(done),
        out_specs=[new, new, rows],
        out_shape=[shape(1, BS, Q, kind=F32), shape(1, BS, Q, kind=F32), shape(size, Q)],
        input_output_aliases={4 + n: n for n in range(len(done))},
        compiler_params=PARAMS,
        cost_estimate=cost(1 << 10, 1 << 10),
        name="adam",
    )(own, far, *moments, *done)


def turn_kernel(own, near, far, right, *rest):
    *cross, out = rest
    both = ((1,), (1,))
    size = out.shape[0] // len(cross)
    for n, piece in enumerate(cross):
        rows = slice(n * size, (n + 1) * size)
        total = dot_f32(own[rows], right[0], both) + dot_f32(near[rows], right[1], both)
        total += dot_f32(far[rows], right[2], both) + dot_f32(piece[...], right[3], both)
        out[rows] = total.astype(BF16)


def turn(own, near, far, cross, right):
    return whole(turn_kernel, [shape(BS // PARTS, Q)], own, near, far, right, *cross, name="turn")[0]


def update_kernel(left, turned0, turned1, out):
    size = BS // PARTS
    total = dot_f32(left[:, :size], turned0[...]) + dot_f32(left[:, size:], turned1[...])
    out[...] = total.astype(BF16).reshape(out.shape)


def update(left, *turned):
    return whole(update_kernel, [shape(NB, ROWS, Q)], left, *turned, name="update")[0]


def apply_kernel(swap_ref, pieces, weights, out):
    swap = swap_ref[...]
    for part in range(NB // ROWS):
        here = pl.ds(part * ROWS, ROWS)
        total = dot_f32(swap, pieces[here].reshape(Q, Q))
        out[:, here, :] = weights[:, here, :] - 0.5 * total.reshape(ROWS, ROWS, Q)


def apply(pieces, weights):
    swap = jnp.asarray(SWAP_ROWS, BF16)
    return whole(apply_kernel, [shape(ROWS, NB, Q, kind=F32)], swap, pieces, weights, name="apply")[0]


def exchange(pieces):
    return lax.all_to_all(pieces, FSDP, split_axis=0, concat_axis=0, tiled=True)


def local(grads, weights, moment_first, moment_second, left_basis, right_basis):
    core = lax.axis_index("core").astype(jnp.int32)
    x_hi = lax.axis_index("x_hi").astype(jnp.int32)
    at = jnp.stack([x_hi, core])
    left = left_basis[0]

    own, near, far, cross = split(at, grads[0])
    near = lax.ppermute(near, "core", SWAP)
    far = pack(far, lax.ppermute(cross, "core", SWAP), BF16)
    there = lax.ppermute(far, "x_hi", SWAP)
    far, near = lax.optimization_barrier((far, near))
    here = pack(own, near, F32)
    there, here, left_turned, right = lax.optimization_barrier((there, here, flip(left), arrange(at, right_basis[0])))

    grad_block = exchange(add(here, there)).reshape(BS, Q)

    parts = range(PARTS)
    sent, kept = [], []
    for part in parts:
        send, keep = term(part, left_turned, grad_block, right)
        sent.append(lax.ppermute(send, "core", SWAP))
        kept.append(keep)
    sums = [chip_sum(kept[part], sent[part]) for part in parts]
    arrived = [lax.ppermute(send, "x_hi", SWAP) for send, _ in sums]
    arrived[0], sums[1] = lax.optimization_barrier((arrived[0], sums[1]))
    moments = (moment_first, moment_second)
    *done, own0 = adam(0, sums[0][1], arrived[0], moments, ())
    far0, near0 = lax.ppermute(own0, "x_hi", SWAP), lax.ppermute(own0, "core", SWAP)
    arrived[1], own0 = lax.optimization_barrier((arrived[1], own0))
    *done, own1 = adam(1, sums[1][1], arrived[1], moments, done)
    far1, near1 = lax.ppermute(own1, "x_hi", SWAP), lax.ppermute(own1, "core", SWAP)
    far0, own1 = lax.optimization_barrier((far0, own1))
    quarter = BS // PARTS // 2
    cross0 = [lax.ppermute(far0[n * quarter : (n + 1) * quarter], "core", SWAP) for n in range(2)]
    turned0 = turn(own0, near0, far0, cross0, right)
    far1, turned0 = lax.optimization_barrier((far1, turned0))
    turned1 = turn(own1, near1, far1, [lax.ppermute(far1, "core", SWAP)], right)

    return (apply(exchange(update(left, turned0, turned1)), weights), *done)


def solution(mesh):
    fine = Mesh(mesh.devices.reshape(8, 4, 2, 2, 2), FSDP + DP)
    placed = (
        P(DP, FSDP, None, None),
        P(FSDP, None, DP),
        P(FSDP, None, DP),
        P(FSDP, None, DP),
        P(FSDP, None, None),
        P(FSDP, DP, None),
    )
    return jax.shard_map(
        local,
        mesh=fine,
        in_specs=placed,
        out_specs=(P(FSDP, None, DP), P(FSDP, None, DP), P(FSDP, None, DP)),
        check_vma=False,
    )
```

time: 243 us -> 109 us (0.45)
  waiting for transfers between devices: 113 us -> 26.7 us
  blocking collectives: 91.4 us -> 53.2 us
  starting transfers between devices: 0.12 us -> 14.7 us
  between operations: 13.8 us -> 0.8 us
  Pallas kernels: 0 us -> 11.4 us
  matrix products: 8.54 us -> 0 us
  local copies, waits for them, and re-layouts: 10.1 us -> 1.64 us
  other arithmetic: 5.39 us -> 0.08 us
    reduce_scatter x2 -> x0, waiting for transfers between devices: 84.1 us -> none  [the longest x1 43 us: local(): lax.psum_scatter(group_term.astype(jnp.bfloat16), 'dp', scatter_dimension...]
    all_to_all x2, blocking collectives: 91.4 us -> 53.2 us  [exchange(): return lax.all_to_all(pieces, FSDP, split_axis=0, concat_axis=0, tiled=True)]
    all_gather x1 -> x0, waiting for transfers between devices: 29.1 us -> none  [local(): lax.all_gather(direction, 'dp', axis=1, tiled=True)]
    ppermute x0 -> x14, waiting for transfers between devices: none -> 26.7 us  [the longest x1 10.2 us: local(): there = lax.ppermute(far, 'x_hi', SWAP)]
    ppermute x0 -> x14, starting transfers between devices: none -> 14.7 us  [the longest x2 4.2 us: local(): arrived = [lax.ppermute(send, 'x_hi', SWAP) for send, _ in sums]]
    pallas_call x0 -> x16, Pallas kernels: none -> 11.4 us  [the longest x11 6.47 us: whole(): pl.pallas_call(kernel, grid=(1,), in_specs=[spec(value) for value in args...]
    dot_general x2 -> x0, matrix products: 8.54 us -> none  [the longest x1 4.58 us: local(): jnp.dot(rotated_left, right_rows, preferred_element_type=jnp.float32)]
    unnamed x13 -> x14, local copies, waits for them, and re-layouts: 9.55 us -> 1.62 us
  transfers between devices with their start and end apart: 3 -> 14, of which waited for: 3 -> 10; matrix products, arithmetic and copies ran while one was open for 0% -> 0% of each run, Pallas kernels for 0% -> 6%
where the time goes in v5:
time: 109 us
  blocking collectives  53.2 us (49%)
  waiting for transfers between devices  26.7 us (24%)
  starting transfers between devices  14.7 us (13%)
  Pallas kernels  11.4 us (10%)
  local copies, waits for them, and re-layouts  1.64 us (2%)
    all_to_all x2, blocking collectives, exchange(): return lax.all_to_all(pieces, FSDP, split_axis=0, concat_axis=0, tiled=True)  53.2 us
    ppermute x1, waiting for transfers between devices, local(): there = lax.ppermute(far, 'x_hi', SWAP)  10.2 us
    ppermute x2, waiting for transfers between devices, local(): arrived = [lax.ppermute(send, 'x_hi', SWAP) for send, _ in sums]  8.14 us
    pallas_call x11, Pallas kernels, whole(): pl.pallas_call(kernel, grid=(1,), in_specs=[spec(value) for value in args...  6.47 us
    ppermute x2, starting transfers between devices, local(): arrived = [lax.ppermute(send, 'x_hi', SWAP) for send, _ in sums]  4.2 us
    ppermute x1, starting transfers between devices, local(): there = lax.ppermute(far, 'x_hi', SWAP)  3.11 us
    ppermute x1, waiting for transfers between devices, local(): lax.ppermute(own1, 'x_hi', SWAP)  2.85 us
    ppermute x1, starting transfers between devices, local(): lax.ppermute(own0, 'x_hi', SWAP)  2.72 us
  transfers between devices with their start and end apart: 14, of which 10 were waited for; matrix products, arithmetic and copies ran while one was open for 0% of the time, Pallas kernels for 6%

profile of v5, /device:TPU:32, one launch (start us, length us, event | category | flops | bytes accessed | tf_op | source)
XLA Modules:
  0.0 108.5 jit_solution(10189156172661388644)
XLA Ops:
  0.6 0.1 pad_add_fusion.at
  0.7 1.6 %copy-done = bf16[1,16,64,1024]{3,2,1,0:T(8,128)(2,1)S(1)} copy-done((bf16[1,16,64,1024]{3,2,1,0:T(8,128)(2,1)S(1)}, bf16[1,16,64,1024]{3,2,1,0:T(8,128)(2,1)}, u32[]{:S(2)}) %copy-start) | copy-done | bytes 2097176
  2.3 0.8 split.1
  3.1 0.1 collective-permute-start
  3.2 0.5 collective-permute-start.2
  3.7 1.4 %collective-permute-done.arrived = bf16[16,64,256]{2,1,0:T(8,128)(2,1)S(1)} collective-permute-done((bf16[16,64,256]{2,1,0:T(8,128)(2,1)S(1)}, bf16[16,64,256]{2,1,0:T(8,128)(2,1)S(1)}, u32[]{:S(2)}, u32[]{:S(2)}) %collective-permute-start) | collective-permute-done | bytes 524320 | tf_op jit(solution)/shard_map/ppermute | solution.py:257
  5.1 0.4 pack.2
  5.6 3.1 %collective-permute-start.1 = (bf16[64,16,256]{2,1,0:T(8,128)(2,1)S(1)}, bf16[64,16,256]{2,1,0:T(8,128)(2,1)S(1)}, u32[]{:S(2)}, u32[]{:S(2)}) collective-permute-start(bf16[64,16,256]{2,1,0:T(8,128)(2,1)S(1)} %pack.2), channel_id=1, source_target_pairs={{0,2},{2,0},{1,3},{3,1},{4,6},{6,4},{5,7},{7,5},{8,10},{10,8},{9,1... | collective-permute-start | bytes 1572872 | tf_op jit(solution)/shard_map/ppermute | solution.py:258
  8.7 0.6 arrange.1.right
  9.3 1.1 %flip.1.left = bf16[1024,1024]{1,0:T(8,128)(2,1)S(1)} custom-call(bf16[1024,1024]{1,0:T(8,128)(2,1)S(1)} %bitcast.10), custom_call_target="tpu_custom_call" | custom-call | bytes 8388608 | tf_op jit(solution)/shard_map/flip/pallas_call | solution.py:137
  10.5 0.4 pack.3.here
  10.9 10.2 %collective-permute-done.1.there = bf16[64,16,256]{2,1,0:T(8,128)(2,1)S(1)} collective-permute-done((bf16[64,16,256]{2,1,0:T(8,128)(2,1)S(1)}, bf16[64,16,256]{2,1,0:T(8,128)(2,1)S(1)}, u32[]{:S(2)}, u32[]{:S(2)}) %collective-permute-start.1) | collective-permute-done | bytes 524320 | tf_op jit(solution)/shard_map/ppermute | solution.py:258
  21.1 0.1 add.3
  21.2 29.7 %all_to_all.10 = bf16[64,16,256]{2,1,0:T(8,128)(2,1)S(1)} all-to-all(bf16[64,16,256]{2,1,0:T(8,128)(2,1)S(1)} %add.3), channel_id=1, replica_groups=mesh['z'=8,'y'=4,'x_lo'=2,'x_hi'=2,'core'=2] {'z','y','x_lo'}, dimensions={0} | all-to-all | bytes 1048576 | tf_op jit(solution)/shard_map/all_to_all | solution.py:246
  50.9 1.2 %term.2 = (bf16[2,512,256]{2,1,0:T(8,128)(2,1)S(1)}, f32[2,512,256]{2,1,0:T(8,128)S(1)}) custom-call(bf16[1024,1024]{1,0:T(8,128)(2,1)S(1)} %flip.1.left, bf16[1024,256]{1,0:T(8,128)(2,1)S(1)} %bitcast.16, bf16[4,256,256]{2,1,0:T(8,128)(2,1)S(1)} %arrange.1.right), custom_call_target="tpu_custom_call" | custom-call | flops 536870912 | bytes 1024 | tf_op jit(solution)/shard_map/term/pallas_call | solution.py:94
  52.1 0.1 collective-permute-start.3
  52.2 1.2 %term.3 = (bf16[2,512,256]{2,1,0:T(8,128)(2,1)S(1)}, f32[2,512,256]{2,1,0:T(8,128)S(1)}) custom-call(bf16[1024,1024]{1,0:T(8,128)(2,1)S(1)} %flip.1.left, bf16[1024,256]{1,0:T(8,128)(2,1)S(1)} %bitcast.17, bf16[4,256,256]{2,1,0:T(8,128)(2,1)S(1)} %arrange.1.right), custom_call_target="tpu_custom_call" | custom-call | flops 536870912 | bytes 1024 | tf_op jit(solution)/shard_map/term/pallas_call | solution.py:94
  53.5 0.0 copy-start.3
  53.5 0.0 copy-start.4
  53.5 0.6 collective-permute-start.5
  54.1 0.1 collective-permute-done.3.arrived
  54.1 0.1 chip_sum.2
  54.2 2.8 %collective-permute-start.4 = (bf16[512,256]{1,0:T(8,128)(2,1)S(1)}, bf16[512,256]{1,0:T(8,128)(2,1)S(1)}, u32[]{:S(2)}, u32[]{:S(2)}) collective-permute-start(bf16[512,256]{1,0:T(8,128)(2,1)S(1)} %get-tuple-element.45), channel_id=1, source_target_pairs={{0,2},{2,0},{1,3},{3,1},{4,6},{6,4},{5,7},{7,5},{8,10},{10,8},{9,1... | collective-permute-start | bytes 786440 | tf_op jit(solution)/shard_map/ppermute | solution.py:272
  57.0 0.0 collective-permute-done.5.arrived
  57.0 0.1 chip_sum.3
  57.1 1.4 %collective-permute-start.6 = (bf16[512,256]{1,0:T(8,128)(2,1)S(1)}, bf16[512,256]{1,0:T(8,128)(2,1)S(1)}, u32[]{:S(2)}, u32[]{:S(2)}) collective-permute-start(bf16[512,256]{1,0:T(8,128)(2,1)S(1)} %get-tuple-element.48), channel_id=1, source_target_pairs={{0,2},{2,0},{1,3},{3,1},{4,6},{6,4},{5,7},{7,5},{8,10},{10,8},{9,1... | collective-permute-start | bytes 786440 | tf_op jit(solution)/shard_map/ppermute | solution.py:272
  58.5 6.4 %collective-permute-done.4.far = bf16[512,256]{1,0:T(8,128)(2,1)S(1)} collective-permute-done((bf16[512,256]{1,0:T(8,128)(2,1)S(1)}, bf16[512,256]{1,0:T(8,128)(2,1)S(1)}, u32[]{:S(2)}, u32[]{:S(2)}) %collective-permute-start.4) | collective-permute-done | bytes 262176 | tf_op jit(solution)/shard_map/ppermute | solution.py:272
  65.0 1.2 %adam.2 = (f32[1,1024,256]{2,1,0:T(8,128)}, f32[1,1024,256]{2,1,0:T(8,128)}, bf16[512,256]{1,0:T(8,128)(2,1)S(1)}) custom-call(f32[512,256]{1,0:T(8,128)S(1)} %get-tuple-element.51.own, bf16[512,256]{1,0:T(8,128)(2,1)S(1)} %collective-permute-done.4.far, f32[1,1024,256]{2,1,0:T(8,128)S(1)} %copy-done.3, f32[1,1024,256]{2,1,0:T(8,128)S(1)} %copy-done.4), custom_call_target="tpu_custom_call" | custom-call | flops 1024 | bytes 1024 | tf_op jit(solution)/shard_map/adam/pallas_call | solution.py:194
  66.2 2.7 %collective-permute-start.9 = (bf16[512,256]{1,0:T(8,128)(2,1)S(1)}, bf16[512,256]{1,0:T(8,128)(2,1)S(1)}, u32[]{:S(2)}, u32[]{:S(2)}) collective-permute-start(bf16[512,256]{1,0:T(8,128)(2,1)S(1)} %get-tuple-element.58.own), channel_id=1, source_target_pairs={{0,2},{2,0},{1,3},{3,1},{4,6},{6,4},{5,7},{7,5},{8,10},{10,8},{9,1... | collective-permute-start | bytes 786440 | tf_op jit(solution)/shard_map/ppermute | solution.py:276
  68.9 1.7 %collective-permute-done.6.far = bf16[512,256]{1,0:T(8,128)(2,1)S(1)} collective-permute-done((bf16[512,256]{1,0:T(8,128)(2,1)S(1)}, bf16[512,256]{1,0:T(8,128)(2,1)S(1)}, u32[]{:S(2)}, u32[]{:S(2)}) %collective-permute-start.6) | collective-permute-done | bytes 262176 | tf_op jit(solution)/shard_map/ppermute | solution.py:272
  70.6 1.2 %adam.3 = (f32[1,1024,256]{2,1,0:T(8,128)}, f32[1,1024,256]{2,1,0:T(8,128)}, bf16[512,256]{1,0:T(8,128)(2,1)S(1)}) custom-call(f32[512,256]{1,0:T(8,128)S(1)} %get-tuple-element.50.own, bf16[512,256]{1,0:T(8,128)(2,1)S(1)} %collective-permute-done.6.far, f32[1,1024,256]{2,1,0:T(8,128)S(1)} %copy-done.3, ...), custom_call_target="tpu_custom_call", output_to_operand_aliasing={{0}: (4, {}), {1}: (5, {})} | custom-call | flops 1024 | bytes 1024 | tf_op jit(solution)/shard_map/adam/pallas_call | solution.py:194
  71.8 2.7 %collective-permute-start.7 = (bf16[512,256]{1,0:T(8,128)(2,1)S(1)}, bf16[512,256]{1,0:T(8,128)(2,1)S(1)}, u32[]{:S(2)}, u32[]{:S(2)}) collective-permute-start(bf16[512,256]{1,0:T(8,128)(2,1)S(1)} %get-tuple-element.61.own), channel_id=1, source_target_pairs={{0,2},{2,0},{1,3},{3,1},{4,6},{6,4},{5,7},{7,5},{8,10},{10,8},{9,1... | collective-permute-start | bytes 786440 | tf_op jit(solution)/shard_map/ppermute | solution.py:279
  74.5 1.6 %collective-permute-done.9.far = bf16[512,256]{1,0:T(8,128)(2,1)S(1)} collective-permute-done((bf16[512,256]{1,0:T(8,128)(2,1)S(1)}, bf16[512,256]{1,0:T(8,128)(2,1)S(1)}, u32[]{:S(2)}, u32[]{:S(2)}) %collective-permute-start.9) | collective-permute-done | bytes 262176 | tf_op jit(solution)/shard_map/ppermute | solution.py:276
  76.1 0.1 collective-permute-start.10
  76.2 0.5 collective-permute-start.11
  76.7 0.1 collective-permute-start.12
  76.8 0.0 collective-permute-done.8.near
  76.8 0.7 collective-permute-done.10.rest_0_
  77.5 0.2 collective-permute-done.11.rest_1_
  77.7 0.5 turn.2.turned0
  78.2 2.9 %collective-permute-done.7.far = bf16[512,256]{1,0:T(8,128)(2,1)S(1)} collective-permute-done((bf16[512,256]{1,0:T(8,128)(2,1)S(1)}, bf16[512,256]{1,0:T(8,128)(2,1)S(1)}, u32[]{:S(2)}, u32[]{:S(2)}) %collective-permute-start.7) | collective-permute-done | bytes 262176 | tf_op jit(solution)/shard_map/ppermute | solution.py:279
  81.0 0.0 collective-permute-start.13
  81.0 1.5 %collective-permute-done.13.rest_0_ = bf16[512,256]{1,0:T(8,128)(2,1)S(1)} collective-permute-done((bf16[512,256]{1,0:T(8,128)(2,1)S(1)}, bf16[512,256]{1,0:T(8,128)(2,1)S(1)}, u32[]{:S(2)}, u32[]{:S(2)}) %collective-permute-start.13) | collective-permute-done | bytes 262176 | tf_op jit(solution)/shard_map/ppermute | solution.py:285
  82.6 0.5 turn.3.turned1
  83.0 0.0 copy-start.6
  83.0 0.7 update.1
  83.8 23.5 %all_to_all.11.pieces = bf16[64,16,256]{2,1,0:T(8,128)(2,1)S(1)} all-to-all(bf16[64,16,256]{2,1,0:T(8,128)(2,1)S(1)} %update.1), channel_id=1, replica_groups=mesh['z'=8,'y'=4,'x_lo'=2,'x_hi'=2,'core'=2] {'z','y','x_lo'}, dimensions={0} | all-to-all | bytes 1048576 | tf_op jit(solution)/shard_map/all_to_all | solution.py:246
  107.3 1.3 %apply.1 = f32[16,64,256]{2,1,0:T(8,128)} custom-call(bf16[256,256]{1,0:T(8,128)(2,1)S(1)} %copy-done.5, bf16[64,16,256]{2,1,0:T(8,128)(2,1)S(1)} %all_to_all.11.pieces, f32[16,64,256]{2,1,0:T(8,128)S(1)} %copy-done.6), custom_call_target="tpu_custom_call" | custom-call | bytes 1024 | tf_op jit(solution)/shard_map/apply/pallas_call | solution.py:94
  (14 shorter events, 0.0 us)
Async XLA Ops:
  0.7 1.6 %copy-start = (bf16[1,16,64,1024]{3,2,1,0:T(8,128)(2,1)S(1)}, bf16[1,16,64,1024]{3,2,1,0:T(8,128)(2,1)}, u32[]{:S(2)}) copy-start(bf16[1,16,64,1024]{3,2,1,0:T(8,128)(2,1)} %param.9) | copy-start | bytes 6291460
  2.3 2.8 %copy-start.5 = (bf16[256,256]{1,0:T(8,128)(2,1)S(1)}, bf16[256,256]{1,0:T(8,128)(2,1)}, u32[]{:S(2)}) copy-start(bf16[256,256]{1,0:T(8,128)(2,1)} %constant.8.clone.swap_ref) | copy-start | bytes 393220
  2.3 6.4 %copy-start.2 = (bf16[1,256,1024]{2,1,0:T(8,128)(2,1)S(1)}, bf16[1,256,1024]{2,1,0:T(8,128)(2,1)}, u32[]{:S(2)}) copy-start(bf16[1,256,1024]{2,1,0:T(8,128)(2,1)} %param.14) | copy-start | bytes 1572868
  3.1 2.0 %collective-permute-start = (bf16[16,64,256]{2,1,0:T(8,128)(2,1)S(1)}, bf16[16,64,256]{2,1,0:T(8,128)(2,1)S(1)}, u32[]{:S(2)}, u32[]{:S(2)}) collective-permute-start(bf16[16,64,256]{2,1,0:T(8,128)(2,1)S(1)} %get-tuple-element.35), channel_id=1, source_target_pairs={{0,1},{1,0},{2,3},{3,2},{4,5},{5,4},{6,7},{7,6},{8,9},{9,8},{10,11... | collective-permute-start | bytes 1572872 | tf_op jit(solution)/shard_map/ppermute | solution.py:257
  3.2 7.2 %collective-permute-start.2 = (bf16[16,64,256]{2,1,0:T(8,128)(2,1)S(1)}, bf16[16,64,256]{2,1,0:T(8,128)(2,1)S(1)}, u32[]{:S(2)}, u32[]{:S(2)}) collective-permute-start(bf16[16,64,256]{2,1,0:T(8,128)(2,1)S(1)} %get-tuple-element.37), channel_id=1, source_target_pairs={{0,1},{1,0},{2,3},{3,2},{4,5},{5,4},{6,7},{7,6},{8,9},{9,8},{10,11... | collective-permute-start | bytes 1572872 | tf_op jit(solution)/shard_map/ppermute | solution.py:256
  5.1 4.2 %copy-start.1 = (bf16[1,1024,1024]{2,1,0:T(8,128)(2,1)S(1)}, bf16[1,1024,1024]{2,1,0:T(8,128)(2,1)}, u32[]{:S(2)}) copy-start(bf16[1,1024,1024]{2,1,0:T(8,128)(2,1)} %param.13) | copy-start | bytes 6291460
  5.6 15.6 %collective-permute-start.1 = (bf16[64,16,256]{2,1,0:T(8,128)(2,1)S(1)}, bf16[64,16,256]{2,1,0:T(8,128)(2,1)S(1)}, u32[]{:S(2)}, u32[]{:S(2)}) collective-permute-start(bf16[64,16,256]{2,1,0:T(8,128)(2,1)S(1)} %pack.2), channel_id=1, source_target_pairs={{0,2},{2,0},{1,3},{3,1},{4,6},{6,4},{5,7},{7,5},{8,10},{10,8},{9,1... | collective-permute-start | bytes 1572872 | tf_op jit(solution)/shard_map/ppermute | solution.py:258
  52.1 2.0 %collective-permute-start.3 = (bf16[2,512,256]{2,1,0:T(8,128)(2,1)S(1)}, bf16[2,512,256]{2,1,0:T(8,128)(2,1)S(1)}, u32[]{:S(2)}, u32[]{:S(2)}) collective-permute-start(bf16[2,512,256]{2,1,0:T(8,128)(2,1)S(1)} %get-tuple-element.44), channel_id=1, source_target_pairs={{0,1},{1,0},{2,3},{3,2},{4,5},{5,4},{6,7},{7,6},{8,9},{9,8},{10,11... | collective-permute-start | bytes 1572872 | tf_op jit(solution)/shard_map/ppermute | solution.py:269
  53.5 11.5 %copy-start.3 = (f32[1,1024,256]{2,1,0:T(8,128)S(1)}, f32[1,1024,256]{2,1,0:T(8,128)}, u32[]{:S(2)}) copy-start(f32[1,1024,256]{2,1,0:T(8,128)} %m1.3) | copy-start | bytes 3145732
  53.5 11.5 %copy-start.4 = (f32[1,1024,256]{2,1,0:T(8,128)S(1)}, f32[1,1024,256]{2,1,0:T(8,128)}, u32[]{:S(2)}) copy-start(f32[1,1024,256]{2,1,0:T(8,128)} %m2.3) | copy-start | bytes 3145732
  53.5 3.6 %collective-permute-start.5 = (bf16[2,512,256]{2,1,0:T(8,128)(2,1)S(1)}, bf16[2,512,256]{2,1,0:T(8,128)(2,1)S(1)}, u32[]{:S(2)}, u32[]{:S(2)}) collective-permute-start(bf16[2,512,256]{2,1,0:T(8,128)(2,1)S(1)} %get-tuple-element.47), channel_id=1, source_target_pairs={{0,1},{1,0},{2,3},{3,2},{4,5},{5,4},{6,7},{7,6},{8,9},{9,8},{10,11... | collective-permute-start | bytes 1572872 | tf_op jit(solution)/shard_map/ppermute | solution.py:269
  54.2 10.7 %collective-permute-start.4 = (bf16[512,256]{1,0:T(8,128)(2,1)S(1)}, bf16[512,256]{1,0:T(8,128)(2,1)S(1)}, u32[]{:S(2)}, u32[]{:S(2)}) collective-permute-start(bf16[512,256]{1,0:T(8,128)(2,1)S(1)} %get-tuple-element.45), channel_id=1, source_target_pairs={{0,2},{2,0},{1,3},{3,1},{4,6},{6,4},{5,7},{7,5},{8,10},{10,8},{9,1... | collective-permute-start | bytes 786440 | tf_op jit(solution)/shard_map/ppermute | solution.py:272
  57.1 13.5 %collective-permute-start.6 = (bf16[512,256]{1,0:T(8,128)(2,1)S(1)}, bf16[512,256]{1,0:T(8,128)(2,1)S(1)}, u32[]{:S(2)}, u32[]{:S(2)}) collective-permute-start(bf16[512,256]{1,0:T(8,128)(2,1)S(1)} %get-tuple-element.48), channel_id=1, source_target_pairs={{0,2},{2,0},{1,3},{3,1},{4,6},{6,4},{5,7},{7,5},{8,10},{10,8},{9,1... | collective-permute-start | bytes 786440 | tf_op jit(solution)/shard_map/ppermute | solution.py:272
  66.2 9.9 %collective-permute-start.9 = (bf16[512,256]{1,0:T(8,128)(2,1)S(1)}, bf16[512,256]{1,0:T(8,128)(2,1)S(1)}, u32[]{:S(2)}, u32[]{:S(2)}) collective-permute-start(bf16[512,256]{1,0:T(8,128)(2,1)S(1)} %get-tuple-element.58.own), channel_id=1, source_target_pairs={{0,2},{2,0},{1,3},{3,1},{4,6},{6,4},{5,7},{7,5},{8,10},{10,8},{9,1... | collective-permute-start | bytes 786440 | tf_op jit(solution)/shard_map/ppermute | solution.py:276
  68.9 7.9 %collective-permute-start.8 = (bf16[512,256]{1,0:T(8,128)(2,1)S(1)}, bf16[512,256]{1,0:T(8,128)(2,1)S(1)}, u32[]{:S(2)}, u32[]{:S(2)}) collective-permute-start(bf16[512,256]{1,0:T(8,128)(2,1)S(1)} %get-tuple-element.58.own), channel_id=1, source_target_pairs={{0,1},{1,0},{2,3},{3,2},{4,5},{5,4},{6,7},{7,6},{8,9},{9,8},{10,11... | collective-permute-start | bytes 786440 | tf_op jit(solution)/shard_map/ppermute | solution.py:276
  71.8 9.2 %collective-permute-start.7 = (bf16[512,256]{1,0:T(8,128)(2,1)S(1)}, bf16[512,256]{1,0:T(8,128)(2,1)S(1)}, u32[]{:S(2)}, u32[]{:S(2)}) collective-permute-start(bf16[512,256]{1,0:T(8,128)(2,1)S(1)} %get-tuple-element.61.own), channel_id=1, source_target_pairs={{0,2},{2,0},{1,3},{3,1},{4,6},{6,4},{5,7},{7,5},{8,10},{10,8},{9,1... | collective-permute-start | bytes 786440 | tf_op jit(solution)/shard_map/ppermute | solution.py:279
  76.1 1.4 %collective-permute-start.10 = (bf16[256,256]{1,0:T(8,128)(2,1)S(1)}, bf16[256,256]{1,0:T(8,128)(2,1)S(1)}, u32[]{:S(2)}, u32[]{:S(2)}) collective-permute-start(bf16[256,256]{1,0:T(8,128)(2,1)S(1)} %get-tuple-element.66), channel_id=1, source_target_pairs={{0,1},{1,0},{2,3},{3,2},{4,5},{5,4},{6,7},{7,6},{8,9},{9,8},{10,11... | collective-permute-start | bytes 393224 | tf_op jit(solution)/shard_map/ppermute | solution.py:282
  76.2 1.5 %collective-permute-start.11 = (bf16[256,256]{1,0:T(8,128)(2,1)S(1)}, bf16[256,256]{1,0:T(8,128)(2,1)S(1)}, u32[]{:S(2)}, u32[]{:S(2)}) collective-permute-start(bf16[256,256]{1,0:T(8,128)(2,1)S(1)} %get-tuple-element.65), channel_id=1, source_target_pairs={{0,1},{1,0},{2,3},{3,2},{4,5},{5,4},{6,7},{7,6},{8,9},{9,8},{10,11... | collective-permute-start | bytes 393224 | tf_op jit(solution)/shard_map/ppermute | solution.py:282
  76.7 4.4 %collective-permute-start.12 = (bf16[512,256]{1,0:T(8,128)(2,1)S(1)}, bf16[512,256]{1,0:T(8,128)(2,1)S(1)}, u32[]{:S(2)}, u32[]{:S(2)}) collective-permute-start(bf16[512,256]{1,0:T(8,128)(2,1)S(1)} %get-tuple-element.61.own), channel_id=1, source_target_pairs={{0,1},{1,0},{2,3},{3,2},{4,5},{5,4},{6,7},{7,6},{8,9},{9,8},{10,11... | collective-permute-start | bytes 786440 | tf_op jit(solution)/shard_map/ppermute | solution.py:279
  81.0 1.5 %collective-permute-start.13 = (bf16[512,256]{1,0:T(8,128)(2,1)S(1)}, bf16[512,256]{1,0:T(8,128)(2,1)S(1)}, u32[]{:S(2)}, u32[]{:S(2)}) collective-permute-start(bf16[512,256]{1,0:T(8,128)(2,1)S(1)} %collective-permute-done.7.far), channel_id=1, source_target_pairs={{0,1},{1,0},{2,3},{3,2},{4,5},{5,4},{6,7},{7,6},{8,9},{9,8},{10,11... | collective-permute-start | bytes 786440 | tf_op jit(solution)/shard_map/ppermute | solution.py:285
  83.0 24.2 %copy-start.6 = (f32[16,64,256]{2,1,0:T(8,128)S(1)}, f32[16,64,256]{2,1,0:T(8,128)}, u32[]{:S(2)}) copy-start(f32[16,64,256]{2,1,0:T(8,128)} %weights.1) | copy-start | bytes 3145732

commit v6 on v5

--- a/solution.py
+++ b/solution.py
@@ -44,22 +44,26 @@
     ]
 
 
-def split_kernel(at, *refs):
-    for n in range(4):
-        refs[4 + n][...] = refs[n][...]
+def split_kernel(at, own, near, far, cross, own_out, near_out, far_out, cross_low, cross_high):
+    own_out[...] = own[...]
+    near_out[...] = near[...]
+    far_out[...] = far[...]
+    cross_low[...] = cross[:, : NB // 2]
+    cross_high[...] = cross[:, NB // 2 :]
 
 
 def split(at, grads):
     held = pl.BlockSpec((ROWS, NB, Q), lambda i, at: (0, 0, 0))
+    half = pl.BlockSpec((ROWS, NB // 2, Q), lambda i, at: (0, 0, 0))
     return pl.pallas_call(
         split_kernel,
         grid_spec=pltpu.PrefetchScalarGridSpec(
             num_scalar_prefetch=1,
             grid=(1,),
             in_specs=group_specs((ROWS, NB, Q), 2),
-            out_specs=[held] * 4,
+            out_specs=[held] * 3 + [half] * 2,
         ),
-        out_shape=[jax.ShapeDtypeStruct((ROWS, NB, Q), BF16)] * 4,
+        out_shape=[shape(ROWS, NB, Q)] * 3 + [shape(ROWS, NB // 2, Q)] * 2,
         compiler_params=PARAMS,
         cost_estimate=cost(0, 4 << 20),
         name="split",
@@ -107,25 +111,29 @@
     return jax.ShapeDtypeStruct(dims, kind)
 
 
-def pack_kernel(swap_ref, kept, arrived, out):
+def pack_kernel(first, swap_ref, kept, arrived, out):
     swap = swap_ref[...]
-    for part in range(NB // ROWS):
-        here = pl.ds(part * ROWS, ROWS)
-        total = dot_f32(swap, kept[:, here, :].reshape(Q, Q)) + dot_f32(swap, arrived[:, here, :].reshape(Q, Q))
+    for part in range(out.shape[0] // ROWS):
+        here = slice(part * ROWS, (part + 1) * ROWS)
+        there = slice(first + part * ROWS, first + (part + 1) * ROWS)
+        total = dot_f32(swap, kept[:, there, :].reshape(Q, Q)) + dot_f32(swap, arrived[:, here, :].reshape(Q, Q))
         out[here] = total.astype(out.dtype).reshape(ROWS, ROWS, Q)
 
 
-def pack(kept, arrived, kind):
+def pack(first, kept, arrived, kind):
     swap = jnp.asarray(SWAP_ROWS, BF16)
-    return whole(pack_kernel, [shape(NB, ROWS, Q, kind=kind)], swap, kept, arrived, name="pack")[0]
-
-
-def add_kernel(here, there, out):
-    out[...] = (here[...] + there[...].astype(F32)).astype(BF16)
-
-
-def add(here, there):
-    return whole(add_kernel, [shape(NB, ROWS, Q)], here, there, name="add")[0]
+    outs = [shape(arrived.shape[1], ROWS, Q, kind=kind)]
+    return whole(functools.partial(pack_kernel, first), outs, swap, kept, arrived, name="pack")[0]
+
+
+def add_kernel(here, low, high, out):
+    half = NB // 2
+    out[:half] = (here[:half] + low[...].astype(F32)).astype(BF16)
+    out[half:] = (here[half:] + high[...].astype(F32)).astype(BF16)
+
+
+def add(here, low, high):
+    return whole(add_kernel, [shape(NB, ROWS, Q)], here, low, high, name="add")[0]
 
 
 def flip_kernel(values, out):
@@ -172,36 +180,36 @@
     return whole(chip_kernel, [shape(size, Q), shape(size, Q, kind=F32)], kept, arrived, name="chip_sum")
 
 
-def adam_kernel(part, own, far, m1, m2, *rest):
-    first, second, direction = rest[-3:]
+def moments_of(rotated, m1, m2):
+    return 0.9 * m1 + 0.1 * rotated, 0.95 * m2 + 0.05 * rotated * rotated
+
+
+def adam_kernel(part, own, far, m1, m2, rotated, direction):
     size = own.shape[0]
     rows = slice(part * size, (part + 1) * size)
-    rotated = own[...] + far[...].astype(F32)
-    new1 = 0.9 * m1[0, rows] + 0.1 * rotated
-    new2 = 0.95 * m2[0, rows] + 0.05 * rotated * rotated
-    first[0] = new1
-    second[0] = new2
+    rotated[...] = own[...] + far[...].astype(F32)
+    new1, new2 = moments_of(rotated[...], m1[0, rows], m2[0, rows])
     bias_first = 1.0 - 0.9**10
     bias_second = 1.0 - 0.95**10
     direction[...] = (new1 / bias_first / (jnp.sqrt(new2 / bias_second) + 1e-08)).astype(BF16)
 
 
-def adam(part, own, far, moments, done):
-    size = BS // PARTS
-    rows = pl.BlockSpec((size, Q), lambda i: (0, 0))
-    old = pl.BlockSpec((1, BS, Q), lambda i: (0, 0, 0))
-    new = pl.BlockSpec((1, size, Q), lambda i: (0, part, 0))
-    return pl.pallas_call(
-        functools.partial(adam_kernel, part),
-        grid=(1,),
-        in_specs=[rows] * 2 + [old] * 2 + [pl.BlockSpec(memory_space=pl.ANY)] * len(done),
-        out_specs=[new, new, rows],
-        out_shape=[shape(1, BS, Q, kind=F32), shape(1, BS, Q, kind=F32), shape(size, Q)],
-        input_output_aliases={4 + n: n for n in range(len(done))},
-        compiler_params=PARAMS,
-        cost_estimate=cost(1 << 10, 1 << 10),
-        name="adam",
-    )(own, far, *moments, *done)
+def adam(part, own, far, moments):
+    size = BS // PARTS
+    kernel = functools.partial(adam_kernel, part)
+    return whole(kernel, [shape(size, Q, kind=F32), shape(size, Q)], own, far, *moments, name="adam")
+
+
+def moments_kernel(rotated0, rotated1, m1, m2, first, second):
+    size = BS // PARTS
+    for part, rotated in enumerate((rotated0, rotated1)):
+        rows = slice(part * size, (part + 1) * size)
+        first[0, rows], second[0, rows] = moments_of(rotated[...], m1[0, rows], m2[0, rows])
+
+
+def new_moments(rotated, moments):
+    outs = [shape(1, BS, Q, kind=F32)] * 2
+    return whole(moments_kernel, outs, *rotated, *moments, name="moments")
 
 
 def turn_kernel(own, near, far, right, *rest):
@@ -252,15 +260,20 @@
     at = jnp.stack([x_hi, core])
     left = left_basis[0]
 
-    own, near, far, cross = split(at, grads[0])
-    near = lax.ppermute(near, "core", SWAP)
-    far = pack(far, lax.ppermute(cross, "core", SWAP), BF16)
-    there = lax.ppermute(far, "x_hi", SWAP)
-    far, near = lax.optimization_barrier((far, near))
-    here = pack(own, near, F32)
-    there, here, left_turned, right = lax.optimization_barrier((there, here, flip(left), arrange(at, right_basis[0])))
-
-    grad_block = exchange(add(here, there)).reshape(BS, Q)
+    own, near, far, low, high = split(at, grads[0])
+    low, high, near = (lax.ppermute(value, "core", SWAP) for value in (low, high, near))
+    low = pack(0, far, low, BF16)
+    low_there = lax.ppermute(low, "x_hi", SWAP)
+    low, high = lax.optimization_barrier((low, high))
+    high = pack(NB // 2, far, high, BF16)
+    high_there = lax.ppermute(high, "x_hi", SWAP)
+    high, near = lax.optimization_barrier((high, near))
+    here = pack(0, own, near, F32)
+    low_there, high_there, here, left_turned, right = lax.optimization_barrier(
+        (low_there, high_there, here, flip(left), arrange(at, right_basis[0]))
+    )
+
+    grad_block = exchange(add(here, low_there, high_there)).reshape(BS, Q)
 
     parts = range(PARTS)
     sent, kept = [], []
@@ -272,19 +285,20 @@
     arrived = [lax.ppermute(send, "x_hi", SWAP) for send, _ in sums]
     arrived[0], sums[1] = lax.optimization_barrier((arrived[0], sums[1]))
     moments = (moment_first, moment_second)
-    *done, own0 = adam(0, sums[0][1], arrived[0], moments, ())
+    rotated0, own0 = adam(0, sums[0][1], arrived[0], moments)
     far0, near0 = lax.ppermute(own0, "x_hi", SWAP), lax.ppermute(own0, "core", SWAP)
     arrived[1], own0 = lax.optimization_barrier((arrived[1], own0))
-    *done, own1 = adam(1, sums[1][1], arrived[1], moments, done)
+    rotated1, own1 = adam(1, sums[1][1], arrived[1], moments)
     far1, near1 = lax.ppermute(own1, "x_hi", SWAP), lax.ppermute(own1, "core", SWAP)
-    far0, own1 = lax.optimization_barrier((far0, own1))
+    first_new, second_new = new_moments((rotated0, rotated1), moments)
+    far0, own1, first_new, second_new = lax.optimization_barrier((far0, own1, first_new, second_new))
     quarter = BS // PARTS // 2
     cross0 = [lax.ppermute(far0[n * quarter : (n + 1) * quarter], "core", SWAP) for n in range(2)]
     turned0 = turn(own0, near0, far0, cross0, right)
     far1, turned0 = lax.optimization_barrier((far1, turned0))
     turned1 = turn(own1, near1, far1, [lax.ppermute(far1, "core", SWAP)], right)
 
-    return (apply(exchange(update(left, turned0, turned1)), weights), *done)
+    return (apply(exchange(update(left, turned0, turned1)), weights), first_new, second_new)
 
 
 def solution(mesh):

time: 109 us -> 109 us (level)
  waiting for transfers between devices: 26.7 us -> 25.5 us
    pallas_call x11 -> x15, Pallas kernels: 6.47 us -> 9.63 us  [whole(): pl.pallas_call(kernel, grid=(1,), in_specs=[spec(value) for value in args...]
    pallas_call x2 -> x0, Pallas kernels: 2.37 us -> none  [adam(): pl.pallas_call(functools.partial(adam_kernel, part), grid=(1,), in_specs=...]
    ppermute x3 -> x5, starting transfers between devices: 3.7 us -> 4.31 us  [the longest x1 3.12 us: local(): high_there = lax.ppermute(high, 'x_hi', SWAP)]
    ppermute x3 -> x5, waiting for transfers between devices: 11.6 us -> 11.5 us  [the longest x1 4.92 us: local(): high_there = lax.ppermute(high, 'x_hi', SWAP)]
  transfers between devices with their start and end apart: 14 -> 16, of which waited for: 10 -> 12; matrix products, arithmetic and copies ran while one was open for 0% -> 0% of each run, Pallas kernels for 6% -> 7%
where the time goes in v6:
time: 109 us
  blocking collectives  53.2 us (49%)
  waiting for transfers between devices  25.5 us (23%)
  starting transfers between devices  15.7 us (14%)
  Pallas kernels  12.2 us (11%)
  local copies, waits for them, and re-layouts  1.64 us (2%)
    all_to_all x2, blocking collectives, exchange(): return lax.all_to_all(pieces, FSDP, split_axis=0, concat_axis=0, tiled=True)  53.2 us
    pallas_call x15, Pallas kernels, whole(): pl.pallas_call(kernel, grid=(1,), in_specs=[spec(value) for value in args...  9.63 us
    ppermute x2, waiting for transfers between devices, local(): arrived = [lax.ppermute(send, 'x_hi', SWAP) for send, _ in sums]  8.51 us
    ppermute x1, waiting for transfers between devices, local(): high_there = lax.ppermute(high, 'x_hi', SWAP)  4.92 us
    ppermute x1, waiting for transfers between devices, local(): low_there = lax.ppermute(low, 'x_hi', SWAP)  4.81 us
    ppermute x2, starting transfers between devices, local(): arrived = [lax.ppermute(send, 'x_hi', SWAP) for send, _ in sums]  4.21 us
    ppermute x1, starting transfers between devices, local(): high_there = lax.ppermute(high, 'x_hi', SWAP)  3.12 us
    ppermute x1, starting transfers between devices, local(): lax.ppermute(own1, 'x_hi', SWAP)  3 us
  transfers between devices with their start and end apart: 16, of which 12 were waited for; matrix products, arithmetic and copies ran while one was open for 0% of the time, Pallas kernels for 7%

profile of v6, /device:TPU:32, one launch (start us, length us, event | category | flops | bytes accessed | tf_op | source)
XLA Modules:
  0.0 109.1 jit_solution(5037070971188960365)
XLA Ops:
  0.6 0.1 pad_add_fusion.at
  0.7 1.6 %copy-done = bf16[1,16,64,1024]{3,2,1,0:T(8,128)(2,1)S(1)} copy-done((bf16[1,16,64,1024]{3,2,1,0:T(8,128)(2,1)S(1)}, bf16[1,16,64,1024]{3,2,1,0:T(8,128)(2,1)}, u32[]{:S(2)}) %copy-start) | copy-done | bytes 2097176
  2.3 0.8 split.1
  3.1 0.1 collective-permute-start
  3.2 0.5 collective-permute-start.4
  3.7 0.1 collective-permute-start.2
  3.8 0.9 collective-permute-done.arrived
  4.8 0.3 pack.3
  5.1 0.8 collective-permute-done.2.arrived
  5.9 0.3 pack.4
  6.2 3.1 %collective-permute-start.3 = (bf16[32,16,256]{2,1,0:T(8,128)(2,1)S(1)}, bf16[32,16,256]{2,1,0:T(8,128)(2,1)S(1)}, u32[]{:S(2)}, u32[]{:S(2)}) collective-permute-start(bf16[32,16,256]{2,1,0:T(8,128)(2,1)S(1)} %pack.4), channel_id=1, source_target_pairs={{0,2},{2,0},{1,3},{3,1},{4,6},{6,4},{5,7},{7,5},{8,10},{10,8},{9,1... | collective-permute-start | bytes 786440 | tf_op jit(solution)/shard_map/ppermute | solution.py:269
  9.3 0.5 collective-permute-start.1
  9.8 0.6 arrange.1.right
  10.4 1.1 %flip.1.left = bf16[1024,1024]{1,0:T(8,128)(2,1)S(1)} custom-call(bf16[1024,1024]{1,0:T(8,128)(2,1)S(1)} %bitcast.10), custom_call_target="tpu_custom_call" | custom-call | bytes 8388608 | tf_op jit(solution)/shard_map/flip/pallas_call | solution.py:145
  11.6 0.4 pack.5.here
  12.0 4.9 %collective-permute-done.3.high = bf16[32,16,256]{2,1,0:T(8,128)(2,1)S(1)} collective-permute-done((bf16[32,16,256]{2,1,0:T(8,128)(2,1)S(1)}, bf16[32,16,256]{2,1,0:T(8,128)(2,1)S(1)}, u32[]{:S(2)}, u32[]{:S(2)}) %collective-permute-start.3) | collective-permute-done | bytes 262176 | tf_op jit(solution)/shard_map/ppermute | solution.py:269
  16.9 4.8 %collective-permute-done.1.low = bf16[32,16,256]{2,1,0:T(8,128)(2,1)S(1)} collective-permute-done((bf16[32,16,256]{2,1,0:T(8,128)(2,1)S(1)}, bf16[32,16,256]{2,1,0:T(8,128)(2,1)S(1)}, u32[]{:S(2)}, u32[]{:S(2)}) %collective-permute-start.1) | collective-permute-done | bytes 262176 | tf_op jit(solution)/shard_map/ppermute | solution.py:266
  21.7 0.1 add.3
  21.8 29.7 %all_to_all.10 = bf16[64,16,256]{2,1,0:T(8,128)(2,1)S(1)} all-to-all(bf16[64,16,256]{2,1,0:T(8,128)(2,1)S(1)} %add.3), channel_id=1, replica_groups=mesh['z'=8,'y'=4,'x_lo'=2,'x_hi'=2,'core'=2] {'z','y','x_lo'}, dimensions={0} | all-to-all | bytes 1048576 | tf_op jit(solution)/shard_map/all_to_all | solution.py:254
  51.5 1.2 %term.2 = (bf16[2,512,256]{2,1,0:T(8,128)(2,1)S(1)}, f32[2,512,256]{2,1,0:T(8,128)S(1)}) custom-call(bf16[1024,1024]{1,0:T(8,128)(2,1)S(1)} %flip.1.left, bf16[1024,256]{1,0:T(8,128)(2,1)S(1)} %bitcast.16, bf16[4,256,256]{2,1,0:T(8,128)(2,1)S(1)} %arrange.1.right), custom_call_target="tpu_custom_call" | custom-call | flops 536870912 | bytes 1024 | tf_op jit(solution)/shard_map/term/pallas_call | solution.py:98
  52.8 0.1 collective-permute-start.5
  52.9 1.2 %term.3 = (bf16[2,512,256]{2,1,0:T(8,128)(2,1)S(1)}, f32[2,512,256]{2,1,0:T(8,128)S(1)}) custom-call(bf16[1024,1024]{1,0:T(8,128)(2,1)S(1)} %flip.1.left, bf16[1024,256]{1,0:T(8,128)(2,1)S(1)} %bitcast.17, bf16[4,256,256]{2,1,0:T(8,128)(2,1)S(1)} %arrange.1.right), custom_call_target="tpu_custom_call" | custom-call | flops 536870912 | bytes 1024 | tf_op jit(solution)/shard_map/term/pallas_call | solution.py:98
  54.1 0.6 collective-permute-start.7
  54.7 0.1 collective-permute-done.5.arrived
  54.8 0.1 chip_sum.2
  54.8 2.8 %collective-permute-start.6 = (bf16[512,256]{1,0:T(8,128)(2,1)S(1)}, bf16[512,256]{1,0:T(8,128)(2,1)S(1)}, u32[]{:S(2)}, u32[]{:S(2)}) collective-permute-start(bf16[512,256]{1,0:T(8,128)(2,1)S(1)} %get-tuple-element.53), channel_id=1, source_target_pairs={{0,2},{2,0},{1,3},{3,1},{4,6},{6,4},{5,7},{7,5},{8,10},{10,8},{9,1... | collective-permute-start | bytes 786440 | tf_op jit(solution)/shard_map/ppermute | solution.py:285
  57.7 0.1 chip_sum.3
  57.8 1.4 %collective-permute-start.8 = (bf16[512,256]{1,0:T(8,128)(2,1)S(1)}, bf16[512,256]{1,0:T(8,128)(2,1)S(1)}, u32[]{:S(2)}, u32[]{:S(2)}) collective-permute-start(bf16[512,256]{1,0:T(8,128)(2,1)S(1)} %get-tuple-element.56), channel_id=1, source_target_pairs={{0,2},{2,0},{1,3},{3,1},{4,6},{6,4},{5,7},{7,5},{8,10},{10,8},{9,1... | collective-permute-start | bytes 786440 | tf_op jit(solution)/shard_map/ppermute | solution.py:285
  59.1 6.4 %collective-permute-done.6.far = bf16[512,256]{1,0:T(8,128)(2,1)S(1)} collective-permute-done((bf16[512,256]{1,0:T(8,128)(2,1)S(1)}, bf16[512,256]{1,0:T(8,128)(2,1)S(1)}, u32[]{:S(2)}, u32[]{:S(2)}) %collective-permute-start.6) | collective-permute-done | bytes 262176 | tf_op jit(solution)/shard_map/ppermute | solution.py:285
  65.6 0.7 adam.2
  66.3 2.8 %collective-permute-start.11 = (bf16[512,256]{1,0:T(8,128)(2,1)S(1)}, bf16[512,256]{1,0:T(8,128)(2,1)S(1)}, u32[]{:S(2)}, u32[]{:S(2)}) collective-permute-start(bf16[512,256]{1,0:T(8,128)(2,1)S(1)} %get-tuple-element.64.own), channel_id=1, source_target_pairs={{0,2},{2,0},{1,3},{3,1},{4,6},{6,4},{5,7},{7,5},{8,10},{10,8},{9,1... | collective-permute-start | bytes 786440 | tf_op jit(solution)/shard_map/ppermute | solution.py:289
  69.1 2.1 %collective-permute-done.8.far = bf16[512,256]{1,0:T(8,128)(2,1)S(1)} collective-permute-done((bf16[512,256]{1,0:T(8,128)(2,1)S(1)}, bf16[512,256]{1,0:T(8,128)(2,1)S(1)}, u32[]{:S(2)}, u32[]{:S(2)}) %collective-permute-start.8) | collective-permute-done | bytes 262176 | tf_op jit(solution)/shard_map/ppermute | solution.py:285
  71.2 0.7 adam.3
  71.9 3.0 %collective-permute-start.9 = (bf16[512,256]{1,0:T(8,128)(2,1)S(1)}, bf16[512,256]{1,0:T(8,128)(2,1)S(1)}, u32[]{:S(2)}, u32[]{:S(2)}) collective-permute-start(bf16[512,256]{1,0:T(8,128)(2,1)S(1)} %get-tuple-element.71.own), channel_id=1, source_target_pairs={{0,2},{2,0},{1,3},{3,1},{4,6},{6,4},{5,7},{7,5},{8,10},{10,8},{9,1... | collective-permute-start | bytes 786440 | tf_op jit(solution)/shard_map/ppermute | solution.py:292
  74.9 1.6 %moments.1 = (f32[1,1024,256]{2,1,0:T(8,128)}, f32[1,1024,256]{2,1,0:T(8,128)}) custom-call(f32[512,256]{1,0:T(8,128)S(1)} %get-tuple-element.65.rotated0, f32[512,256]{1,0:T(8,128)S(1)} %get-tuple-element.66.rotated1, f32[1,1024,256]{2,1,0:T(8,128)S(1)} %copy-done.1, f32[1,1024,256]{2,1,0:T(8,128)S(1)} %copy-done.2), custom_call_target="tpu_custom_call" | custom-call | bytes 1024 | tf_op jit(solution)/shard_map/moments/pallas_call | solution.py:98
  76.5 0.6 collective-permute-done.11.far
  77.2 0.1 collective-permute-start.12
  77.3 0.5 collective-permute-start.13
  77.7 0.1 collective-permute-start.14
  77.9 0.7 collective-permute-done.12.rest_0_
  78.6 0.2 collective-permute-done.13.rest_1_
  78.8 0.5 turn.2.turned0
  79.3 2.4 %collective-permute-done.9.far = bf16[512,256]{1,0:T(8,128)(2,1)S(1)} collective-permute-done((bf16[512,256]{1,0:T(8,128)(2,1)S(1)}, bf16[512,256]{1,0:T(8,128)(2,1)S(1)}, u32[]{:S(2)}, u32[]{:S(2)}) %collective-permute-start.9) | collective-permute-done | bytes 262176 | tf_op jit(solution)/shard_map/ppermute | solution.py:292
  81.6 1.5 %collective-permute-done.15.rest_0_ = bf16[512,256]{1,0:T(8,128)(2,1)S(1)} collective-permute-done((bf16[512,256]{1,0:T(8,128)(2,1)S(1)}, bf16[512,256]{1,0:T(8,128)(2,1)S(1)}, u32[]{:S(2)}, u32[]{:S(2)}) %collective-permute-start.15) | collective-permute-done | bytes 262176 | tf_op jit(solution)/shard_map/ppermute | solution.py:299
  83.2 0.5 turn.3.turned1
  83.7 0.7 update.1
  84.4 23.5 %all_to_all.11.pieces = bf16[64,16,256]{2,1,0:T(8,128)(2,1)S(1)} all-to-all(bf16[64,16,256]{2,1,0:T(8,128)(2,1)S(1)} %update.1), channel_id=1, replica_groups=mesh['z'=8,'y'=4,'x_lo'=2,'x_hi'=2,'core'=2] {'z','y','x_lo'}, dimensions={0} | all-to-all | bytes 1048576 | tf_op jit(solution)/shard_map/all_to_all | solution.py:254
  107.9 1.3 %apply.1 = f32[16,64,256]{2,1,0:T(8,128)} custom-call(bf16[256,256]{1,0:T(8,128)(2,1)S(1)} %copy-done.5, bf16[64,16,256]{2,1,0:T(8,128)(2,1)S(1)} %all_to_all.11.pieces, f32[16,64,256]{2,1,0:T(8,128)S(1)} %copy-done.6), custom_call_target="tpu_custom_call" | custom-call | bytes 1024 | tf_op jit(solution)/shard_map/apply/pallas_call | solution.py:98
  (20 shorter events, 0.1 us)
Async XLA Ops:
  0.7 1.6 %copy-start = (bf16[1,16,64,1024]{3,2,1,0:T(8,128)(2,1)S(1)}, bf16[1,16,64,1024]{3,2,1,0:T(8,128)(2,1)}, u32[]{:S(2)}) copy-start(bf16[1,16,64,1024]{3,2,1,0:T(8,128)(2,1)} %param.10) | copy-start | bytes 6291460
  2.3 2.5 %copy-start.5 = (bf16[256,256]{1,0:T(8,128)(2,1)S(1)}, bf16[256,256]{1,0:T(8,128)(2,1)}, u32[]{:S(2)}) copy-start(bf16[256,256]{1,0:T(8,128)(2,1)} %constant.8.clone.swap_ref) | copy-start | bytes 393220
  3.1 6.7 %copy-start.4 = (bf16[1,256,1024]{2,1,0:T(8,128)(2,1)S(1)}, bf16[1,256,1024]{2,1,0:T(8,128)(2,1)}, u32[]{:S(2)}) copy-start(bf16[1,256,1024]{2,1,0:T(8,128)(2,1)} %param.15) | copy-start | bytes 1572868
  3.1 1.6 %collective-permute-start = (bf16[16,32,256]{2,1,0:T(8,128)(2,1)S(1)}, bf16[16,32,256]{2,1,0:T(8,128)(2,1)S(1)}, u32[]{:S(2)}, u32[]{:S(2)}) collective-permute-start(bf16[16,32,256]{2,1,0:T(8,128)(2,1)S(1)} %get-tuple-element.40), channel_id=1, source_target_pairs={{0,1},{1,0},{2,3},{3,2},{4,5},{5,4},{6,7},{7,6},{8,9},{9,8},{10,11... | collective-permute-start | bytes 786440 | tf_op jit(solution)/shard_map/ppermute | solution.py:264
  3.2 8.3 %collective-permute-start.4 = (bf16[16,64,256]{2,1,0:T(8,128)(2,1)S(1)}, bf16[16,64,256]{2,1,0:T(8,128)(2,1)S(1)}, u32[]{:S(2)}, u32[]{:S(2)}) collective-permute-start(bf16[16,64,256]{2,1,0:T(8,128)(2,1)S(1)} %get-tuple-element.44), channel_id=1, source_target_pairs={{0,1},{1,0},{2,3},{3,2},{4,5},{5,4},{6,7},{7,6},{8,9},{9,8},{10,11... | collective-permute-start | bytes 1572872 | tf_op jit(solution)/shard_map/ppermute | solution.py:264
  3.7 2.1 %collective-permute-start.2 = (bf16[16,32,256]{2,1,0:T(8,128)(2,1)S(1)}, bf16[16,32,256]{2,1,0:T(8,128)(2,1)S(1)}, u32[]{:S(2)}, u32[]{:S(2)}) collective-permute-start(bf16[16,32,256]{2,1,0:T(8,128)(2,1)S(1)} %get-tuple-element.41), channel_id=1, source_target_pairs={{0,1},{1,0},{2,3},{3,2},{4,5},{5,4},{6,7},{7,6},{8,9},{9,8},{10,11... | collective-permute-start | bytes 786440 | tf_op jit(solution)/shard_map/ppermute | solution.py:264
  5.1 5.4 %copy-start.3 = (bf16[1,1024,1024]{2,1,0:T(8,128)(2,1)S(1)}, bf16[1,1024,1024]{2,1,0:T(8,128)(2,1)}, u32[]{:S(2)}) copy-start(bf16[1,1024,1024]{2,1,0:T(8,128)(2,1)} %param.14) | copy-start | bytes 6291460
  6.2 10.7 %collective-permute-start.3 = (bf16[32,16,256]{2,1,0:T(8,128)(2,1)S(1)}, bf16[32,16,256]{2,1,0:T(8,128)(2,1)S(1)}, u32[]{:S(2)}, u32[]{:S(2)}) collective-permute-start(bf16[32,16,256]{2,1,0:T(8,128)(2,1)S(1)} %pack.4), channel_id=1, source_target_pairs={{0,2},{2,0},{1,3},{3,1},{4,6},{6,4},{5,7},{7,5},{8,10},{10,8},{9,1... | collective-permute-start | bytes 786440 | tf_op jit(solution)/shard_map/ppermute | solution.py:269
  9.3 12.4 %collective-permute-start.1 = (bf16[32,16,256]{2,1,0:T(8,128)(2,1)S(1)}, bf16[32,16,256]{2,1,0:T(8,128)(2,1)S(1)}, u32[]{:S(2)}, u32[]{:S(2)}) collective-permute-start(bf16[32,16,256]{2,1,0:T(8,128)(2,1)S(1)} %pack.3), channel_id=1, source_target_pairs={{0,2},{2,0},{1,3},{3,1},{4,6},{6,4},{5,7},{7,5},{8,10},{10,8},{9,1... | collective-permute-start | bytes 786440 | tf_op jit(solution)/shard_map/ppermute | solution.py:266
  52.8 2.0 %collective-permute-start.5 = (bf16[2,512,256]{2,1,0:T(8,128)(2,1)S(1)}, bf16[2,512,256]{2,1,0:T(8,128)(2,1)S(1)}, u32[]{:S(2)}, u32[]{:S(2)}) collective-permute-start(bf16[2,512,256]{2,1,0:T(8,128)(2,1)S(1)} %get-tuple-element.52), channel_id=1, source_target_pairs={{0,1},{1,0},{2,3},{3,2},{4,5},{5,4},{6,7},{7,6},{8,9},{9,8},{10,11... | collective-permute-start | bytes 1572872 | tf_op jit(solution)/shard_map/ppermute | solution.py:282
  54.1 11.5 %copy-start.1 = (f32[1,1024,256]{2,1,0:T(8,128)S(1)}, f32[1,1024,256]{2,1,0:T(8,128)}, u32[]{:S(2)}) copy-start(f32[1,1024,256]{2,1,0:T(8,128)} %m1.5) | copy-start | bytes 3145732
  54.1 11.5 %copy-start.2 = (f32[1,1024,256]{2,1,0:T(8,128)S(1)}, f32[1,1024,256]{2,1,0:T(8,128)}, u32[]{:S(2)}) copy-start(f32[1,1024,256]{2,1,0:T(8,128)} %m2.5) | copy-start | bytes 3145732
  54.1 3.6 %collective-permute-start.7 = (bf16[2,512,256]{2,1,0:T(8,128)(2,1)S(1)}, bf16[2,512,256]{2,1,0:T(8,128)(2,1)S(1)}, u32[]{:S(2)}, u32[]{:S(2)}) collective-permute-start(bf16[2,512,256]{2,1,0:T(8,128)(2,1)S(1)} %get-tuple-element.55), channel_id=1, source_target_pairs={{0,1},{1,0},{2,3},{3,2},{4,5},{5,4},{6,7},{7,6},{8,9},{9,8},{10,11... | collective-permute-start | bytes 1572872 | tf_op jit(solution)/shard_map/ppermute | solution.py:282
  54.8 10.7 %collective-permute-start.6 = (bf16[512,256]{1,0:T(8,128)(2,1)S(1)}, bf16[512,256]{1,0:T(8,128)(2,1)S(1)}, u32[]{:S(2)}, u32[]{:S(2)}) collective-permute-start(bf16[512,256]{1,0:T(8,128)(2,1)S(1)} %get-tuple-element.53), channel_id=1, source_target_pairs={{0,2},{2,0},{1,3},{3,1},{4,6},{6,4},{5,7},{7,5},{8,10},{10,8},{9,1... | collective-permute-start | bytes 786440 | tf_op jit(solution)/shard_map/ppermute | solution.py:285
  57.8 13.4 %collective-permute-start.8 = (bf16[512,256]{1,0:T(8,128)(2,1)S(1)}, bf16[512,256]{1,0:T(8,128)(2,1)S(1)}, u32[]{:S(2)}, u32[]{:S(2)}) collective-permute-start(bf16[512,256]{1,0:T(8,128)(2,1)S(1)} %get-tuple-element.56), channel_id=1, source_target_pairs={{0,2},{2,0},{1,3},{3,1},{4,6},{6,4},{5,7},{7,5},{8,10},{10,8},{9,1... | collective-permute-start | bytes 786440 | tf_op jit(solution)/shard_map/ppermute | solution.py:285
  66.3 10.8 %collective-permute-start.11 = (bf16[512,256]{1,0:T(8,128)(2,1)S(1)}, bf16[512,256]{1,0:T(8,128)(2,1)S(1)}, u32[]{:S(2)}, u32[]{:S(2)}) collective-permute-start(bf16[512,256]{1,0:T(8,128)(2,1)S(1)} %get-tuple-element.64.own), channel_id=1, source_target_pairs={{0,2},{2,0},{1,3},{3,1},{4,6},{6,4},{5,7},{7,5},{8,10},{10,8},{9,1... | collective-permute-start | bytes 786440 | tf_op jit(solution)/shard_map/ppermute | solution.py:289
  69.1 8.7 %collective-permute-start.10 = (bf16[512,256]{1,0:T(8,128)(2,1)S(1)}, bf16[512,256]{1,0:T(8,128)(2,1)S(1)}, u32[]{:S(2)}, u32[]{:S(2)}) collective-permute-start(bf16[512,256]{1,0:T(8,128)(2,1)S(1)} %get-tuple-element.64.own), channel_id=1, source_target_pairs={{0,1},{1,0},{2,3},{3,2},{4,5},{5,4},{6,7},{7,6},{8,9},{9,8},{10,11... | collective-permute-start | bytes 786440 | tf_op jit(solution)/shard_map/ppermute | solution.py:289
  71.9 9.7 %collective-permute-start.9 = (bf16[512,256]{1,0:T(8,128)(2,1)S(1)}, bf16[512,256]{1,0:T(8,128)(2,1)S(1)}, u32[]{:S(2)}, u32[]{:S(2)}) collective-permute-start(bf16[512,256]{1,0:T(8,128)(2,1)S(1)} %get-tuple-element.71.own), channel_id=1, source_target_pairs={{0,2},{2,0},{1,3},{3,1},{4,6},{6,4},{5,7},{7,5},{8,10},{10,8},{9,1... | collective-permute-start | bytes 786440 | tf_op jit(solution)/shard_map/ppermute | solution.py:292
  77.2 1.4 %collective-permute-start.12 = (bf16[256,256]{1,0:T(8,128)(2,1)S(1)}, bf16[256,256]{1,0:T(8,128)(2,1)S(1)}, u32[]{:S(2)}, u32[]{:S(2)}) collective-permute-start(bf16[256,256]{1,0:T(8,128)(2,1)S(1)} %get-tuple-element.76), channel_id=1, source_target_pairs={{0,1},{1,0},{2,3},{3,2},{4,5},{5,4},{6,7},{7,6},{8,9},{9,8},{10,11... | collective-permute-start | bytes 393224 | tf_op jit(solution)/shard_map/ppermute | solution.py:296
  77.3 1.5 %collective-permute-start.13 = (bf16[256,256]{1,0:T(8,128)(2,1)S(1)}, bf16[256,256]{1,0:T(8,128)(2,1)S(1)}, u32[]{:S(2)}, u32[]{:S(2)}) collective-permute-start(bf16[256,256]{1,0:T(8,128)(2,1)S(1)} %get-tuple-element.75), channel_id=1, source_target_pairs={{0,1},{1,0},{2,3},{3,2},{4,5},{5,4},{6,7},{7,6},{8,9},{9,8},{10,11... | collective-permute-start | bytes 393224 | tf_op jit(solution)/shard_map/ppermute | solution.py:296
  77.7 3.9 %collective-permute-start.14 = (bf16[512,256]{1,0:T(8,128)(2,1)S(1)}, bf16[512,256]{1,0:T(8,128)(2,1)S(1)}, u32[]{:S(2)}, u32[]{:S(2)}) collective-permute-start(bf16[512,256]{1,0:T(8,128)(2,1)S(1)} %get-tuple-element.71.own), channel_id=1, source_target_pairs={{0,1},{1,0},{2,3},{3,2},{4,5},{5,4},{6,7},{7,6},{8,9},{9,8},{10,11... | collective-permute-start | bytes 786440 | tf_op jit(solution)/shard_map/ppermute | solution.py:292
  81.6 1.5 %collective-permute-start.15 = (bf16[512,256]{1,0:T(8,128)(2,1)S(1)}, bf16[512,256]{1,0:T(8,128)(2,1)S(1)}, u32[]{:S(2)}, u32[]{:S(2)}) collective-permute-start(bf16[512,256]{1,0:T(8,128)(2,1)S(1)} %collective-permute-done.9.far), channel_id=1, source_target_pairs={{0,1},{1,0},{2,3},{3,2},{4,5},{5,4},{6,7},{7,6},{8,9},{9,8},{10,11... | collective-permute-start | bytes 786440 | tf_op jit(solution)/shard_map/ppermute | solution.py:299
  83.6 24.2 %copy-start.6 = (f32[16,64,256]{2,1,0:T(8,128)S(1)}, f32[16,64,256]{2,1,0:T(8,128)}, u32[]{:S(2)}) copy-start(f32[16,64,256]{2,1,0:T(8,128)} %weights.1) | copy-start | bytes 3145732

commit v7 on v5

--- a/solution.py
+++ b/solution.py
@@ -172,36 +172,36 @@
     return whole(chip_kernel, [shape(size, Q), shape(size, Q, kind=F32)], kept, arrived, name="chip_sum")
 
 
-def adam_kernel(part, own, far, m1, m2, *rest):
-    first, second, direction = rest[-3:]
+def moments_of(rotated, m1, m2):
+    return 0.9 * m1 + 0.1 * rotated, 0.95 * m2 + 0.05 * rotated * rotated
+
+
+def adam_kernel(part, own, far, m1, m2, rotated, direction):
     size = own.shape[0]
     rows = slice(part * size, (part + 1) * size)
-    rotated = own[...] + far[...].astype(F32)
-    new1 = 0.9 * m1[0, rows] + 0.1 * rotated
-    new2 = 0.95 * m2[0, rows] + 0.05 * rotated * rotated
-    first[0] = new1
-    second[0] = new2
+    rotated[...] = own[...] + far[...].astype(F32)
+    new1, new2 = moments_of(rotated[...], m1[0, rows], m2[0, rows])
     bias_first = 1.0 - 0.9**10
     bias_second = 1.0 - 0.95**10
     direction[...] = (new1 / bias_first / (jnp.sqrt(new2 / bias_second) + 1e-08)).astype(BF16)
 
 
-def adam(part, own, far, moments, done):
-    size = BS // PARTS
-    rows = pl.BlockSpec((size, Q), lambda i: (0, 0))
-    old = pl.BlockSpec((1, BS, Q), lambda i: (0, 0, 0))
-    new = pl.BlockSpec((1, size, Q), lambda i: (0, part, 0))
-    return pl.pallas_call(
-        functools.partial(adam_kernel, part),
-        grid=(1,),
-        in_specs=[rows] * 2 + [old] * 2 + [pl.BlockSpec(memory_space=pl.ANY)] * len(done),
-        out_specs=[new, new, rows],
-        out_shape=[shape(1, BS, Q, kind=F32), shape(1, BS, Q, kind=F32), shape(size, Q)],
-        input_output_aliases={4 + n: n for n in range(len(done))},
-        compiler_params=PARAMS,
-        cost_estimate=cost(1 << 10, 1 << 10),
-        name="adam",
-    )(own, far, *moments, *done)
+def adam(part, own, far, moments):
+    size = BS // PARTS
+    kernel = functools.partial(adam_kernel, part)
+    return whole(kernel, [shape(size, Q, kind=F32), shape(size, Q)], own, far, *moments, name="adam")
+
+
+def moments_kernel(rotated0, rotated1, m1, m2, first, second):
+    size = BS // PARTS
+    for part, rotated in enumerate((rotated0, rotated1)):
+        rows = slice(part * size, (part + 1) * size)
+        first[0, rows], second[0, rows] = moments_of(rotated[...], m1[0, rows], m2[0, rows])
+
+
+def new_moments(rotated, moments):
+    outs = [shape(1, BS, Q, kind=F32)] * 2
+    return whole(moments_kernel, outs, *rotated, *moments, name="moments")
 
 
 def turn_kernel(own, near, far, right, *rest):
@@ -272,19 +272,20 @@
     arrived = [lax.ppermute(send, "x_hi", SWAP) for send, _ in sums]
     arrived[0], sums[1] = lax.optimization_barrier((arrived[0], sums[1]))
     moments = (moment_first, moment_second)
-    *done, own0 = adam(0, sums[0][1], arrived[0], moments, ())
+    rotated0, own0 = adam(0, sums[0][1], arrived[0], moments)
     far0, near0 = lax.ppermute(own0, "x_hi", SWAP), lax.ppermute(own0, "core", SWAP)
     arrived[1], own0 = lax.optimization_barrier((arrived[1], own0))
-    *done, own1 = adam(1, sums[1][1], arrived[1], moments, done)
+    rotated1, own1 = adam(1, sums[1][1], arrived[1], moments)
     far1, near1 = lax.ppermute(own1, "x_hi", SWAP), lax.ppermute(own1, "core", SWAP)
-    far0, own1 = lax.optimization_barrier((far0, own1))
+    first_new, second_new = new_moments((rotated0, rotated1), moments)
+    far0, own1, first_new, second_new = lax.optimization_barrier((far0, own1, first_new, second_new))
     quarter = BS // PARTS // 2
     cross0 = [lax.ppermute(far0[n * quarter : (n + 1) * quarter], "core", SWAP) for n in range(2)]
     turned0 = turn(own0, near0, far0, cross0, right)
     far1, turned0 = lax.optimization_barrier((far1, turned0))
     turned1 = turn(own1, near1, far1, [lax.ppermute(far1, "core", SWAP)], right)
 
-    return (apply(exchange(update(left, turned0, turned1)), weights), *done)
+    return (apply(exchange(update(left, turned0, turned1)), weights), first_new, second_new)
 
 
 def solution(mesh):

time: 109 us -> 109 us (level)
    pallas_call x11 -> x14, Pallas kernels: 6.47 us -> 9.46 us  [whole(): pl.pallas_call(kernel, grid=(1,), in_specs=[spec(value) for value in args...]
    pallas_call x2 -> x0, Pallas kernels: 2.37 us -> none  [adam(): pl.pallas_call(functools.partial(adam_kernel, part), grid=(1,), in_specs=...]
  transfers between devices with their start and end apart: 14 -> 14, of which waited for: 10 -> 10; matrix products, arithmetic and copies ran while one was open for 0% -> 0% of each run, Pallas kernels for 6% -> 7%
where the time goes in v7:
time: 109 us
  blocking collectives  53.2 us (49%)
  waiting for transfers between devices  25.7 us (24%)
  starting transfers between devices  15.1 us (14%)
  Pallas kernels  12 us (11%)
  local copies, waits for them, and re-layouts  1.64 us (2%)
    all_to_all x2, blocking collectives, exchange(): return lax.all_to_all(pieces, FSDP, split_axis=0, concat_axis=0, tiled=True)  53.2 us
    ppermute x1, waiting for transfers between devices, local(): there = lax.ppermute(far, 'x_hi', SWAP)  10.2 us
    pallas_call x14, Pallas kernels, whole(): pl.pallas_call(kernel, grid=(1,), in_specs=[spec(value) for value in args...  9.46 us
    ppermute x2, waiting for transfers between devices, local(): arrived = [lax.ppermute(send, 'x_hi', SWAP) for send, _ in sums]  8.54 us
    ppermute x2, starting transfers between devices, local(): arrived = [lax.ppermute(send, 'x_hi', SWAP) for send, _ in sums]  4.2 us
    ppermute x1, starting transfers between devices, local(): there = lax.ppermute(far, 'x_hi', SWAP)  3.11 us
    ppermute x1, starting transfers between devices, local(): lax.ppermute(own0, 'x_hi', SWAP)  2.81 us
    ppermute x1, starting transfers between devices, local(): lax.ppermute(own1, 'x_hi', SWAP)  2.81 us
  transfers between devices with their start and end apart: 14, of which 10 were waited for; matrix products, arithmetic and copies ran while one was open for 0% of the time, Pallas kernels for 7%

profile of v7, /device:TPU:32, one launch (start us, length us, event | category | flops | bytes accessed | tf_op | source)
XLA Modules:
  0.0 108.5 jit_solution(2375778332109157137)
XLA Ops:
  0.6 0.1 pad_add_fusion.at
  0.7 1.6 %copy-done = bf16[1,16,64,1024]{3,2,1,0:T(8,128)(2,1)S(1)} copy-done((bf16[1,16,64,1024]{3,2,1,0:T(8,128)(2,1)S(1)}, bf16[1,16,64,1024]{3,2,1,0:T(8,128)(2,1)}, u32[]{:S(2)}) %copy-start) | copy-done | bytes 2097176
  2.3 0.8 split.1
  3.1 0.1 collective-permute-start
  3.2 0.5 collective-permute-start.2
  3.7 1.4 %collective-permute-done.arrived = bf16[16,64,256]{2,1,0:T(8,128)(2,1)S(1)} collective-permute-done((bf16[16,64,256]{2,1,0:T(8,128)(2,1)S(1)}, bf16[16,64,256]{2,1,0:T(8,128)(2,1)S(1)}, u32[]{:S(2)}, u32[]{:S(2)}) %collective-permute-start) | collective-permute-done | bytes 524320 | tf_op jit(solution)/shard_map/ppermute | solution.py:257
  5.1 0.4 pack.2
  5.6 3.1 %collective-permute-start.1 = (bf16[64,16,256]{2,1,0:T(8,128)(2,1)S(1)}, bf16[64,16,256]{2,1,0:T(8,128)(2,1)S(1)}, u32[]{:S(2)}, u32[]{:S(2)}) collective-permute-start(bf16[64,16,256]{2,1,0:T(8,128)(2,1)S(1)} %pack.2), channel_id=1, source_target_pairs={{0,2},{2,0},{1,3},{3,1},{4,6},{6,4},{5,7},{7,5},{8,10},{10,8},{9,1... | collective-permute-start | bytes 1572872 | tf_op jit(solution)/shard_map/ppermute | solution.py:258
  8.7 0.6 arrange.1.right
  9.3 1.1 %flip.1.left = bf16[1024,1024]{1,0:T(8,128)(2,1)S(1)} custom-call(bf16[1024,1024]{1,0:T(8,128)(2,1)S(1)} %bitcast.10), custom_call_target="tpu_custom_call" | custom-call | bytes 8388608 | tf_op jit(solution)/shard_map/flip/pallas_call | solution.py:137
  10.5 0.4 pack.3.here
  10.9 10.2 %collective-permute-done.1.there = bf16[64,16,256]{2,1,0:T(8,128)(2,1)S(1)} collective-permute-done((bf16[64,16,256]{2,1,0:T(8,128)(2,1)S(1)}, bf16[64,16,256]{2,1,0:T(8,128)(2,1)S(1)}, u32[]{:S(2)}, u32[]{:S(2)}) %collective-permute-start.1) | collective-permute-done | bytes 524320 | tf_op jit(solution)/shard_map/ppermute | solution.py:258
  21.1 0.1 add.3
  21.2 29.7 %all_to_all.10 = bf16[64,16,256]{2,1,0:T(8,128)(2,1)S(1)} all-to-all(bf16[64,16,256]{2,1,0:T(8,128)(2,1)S(1)} %add.3), channel_id=1, replica_groups=mesh['z'=8,'y'=4,'x_lo'=2,'x_hi'=2,'core'=2] {'z','y','x_lo'}, dimensions={0} | all-to-all | bytes 1048576 | tf_op jit(solution)/shard_map/all_to_all | solution.py:246
  50.9 1.2 %term.2 = (bf16[2,512,256]{2,1,0:T(8,128)(2,1)S(1)}, f32[2,512,256]{2,1,0:T(8,128)S(1)}) custom-call(bf16[1024,1024]{1,0:T(8,128)(2,1)S(1)} %flip.1.left, bf16[1024,256]{1,0:T(8,128)(2,1)S(1)} %bitcast.16, bf16[4,256,256]{2,1,0:T(8,128)(2,1)S(1)} %arrange.1.right), custom_call_target="tpu_custom_call" | custom-call | flops 536870912 | bytes 1024 | tf_op jit(solution)/shard_map/term/pallas_call | solution.py:94
  52.1 0.1 collective-permute-start.3
  52.2 1.2 %term.3 = (bf16[2,512,256]{2,1,0:T(8,128)(2,1)S(1)}, f32[2,512,256]{2,1,0:T(8,128)S(1)}) custom-call(bf16[1024,1024]{1,0:T(8,128)(2,1)S(1)} %flip.1.left, bf16[1024,256]{1,0:T(8,128)(2,1)S(1)} %bitcast.17, bf16[4,256,256]{2,1,0:T(8,128)(2,1)S(1)} %arrange.1.right), custom_call_target="tpu_custom_call" | custom-call | flops 536870912 | bytes 1024 | tf_op jit(solution)/shard_map/term/pallas_call | solution.py:94
  53.5 0.0 copy-start.1
  53.5 0.0 copy-start.2
  53.5 0.6 collective-permute-start.5
  54.1 0.1 collective-permute-done.3.arrived
  54.1 0.1 chip_sum.2
  54.2 2.8 %collective-permute-start.4 = (bf16[512,256]{1,0:T(8,128)(2,1)S(1)}, bf16[512,256]{1,0:T(8,128)(2,1)S(1)}, u32[]{:S(2)}, u32[]{:S(2)}) collective-permute-start(bf16[512,256]{1,0:T(8,128)(2,1)S(1)} %get-tuple-element.47), channel_id=1, source_target_pairs={{0,2},{2,0},{1,3},{3,1},{4,6},{6,4},{5,7},{7,5},{8,10},{10,8},{9,1... | collective-permute-start | bytes 786440 | tf_op jit(solution)/shard_map/ppermute | solution.py:272
  57.0 0.0 collective-permute-done.5.arrived
  57.0 0.1 chip_sum.3
  57.1 1.4 %collective-permute-start.6 = (bf16[512,256]{1,0:T(8,128)(2,1)S(1)}, bf16[512,256]{1,0:T(8,128)(2,1)S(1)}, u32[]{:S(2)}, u32[]{:S(2)}) collective-permute-start(bf16[512,256]{1,0:T(8,128)(2,1)S(1)} %get-tuple-element.50), channel_id=1, source_target_pairs={{0,2},{2,0},{1,3},{3,1},{4,6},{6,4},{5,7},{7,5},{8,10},{10,8},{9,1... | collective-permute-start | bytes 786440 | tf_op jit(solution)/shard_map/ppermute | solution.py:272
  58.5 6.4 %collective-permute-done.4.far = bf16[512,256]{1,0:T(8,128)(2,1)S(1)} collective-permute-done((bf16[512,256]{1,0:T(8,128)(2,1)S(1)}, bf16[512,256]{1,0:T(8,128)(2,1)S(1)}, u32[]{:S(2)}, u32[]{:S(2)}) %collective-permute-start.4) | collective-permute-done | bytes 262176 | tf_op jit(solution)/shard_map/ppermute | solution.py:272
  65.0 0.7 adam.2
  65.7 2.8 %collective-permute-start.9 = (bf16[512,256]{1,0:T(8,128)(2,1)S(1)}, bf16[512,256]{1,0:T(8,128)(2,1)S(1)}, u32[]{:S(2)}, u32[]{:S(2)}) collective-permute-start(bf16[512,256]{1,0:T(8,128)(2,1)S(1)} %get-tuple-element.58.own), channel_id=1, source_target_pairs={{0,2},{2,0},{1,3},{3,1},{4,6},{6,4},{5,7},{7,5},{8,10},{10,8},{9,1... | collective-permute-start | bytes 786440 | tf_op jit(solution)/shard_map/ppermute | solution.py:276
  68.5 2.1 %collective-permute-done.6.far = bf16[512,256]{1,0:T(8,128)(2,1)S(1)} collective-permute-done((bf16[512,256]{1,0:T(8,128)(2,1)S(1)}, bf16[512,256]{1,0:T(8,128)(2,1)S(1)}, u32[]{:S(2)}, u32[]{:S(2)}) %collective-permute-start.6) | collective-permute-done | bytes 262176 | tf_op jit(solution)/shard_map/ppermute | solution.py:272
  70.6 0.7 adam.3
  71.3 2.8 %collective-permute-start.7 = (bf16[512,256]{1,0:T(8,128)(2,1)S(1)}, bf16[512,256]{1,0:T(8,128)(2,1)S(1)}, u32[]{:S(2)}, u32[]{:S(2)}) collective-permute-start(bf16[512,256]{1,0:T(8,128)(2,1)S(1)} %get-tuple-element.65.own), channel_id=1, source_target_pairs={{0,2},{2,0},{1,3},{3,1},{4,6},{6,4},{5,7},{7,5},{8,10},{10,8},{9,1... | collective-permute-start | bytes 786440 | tf_op jit(solution)/shard_map/ppermute | solution.py:279
  74.1 1.6 %moments.1 = (f32[1,1024,256]{2,1,0:T(8,128)}, f32[1,1024,256]{2,1,0:T(8,128)}) custom-call(f32[512,256]{1,0:T(8,128)S(1)} %get-tuple-element.59.rotated0, f32[512,256]{1,0:T(8,128)S(1)} %get-tuple-element.60.rotated1, f32[1,1024,256]{2,1,0:T(8,128)S(1)} %copy-done.1, f32[1,1024,256]{2,1,0:T(8,128)S(1)} %copy-done.2), custom_call_target="tpu_custom_call" | custom-call | bytes 1024 | tf_op jit(solution)/shard_map/moments/pallas_call | solution.py:94
  75.7 0.8 collective-permute-done.9.far
  76.5 0.3 collective-permute-start.10
  76.8 0.5 collective-permute-start.11
  77.3 0.1 collective-permute-start.12
  77.4 0.0 collective-permute-done.8.near
  77.4 0.7 collective-permute-done.10.rest_0_
  78.2 0.2 collective-permute-done.11.rest_1_
  78.3 0.5 turn.2.turned0
  78.8 2.2 %collective-permute-done.7.far = bf16[512,256]{1,0:T(8,128)(2,1)S(1)} collective-permute-done((bf16[512,256]{1,0:T(8,128)(2,1)S(1)}, bf16[512,256]{1,0:T(8,128)(2,1)S(1)}, u32[]{:S(2)}, u32[]{:S(2)}) %collective-permute-start.7) | collective-permute-done | bytes 262176 | tf_op jit(solution)/shard_map/ppermute | solution.py:279
  81.0 1.5 %collective-permute-done.13.rest_0_ = bf16[512,256]{1,0:T(8,128)(2,1)S(1)} collective-permute-done((bf16[512,256]{1,0:T(8,128)(2,1)S(1)}, bf16[512,256]{1,0:T(8,128)(2,1)S(1)}, u32[]{:S(2)}, u32[]{:S(2)}) %collective-permute-start.13) | collective-permute-done | bytes 262176 | tf_op jit(solution)/shard_map/ppermute | solution.py:286
  82.6 0.5 turn.3.turned1
  83.0 0.0 copy-start.6
  83.0 0.7 update.1
  83.8 23.5 %all_to_all.11.pieces = bf16[64,16,256]{2,1,0:T(8,128)(2,1)S(1)} all-to-all(bf16[64,16,256]{2,1,0:T(8,128)(2,1)S(1)} %update.1), channel_id=1, replica_groups=mesh['z'=8,'y'=4,'x_lo'=2,'x_hi'=2,'core'=2] {'z','y','x_lo'}, dimensions={0} | all-to-all | bytes 1048576 | tf_op jit(solution)/shard_map/all_to_all | solution.py:246
  107.3 1.3 %apply.1 = f32[16,64,256]{2,1,0:T(8,128)} custom-call(bf16[256,256]{1,0:T(8,128)(2,1)S(1)} %copy-done.5, bf16[64,16,256]{2,1,0:T(8,128)(2,1)S(1)} %all_to_all.11.pieces, f32[16,64,256]{2,1,0:T(8,128)S(1)} %copy-done.6), custom_call_target="tpu_custom_call" | custom-call | bytes 1024 | tf_op jit(solution)/shard_map/apply/pallas_call | solution.py:94
  (15 shorter events, 0.0 us)
Async XLA Ops:
  0.7 1.6 %copy-start = (bf16[1,16,64,1024]{3,2,1,0:T(8,128)(2,1)S(1)}, bf16[1,16,64,1024]{3,2,1,0:T(8,128)(2,1)}, u32[]{:S(2)}) copy-start(bf16[1,16,64,1024]{3,2,1,0:T(8,128)(2,1)} %param.9) | copy-start | bytes 6291460
  2.3 2.8 %copy-start.5 = (bf16[256,256]{1,0:T(8,128)(2,1)S(1)}, bf16[256,256]{1,0:T(8,128)(2,1)}, u32[]{:S(2)}) copy-start(bf16[256,256]{1,0:T(8,128)(2,1)} %constant.8.clone.swap_ref) | copy-start | bytes 393220
  2.3 6.4 %copy-start.4 = (bf16[1,256,1024]{2,1,0:T(8,128)(2,1)S(1)}, bf16[1,256,1024]{2,1,0:T(8,128)(2,1)}, u32[]{:S(2)}) copy-start(bf16[1,256,1024]{2,1,0:T(8,128)(2,1)} %param.14) | copy-start | bytes 1572868
  3.1 2.0 %collective-permute-start = (bf16[16,64,256]{2,1,0:T(8,128)(2,1)S(1)}, bf16[16,64,256]{2,1,0:T(8,128)(2,1)S(1)}, u32[]{:S(2)}, u32[]{:S(2)}) collective-permute-start(bf16[16,64,256]{2,1,0:T(8,128)(2,1)S(1)} %get-tuple-element.37), channel_id=1, source_target_pairs={{0,1},{1,0},{2,3},{3,2},{4,5},{5,4},{6,7},{7,6},{8,9},{9,8},{10,11... | collective-permute-start | bytes 1572872 | tf_op jit(solution)/shard_map/ppermute | solution.py:257
  3.2 7.2 %collective-permute-start.2 = (bf16[16,64,256]{2,1,0:T(8,128)(2,1)S(1)}, bf16[16,64,256]{2,1,0:T(8,128)(2,1)S(1)}, u32[]{:S(2)}, u32[]{:S(2)}) collective-permute-start(bf16[16,64,256]{2,1,0:T(8,128)(2,1)S(1)} %get-tuple-element.39), channel_id=1, source_target_pairs={{0,1},{1,0},{2,3},{3,2},{4,5},{5,4},{6,7},{7,6},{8,9},{9,8},{10,11... | collective-permute-start | bytes 1572872 | tf_op jit(solution)/shard_map/ppermute | solution.py:256
  5.1 4.2 %copy-start.3 = (bf16[1,1024,1024]{2,1,0:T(8,128)(2,1)S(1)}, bf16[1,1024,1024]{2,1,0:T(8,128)(2,1)}, u32[]{:S(2)}) copy-start(bf16[1,1024,1024]{2,1,0:T(8,128)(2,1)} %param.13) | copy-start | bytes 6291460
  5.6 15.6 %collective-permute-start.1 = (bf16[64,16,256]{2,1,0:T(8,128)(2,1)S(1)}, bf16[64,16,256]{2,1,0:T(8,128)(2,1)S(1)}, u32[]{:S(2)}, u32[]{:S(2)}) collective-permute-start(bf16[64,16,256]{2,1,0:T(8,128)(2,1)S(1)} %pack.2), channel_id=1, source_target_pairs={{0,2},{2,0},{1,3},{3,1},{4,6},{6,4},{5,7},{7,5},{8,10},{10,8},{9,1... | collective-permute-start | bytes 1572872 | tf_op jit(solution)/shard_map/ppermute | solution.py:258
  52.1 2.0 %collective-permute-start.3 = (bf16[2,512,256]{2,1,0:T(8,128)(2,1)S(1)}, bf16[2,512,256]{2,1,0:T(8,128)(2,1)S(1)}, u32[]{:S(2)}, u32[]{:S(2)}) collective-permute-start(bf16[2,512,256]{2,1,0:T(8,128)(2,1)S(1)} %get-tuple-element.46), channel_id=1, source_target_pairs={{0,1},{1,0},{2,3},{3,2},{4,5},{5,4},{6,7},{7,6},{8,9},{9,8},{10,11... | collective-permute-start | bytes 1572872 | tf_op jit(solution)/shard_map/ppermute | solution.py:269
  53.5 11.5 %copy-start.1 = (f32[1,1024,256]{2,1,0:T(8,128)S(1)}, f32[1,1024,256]{2,1,0:T(8,128)}, u32[]{:S(2)}) copy-start(f32[1,1024,256]{2,1,0:T(8,128)} %m1.5) | copy-start | bytes 3145732
  53.5 11.5 %copy-start.2 = (f32[1,1024,256]{2,1,0:T(8,128)S(1)}, f32[1,1024,256]{2,1,0:T(8,128)}, u32[]{:S(2)}) copy-start(f32[1,1024,256]{2,1,0:T(8,128)} %m2.5) | copy-start | bytes 3145732
  53.5 3.6 %collective-permute-start.5 = (bf16[2,512,256]{2,1,0:T(8,128)(2,1)S(1)}, bf16[2,512,256]{2,1,0:T(8,128)(2,1)S(1)}, u32[]{:S(2)}, u32[]{:S(2)}) collective-permute-start(bf16[2,512,256]{2,1,0:T(8,128)(2,1)S(1)} %get-tuple-element.49), channel_id=1, source_target_pairs={{0,1},{1,0},{2,3},{3,2},{4,5},{5,4},{6,7},{7,6},{8,9},{9,8},{10,11... | collective-permute-start | bytes 1572872 | tf_op jit(solution)/shard_map/ppermute | solution.py:269
  54.2 10.7 %collective-permute-start.4 = (bf16[512,256]{1,0:T(8,128)(2,1)S(1)}, bf16[512,256]{1,0:T(8,128)(2,1)S(1)}, u32[]{:S(2)}, u32[]{:S(2)}) collective-permute-start(bf16[512,256]{1,0:T(8,128)(2,1)S(1)} %get-tuple-element.47), channel_id=1, source_target_pairs={{0,2},{2,0},{1,3},{3,1},{4,6},{6,4},{5,7},{7,5},{8,10},{10,8},{9,1... | collective-permute-start | bytes 786440 | tf_op jit(solution)/shard_map/ppermute | solution.py:272
  57.1 13.5 %collective-permute-start.6 = (bf16[512,256]{1,0:T(8,128)(2,1)S(1)}, bf16[512,256]{1,0:T(8,128)(2,1)S(1)}, u32[]{:S(2)}, u32[]{:S(2)}) collective-permute-start(bf16[512,256]{1,0:T(8,128)(2,1)S(1)} %get-tuple-element.50), channel_id=1, source_target_pairs={{0,2},{2,0},{1,3},{3,1},{4,6},{6,4},{5,7},{7,5},{8,10},{10,8},{9,1... | collective-permute-start | bytes 786440 | tf_op jit(solution)/shard_map/ppermute | solution.py:272
  65.7 10.8 %collective-permute-start.9 = (bf16[512,256]{1,0:T(8,128)(2,1)S(1)}, bf16[512,256]{1,0:T(8,128)(2,1)S(1)}, u32[]{:S(2)}, u32[]{:S(2)}) collective-permute-start(bf16[512,256]{1,0:T(8,128)(2,1)S(1)} %get-tuple-element.58.own), channel_id=1, source_target_pairs={{0,2},{2,0},{1,3},{3,1},{4,6},{6,4},{5,7},{7,5},{8,10},{10,8},{9,1... | collective-permute-start | bytes 786440 | tf_op jit(solution)/shard_map/ppermute | solution.py:276
  68.5 8.9 %collective-permute-start.8 = (bf16[512,256]{1,0:T(8,128)(2,1)S(1)}, bf16[512,256]{1,0:T(8,128)(2,1)S(1)}, u32[]{:S(2)}, u32[]{:S(2)}) collective-permute-start(bf16[512,256]{1,0:T(8,128)(2,1)S(1)} %get-tuple-element.58.own), channel_id=1, source_target_pairs={{0,1},{1,0},{2,3},{3,2},{4,5},{5,4},{6,7},{7,6},{8,9},{9,8},{10,11... | collective-permute-start | bytes 786440 | tf_op jit(solution)/shard_map/ppermute | solution.py:276
  71.3 9.7 %collective-permute-start.7 = (bf16[512,256]{1,0:T(8,128)(2,1)S(1)}, bf16[512,256]{1,0:T(8,128)(2,1)S(1)}, u32[]{:S(2)}, u32[]{:S(2)}) collective-permute-start(bf16[512,256]{1,0:T(8,128)(2,1)S(1)} %get-tuple-element.65.own), channel_id=1, source_target_pairs={{0,2},{2,0},{1,3},{3,1},{4,6},{6,4},{5,7},{7,5},{8,10},{10,8},{9,1... | collective-permute-start | bytes 786440 | tf_op jit(solution)/shard_map/ppermute | solution.py:279
  76.5 1.6 %collective-permute-start.10 = (bf16[256,256]{1,0:T(8,128)(2,1)S(1)}, bf16[256,256]{1,0:T(8,128)(2,1)S(1)}, u32[]{:S(2)}, u32[]{:S(2)}) collective-permute-start(bf16[256,256]{1,0:T(8,128)(2,1)S(1)} %get-tuple-element.70), channel_id=1, source_target_pairs={{0,1},{1,0},{2,3},{3,2},{4,5},{5,4},{6,7},{7,6},{8,9},{9,8},{10,11... | collective-permute-start | bytes 393224 | tf_op jit(solution)/shard_map/ppermute | solution.py:283
  76.8 1.5 %collective-permute-start.11 = (bf16[256,256]{1,0:T(8,128)(2,1)S(1)}, bf16[256,256]{1,0:T(8,128)(2,1)S(1)}, u32[]{:S(2)}, u32[]{:S(2)}) collective-permute-start(bf16[256,256]{1,0:T(8,128)(2,1)S(1)} %get-tuple-element.69), channel_id=1, source_target_pairs={{0,1},{1,0},{2,3},{3,2},{4,5},{5,4},{6,7},{7,6},{8,9},{9,8},{10,11... | collective-permute-start | bytes 393224 | tf_op jit(solution)/shard_map/ppermute | solution.py:283
  77.3 3.7 %collective-permute-start.12 = (bf16[512,256]{1,0:T(8,128)(2,1)S(1)}, bf16[512,256]{1,0:T(8,128)(2,1)S(1)}, u32[]{:S(2)}, u32[]{:S(2)}) collective-permute-start(bf16[512,256]{1,0:T(8,128)(2,1)S(1)} %get-tuple-element.65.own), channel_id=1, source_target_pairs={{0,1},{1,0},{2,3},{3,2},{4,5},{5,4},{6,7},{7,6},{8,9},{9,8},{10,11... | collective-permute-start | bytes 786440 | tf_op jit(solution)/shard_map/ppermute | solution.py:279
  81.0 1.5 %collective-permute-start.13 = (bf16[512,256]{1,0:T(8,128)(2,1)S(1)}, bf16[512,256]{1,0:T(8,128)(2,1)S(1)}, u32[]{:S(2)}, u32[]{:S(2)}) collective-permute-start(bf16[512,256]{1,0:T(8,128)(2,1)S(1)} %collective-permute-done.7.far), channel_id=1, source_target_pairs={{0,1},{1,0},{2,3},{3,2},{4,5},{5,4},{6,7},{7,6},{8,9},{9,8},{10,11... | collective-permute-start | bytes 786440 | tf_op jit(solution)/shard_map/ppermute | solution.py:286
  83.0 24.2 %copy-start.6 = (f32[16,64,256]{2,1,0:T(8,128)S(1)}, f32[16,64,256]{2,1,0:T(8,128)}, u32[]{:S(2)}) copy-start(f32[16,64,256]{2,1,0:T(8,128)} %weights.1) | copy-start | bytes 3145732
